TPU v7x, 32 devices: a whole 2x2x4 slice. The times are simulated.
32 devices in a mesh: conv: 2 (over y), ctx: 4 (over x, core), head: 4 (over z).
Axes of the slice: x: 2, y: 2, z: 4, core: 2. Of those that a mesh axis runs over, the one named last changes fastest.
Arguments:
- queries: bfloat16 [512, 64, 128], P(('conv', 'ctx'), 'head'), parts along dimension 0, may hold values from -240 to 240, as said below
- new_keys: bfloat16 [512, 8, 128], P(('conv', 'ctx'), 'head'), parts along dimension 0, may hold values from -8 to 8
- new_values: bfloat16 [512, 8, 128], P(('conv', 'ctx'), 'head'), parts along dimension 0, may hold values from -18 to 18
- cache_keys: bfloat16 [16384, 8, 128], P(('conv', 'ctx'), 'head'), parts along dimension 0, may hold values from -6 to 6
- cache_values: bfloat16 [16384, 8, 128], P(('conv', 'ctx'), 'head'), parts along dimension 0, may hold values from -18 to 18
- cache_len: int32 [2], P('conv'), parts along dimension 0, may hold values from 4097 to 8192
Outputs:
- attended: bfloat16 [512, 64, 128], P(('conv', 'ctx'), 'head'), parts along dimension 0
There are 2 independent parts, one for each index of `conv`. A program takes and returns all parts, laid end to end along the dimension named above; each array names one. Nothing has to cross between parts.
Inputs may be any that keep to these rules, and one draw needn't show every extreme that they name: `queries`: each query row is a row of independent entries times a row scale.
All inputs are finite; a program needn't handle non-finite values.
Results may differ from a plain program's by a relative error of at most 0.01.
Values may be sent and summed in bfloat16 or wider, within the bound.
No kernel may reach another device: no remote copies, remote signals or barrier semaphores. Data moves between devices by JAX's collectives and lax.ppermute only.
A program may use at most 64 MiB of HBM per device.

v0:
```python
import math

import jax
import jax.numpy as jnp
from jax import lax
from jax.sharding import PartitionSpec as P

NEG_FILL = -1e30


def attend_block(query_rows, keys, values, valid):
    scores = jnp.einsum("tkgd,skd->tkgs", query_rows, keys, preferred_element_type=jnp.float32) * (
        1.0 / math.sqrt(keys.shape[-1])
    )
    mask = valid[:, None, None, :]
    scores = jnp.where(mask, scores, NEG_FILL)
    peak = jnp.max(scores, axis=-1)
    expo = jnp.where(mask, jnp.exp(scores - peak[..., None]), 0.0)
    total = jnp.sum(expo, axis=-1)
    out = jnp.einsum(
        "tkgs,skd->tkgd", expo.astype(jnp.bfloat16), values, preferred_element_type=jnp.float32
    )
    return (out, peak, total)


def per_device(queries, new_keys, new_values, cache_keys, cache_values, cache_len):
    q_rows, heads_local, head_size = queries.shape
    slots, kv_local, _ = cache_keys.shape
    group = heads_local // kv_local
    place = lax.axis_index("ctx")
    limit = cache_len[0]
    slot_valid = place * slots + lax.iota(jnp.int32, slots) < limit
    piece = lax.all_gather(queries, "ctx", axis=0, tiled=True)
    rows = piece.shape[0]
    block = math.gcd(rows, 64)
    blocks = piece.reshape(rows // block, block, kv_local, group, head_size)

    def one_block(blk):
        out, peak, total = attend_block(blk, cache_keys, cache_values, slot_valid[None, :])
        floored = jnp.maximum(total, 1.0)
        norm = (out / floored[..., None]).astype(jnp.bfloat16)
        lse = peak + jnp.log(floored)
        return (norm.reshape(block, heads_local, head_size), lse.reshape(block, heads_local))

    norm, lse = lax.map(one_block, blocks)
    norm, lse = (norm.reshape(rows, heads_local, head_size), lse.reshape(rows, heads_local))
    turn_k, turn_v = (
        lax.all_gather(new_keys, "ctx", axis=0, tiled=True),
        lax.all_gather(new_values, "ctx", axis=0, tiled=True),
    )
    own_ids = place * q_rows + lax.iota(jnp.int32, q_rows)
    causal = lax.iota(jnp.int32, turn_k.shape[0])[None, :] <= own_ids[:, None]
    turn_out, turn_max, turn_total = attend_block(
        queries.reshape(q_rows, kv_local, group, head_size), turn_k, turn_v, causal
    )
    turn_out = turn_out.reshape(q_rows, heads_local, head_size)
    turn_max = turn_max.reshape(q_rows, heads_local)
    turn_total = turn_total.reshape(q_rows, heads_local)
    got_norm = lax.all_to_all(norm[None], "ctx", split_axis=1, concat_axis=0, tiled=True)
    got_lse = lax.all_to_all(lse[None], "ctx", split_axis=1, concat_axis=0, tiled=True)
    top = jnp.maximum(jnp.max(got_lse, axis=0), turn_max)
    shard_scale = jnp.exp(got_lse - top[None])
    numer = jnp.einsum("sthd,sth->thd", got_norm.astype(jnp.float32), shard_scale)
    denom = jnp.sum(shard_scale, axis=0)
    turn_scale = jnp.exp(turn_max - top)
    numer = numer + turn_out * turn_scale[..., None]
    denom = denom + turn_total * turn_scale
    return (numer / denom[..., None]).astype(jnp.bfloat16)


def solution(mesh):
    return jax.shard_map(
        per_device,
        mesh=mesh,
        in_specs=(
            P(("conv", "ctx"), "head", None),
            P(("conv", "ctx"), "head", None),
            P(("conv", "ctx"), "head", None),
            P(("conv", "ctx"), "head", None),
            P(("conv", "ctx"), "head", None),
            P("conv"),
        ),
        out_specs=P(("conv", "ctx"), "head", None),
        check_vma=False,
    )
```

profile of v0, /device:TPU:0, one launch (start us, length us, event | category | flops | bytes accessed | tf_op | source)
XLA Modules:
  0.0 124.4 jit_solution(1532145493059581780)
XLA Ops:
  6.5 0.7 all-gather.2.cloned.1.call-update
  7.3 1.4 %copy.96 = bf16[2048,2,128]{2,0,1:T(8,128)(2,1)S(1)} copy(bf16[2048,2,128]{2,1,0:T(2,128)(2,1)} %param.11) | data formatting | bytes 2097152
  8.7 1.4 %copy.97 = bf16[2048,2,128]{2,0,1:T(8,128)(2,1)S(1)} copy(bf16[2048,2,128]{2,1,0:T(2,128)(2,1)} %param.12) | data formatting | bytes 2097152
  10.0 0.8 copy.100
  10.8 0.8 copy.104
  11.5 6.5 %all_gather.10 = bf16[256,2,128]{2,0,1:T(8,128)(2,1)S(1)} all-gather(bf16[64,2,128]{2,0,1:T(8,128)(2,1)S(1)} %copy.100), channel_id=1, replica_groups=mesh['conv'=2,'ctx'=4,'head'=4] {'ctx'}, dimensions={0}, use_global_device_ids=true | all-gather | bytes 163840 | tf_op jit(solution)/shard_map/all_gather | solution.py:48
  18.0 6.1 %all_gather.11 = bf16[256,2,128]{2,0,1:T(8,128)(2,1)S(1)} all-gather(bf16[64,2,128]{2,0,1:T(8,128)(2,1)S(1)} %copy.104), channel_id=1, replica_groups=mesh['conv'=2,'ctx'=4,'head'=4] {'ctx'}, dimensions={0}, use_global_device_ids=true | all-gather | bytes 163840 | tf_op jit(solution)/shard_map/all_gather | solution.py:49
  24.1 0.1 iota_compare_fusion
  24.2 1.3 %fusion.47 = (f32[64,2,8]{0,2,1:T(8,128)S(1)}, f32[64,2,8,256]{3,0,2,1:T(8,128)S(1)}) fusion(bf16[64,2,8,128]{3,2,1,0:T(8,128)(2,1)} %bitcast.124, bf16[256,2,128]{2,0,1:T(8,128)(2,1)S(1)} %all_gather.10, pred[64,256]{1,0:T(8,128)(4,1)S(1)} %iota_compare_fusion), kind=kOutput, calls=%fused_computation.53 | convolution fusion | flops 67894272 | bytes 1462272 | tf_op jit(solution)/shard_map/tkgd,skd->tkgs/dot_general | solution.py:12
  25.5 0.4 fusion.33
  25.9 3.1 %all-gather.2.cloned.1.call-done = bf16[256,16,128]{2,1,0:T(8,128)(2,1)} async-done(((bf16[64,16,128]{2,1,0:T(8,128)(2,1)}), bf16[256,16,128]{2,1,0:T(8,128)(2,1)}) %all-gather.2.cloned.1.call-update) | async-done | bytes 1048592 | tf_op jit(solution)/shard_map/all_gather | solution.py:33
  29.1 58.6 %while.13 = (s32[]{:T(128)}, bf16[4,64,16,128]{3,2,1,0:T(8,128)(2,1)}, f32[4,64,16]{1,2,0:T(8,128)S(1)}, bf16[4,64,2,8,128]{4,3,2,1,0:T(8,128)(2,1)}, bf16[2048,...) while((s32[]{:T(128)}, ...), condition=%wide.region_3.4_spmd.clone, body=%wide.region_0.3_spmd.clone.sunk | while | flops 1101272064 | bytes 61953156 | solution.py:45
  29.1 0.7 add_compare_fusion.2
  29.7 2.4 %bitcast_reduce_fusion.2 = (f32[64,2,8]{2,0,1:T(8,128)S(1)}, f32[2,64,8,2048]{3,2,1,0:T(8,128)S(1)}) fusion(pred[2048]{0:T(1024)(128)(4,1)S(1)} %add_compare_fusion.2, bf16[2048,2,128]{2,0,1:T(8,128)(2,1)S(1)} %get-tuple-element.220, bf16[4,64,2,8,128]{4,3,2,1,0:T(8,128)(2,1)} %get-tuple-element.219, s32[]{:T(128)} %get-tuple-element.207), kind=kOutput, calls=%fused_computation.2.clone.1 | convolution fusion | flops 543161344 | bytes 9705984 | tf_op jit(solution)/shard_map/while/body/eval_jaxpr/tkgd,skd->tkgs/dot_general | solution.py:12
  32.2 3.2 %copy-done = f32[2,64,8,2048]{3,2,1,0:T(8,128)} copy-done((f32[2,64,8,2048]{3,2,1,0:T(8,128)}, f32[2,64,8,2048]{3,2,1,0:T(8,128)S(1)}, u32[]{:S(2)}) %copy-start) | copy-done | bytes 8388632 | tf_op jit(solution)/shard_map/while
  35.4 2.2 %fusion.55 = f32[64,2,8]{2,0,1:T(8,128)S(1)} fusion(f32[2,64,8,2048]{3,2,1,0:T(8,128)S(1)} %get-tuple-element.196, f32[64,2,8]{2,0,1:T(8,128)S(1)} %get-tuple-element.197, pred[2048]{0:T(1024)(128)(4,1)S(1)} %add_compare_fusion.2), kind=kLoop, calls=%fused_computation.6.clone.1 | loop fusion | flops 10484736 | bytes 8398848 | tf_op jit(solution)/shard_map/while/body/eval_jaxpr/reduce_sum | solution.py:19
  37.6 0.1 copy.141
  37.7 0.1 copy.143
  37.7 0.1 copy.142
  37.8 5.1 %fusion.56 = bf16[64,2,8,128]{3,2,0,1:T(8,128)(2,1)S(1)} fusion(bf16[2048,2,128]{2,0,1:T(8,128)(2,1)S(1)} %get-tuple-element.221, f32[2,64,8,2048]{3,2,1,0:T(8,128)} %copy-done, f32[64,2,8]{2,0,1:T(8,128)S(1)} %get-tuple-element.197, pred[2048]{0:T(1024)(128)(4,1)S(1)} %add_compare_fusion.2, f32[64,2,8]{2,0,1:T(8,128)S(1)} %copy.142), kind=kOutput, calls=%fused_computation.16.clone.1 | convolution fusion | flops 547618816 | bytes 9709568 | tf_op jit(solution)/shard_map/while/body/eval_jaxpr/tkgs,skd->tkgd/dot_general | solution.py:20
  43.0 0.8 bitcast_dynamic-update-slice_fusion.4
  43.7 0.7 add_compare_fusion.2
  44.4 2.4 %bitcast_reduce_fusion.2 = (f32[64,2,8]{2,0,1:T(8,128)S(1)}, f32[2,64,8,2048]{3,2,1,0:T(8,128)S(1)}) fusion(pred[2048]{0:T(1024)(128)(4,1)S(1)} %add_compare_fusion.2, bf16[2048,2,128]{2,0,1:T(8,128)(2,1)S(1)} %get-tuple-element.220, bf16[4,64,2,8,128]{4,3,2,1,0:T(8,128)(2,1)} %get-tuple-element.219, s32[]{:T(128)} %get-tuple-element.207), kind=kOutput, calls=%fused_computation.2.clone.1 | convolution fusion | flops 543161344 | bytes 9705984 | tf_op jit(solution)/shard_map/while/body/eval_jaxpr/tkgd,skd->tkgs/dot_general | solution.py:12
  46.8 3.2 %copy-done = f32[2,64,8,2048]{3,2,1,0:T(8,128)} copy-done((f32[2,64,8,2048]{3,2,1,0:T(8,128)}, f32[2,64,8,2048]{3,2,1,0:T(8,128)S(1)}, u32[]{:S(2)}) %copy-start) | copy-done | bytes 8388632 | tf_op jit(solution)/shard_map/while
  50.0 2.2 %fusion.55 = f32[64,2,8]{2,0,1:T(8,128)S(1)} fusion(f32[2,64,8,2048]{3,2,1,0:T(8,128)S(1)} %get-tuple-element.196, f32[64,2,8]{2,0,1:T(8,128)S(1)} %get-tuple-element.197, pred[2048]{0:T(1024)(128)(4,1)S(1)} %add_compare_fusion.2), kind=kLoop, calls=%fused_computation.6.clone.1 | loop fusion | flops 10484736 | bytes 8398848 | tf_op jit(solution)/shard_map/while/body/eval_jaxpr/reduce_sum | solution.py:19
  52.2 0.1 copy.141
  52.3 0.1 copy.143
  52.4 0.1 copy.142
  52.5 5.1 %fusion.56 = bf16[64,2,8,128]{3,2,0,1:T(8,128)(2,1)S(1)} fusion(bf16[2048,2,128]{2,0,1:T(8,128)(2,1)S(1)} %get-tuple-element.221, f32[2,64,8,2048]{3,2,1,0:T(8,128)} %copy-done, f32[64,2,8]{2,0,1:T(8,128)S(1)} %get-tuple-element.197, pred[2048]{0:T(1024)(128)(4,1)S(1)} %add_compare_fusion.2, f32[64,2,8]{2,0,1:T(8,128)S(1)} %copy.142), kind=kOutput, calls=%fused_computation.16.clone.1 | convolution fusion | flops 547618816 | bytes 9709568 | tf_op jit(solution)/shard_map/while/body/eval_jaxpr/tkgs,skd->tkgd/dot_general | solution.py:20
  57.6 0.8 bitcast_dynamic-update-slice_fusion.4
  58.4 0.7 add_compare_fusion.2
  59.0 2.4 %bitcast_reduce_fusion.2 = (f32[64,2,8]{2,0,1:T(8,128)S(1)}, f32[2,64,8,2048]{3,2,1,0:T(8,128)S(1)}) fusion(pred[2048]{0:T(1024)(128)(4,1)S(1)} %add_compare_fusion.2, bf16[2048,2,128]{2,0,1:T(8,128)(2,1)S(1)} %get-tuple-element.220, bf16[4,64,2,8,128]{4,3,2,1,0:T(8,128)(2,1)} %get-tuple-element.219, s32[]{:T(128)} %get-tuple-element.207), kind=kOutput, calls=%fused_computation.2.clone.1 | convolution fusion | flops 543161344 | bytes 9705984 | tf_op jit(solution)/shard_map/while/body/eval_jaxpr/tkgd,skd->tkgs/dot_general | solution.py:12
  61.5 3.2 %copy-done = f32[2,64,8,2048]{3,2,1,0:T(8,128)} copy-done((f32[2,64,8,2048]{3,2,1,0:T(8,128)}, f32[2,64,8,2048]{3,2,1,0:T(8,128)S(1)}, u32[]{:S(2)}) %copy-start) | copy-done | bytes 8388632 | tf_op jit(solution)/shard_map/while
  64.7 2.2 %fusion.55 = f32[64,2,8]{2,0,1:T(8,128)S(1)} fusion(f32[2,64,8,2048]{3,2,1,0:T(8,128)S(1)} %get-tuple-element.196, f32[64,2,8]{2,0,1:T(8,128)S(1)} %get-tuple-element.197, pred[2048]{0:T(1024)(128)(4,1)S(1)} %add_compare_fusion.2), kind=kLoop, calls=%fused_computation.6.clone.1 | loop fusion | flops 10484736 | bytes 8398848 | tf_op jit(solution)/shard_map/while/body/eval_jaxpr/reduce_sum | solution.py:19
  66.9 0.1 copy.141
  67.0 0.1 copy.143
  67.1 0.1 copy.142
  67.2 5.1 %fusion.56 = bf16[64,2,8,128]{3,2,0,1:T(8,128)(2,1)S(1)} fusion(bf16[2048,2,128]{2,0,1:T(8,128)(2,1)S(1)} %get-tuple-element.221, f32[2,64,8,2048]{3,2,1,0:T(8,128)} %copy-done, f32[64,2,8]{2,0,1:T(8,128)S(1)} %get-tuple-element.197, pred[2048]{0:T(1024)(128)(4,1)S(1)} %add_compare_fusion.2, f32[64,2,8]{2,0,1:T(8,128)S(1)} %copy.142), kind=kOutput, calls=%fused_computation.16.clone.1 | convolution fusion | flops 547618816 | bytes 9709568 | tf_op jit(solution)/shard_map/while/body/eval_jaxpr/tkgs,skd->tkgd/dot_general | solution.py:20
  72.3 0.8 bitcast_dynamic-update-slice_fusion.4
  73.0 0.7 add_compare_fusion.2
  73.7 2.4 %bitcast_reduce_fusion.2 = (f32[64,2,8]{2,0,1:T(8,128)S(1)}, f32[2,64,8,2048]{3,2,1,0:T(8,128)S(1)}) fusion(pred[2048]{0:T(1024)(128)(4,1)S(1)} %add_compare_fusion.2, bf16[2048,2,128]{2,0,1:T(8,128)(2,1)S(1)} %get-tuple-element.220, bf16[4,64,2,8,128]{4,3,2,1,0:T(8,128)(2,1)} %get-tuple-element.219, s32[]{:T(128)} %get-tuple-element.207), kind=kOutput, calls=%fused_computation.2.clone.1 | convolution fusion | flops 543161344 | bytes 9705984 | tf_op jit(solution)/shard_map/while/body/eval_jaxpr/tkgd,skd->tkgs/dot_general | solution.py:12
  76.1 3.2 %copy-done = f32[2,64,8,2048]{3,2,1,0:T(8,128)} copy-done((f32[2,64,8,2048]{3,2,1,0:T(8,128)}, f32[2,64,8,2048]{3,2,1,0:T(8,128)S(1)}, u32[]{:S(2)}) %copy-start) | copy-done | bytes 8388632 | tf_op jit(solution)/shard_map/while
  79.3 2.2 %fusion.55 = f32[64,2,8]{2,0,1:T(8,128)S(1)} fusion(f32[2,64,8,2048]{3,2,1,0:T(8,128)S(1)} %get-tuple-element.196, f32[64,2,8]{2,0,1:T(8,128)S(1)} %get-tuple-element.197, pred[2048]{0:T(1024)(128)(4,1)S(1)} %add_compare_fusion.2), kind=kLoop, calls=%fused_computation.6.clone.1 | loop fusion | flops 10484736 | bytes 8398848 | tf_op jit(solution)/shard_map/while/body/eval_jaxpr/reduce_sum | solution.py:19
  81.6 0.1 copy.143
  81.7 0.1 copy.142
  81.8 5.1 %fusion.56 = bf16[64,2,8,128]{3,2,0,1:T(8,128)(2,1)S(1)} fusion(bf16[2048,2,128]{2,0,1:T(8,128)(2,1)S(1)} %get-tuple-element.221, f32[2,64,8,2048]{3,2,1,0:T(8,128)} %copy-done, f32[64,2,8]{2,0,1:T(8,128)S(1)} %get-tuple-element.197, pred[2048]{0:T(1024)(128)(4,1)S(1)} %add_compare_fusion.2, f32[64,2,8]{2,0,1:T(8,128)S(1)} %copy.142), kind=kOutput, calls=%fused_computation.16.clone.1 | convolution fusion | flops 547618816 | bytes 9709568 | tf_op jit(solution)/shard_map/while/body/eval_jaxpr/tkgs,skd->tkgd/dot_general | solution.py:20
  86.9 0.8 bitcast_dynamic-update-slice_fusion.4
  87.7 0.1 copy.117
  87.8 0.6 broadcast.66
  88.4 1.0 reduce
  89.4 0.7 reshape.128
  90.1 3.3 %all-to-all-start.1 = ((f32[4,1,1024]{2,1,0:T(1,128)}), f32[4,1,1024]{2,1,0:T(1,128)S(1)}, u32[]{:S(2)}, u32[]{:S(2)}) async-start(f32[4,1,1024]{2,1,0:T(1,128)} %reshape.128), calls=%async_computation.1 | async-start | bytes 32768 | tf_op jit(solution)/shard_map/all_to_all | solution.py:60
  93.4 0.4 convolution_bitcast_fusion
  93.8 3.4 %all-to-all-done.1 = f32[4,1,1024]{2,1,0:T(1,128)S(1)} async-done(((f32[4,1,1024]{2,1,0:T(1,128)}), f32[4,1,1024]{2,1,0:T(1,128)S(1)}, u32[]{:S(2)}, u32[]{:S(2)}) %all-to-all-start.1) | async-done | bytes 16416 | tf_op jit(solution)/shard_map/all_to_all | solution.py:60
  97.2 3.5 %all-to-all-start = ((bf16[1,256,16,128]{3,2,0,1:T(8,128)(2,1)}), bf16[1,256,16,128]{3,2,0,1:T(8,128)(2,1)S(1)}, u32[]{:S(2)}, u32[]{:S(2)}) async-start(bf16[1,256,16,128]{3,2,0,1:T(8,128)(2,1)} %bitcast.2), calls=%async_computation | async-start | bytes 2097152 | tf_op jit(solution)/shard_map/all_to_all | solution.py:59
  100.7 0.7 reduce.1
  101.5 0.2 reshape.129
  101.8 0.1 copy.103
  102.0 0.1 copy.107
  102.1 0.1 copy.109
  102.2 0.7 copy.114
  102.9 12.3 %all-to-all-done = bf16[1,256,16,128]{3,2,0,1:T(8,128)(2,1)S(1)} async-done(((bf16[1,256,16,128]{3,2,0,1:T(8,128)(2,1)}), bf16[1,256,16,128]{3,2,0,1:T(8,128)(2,1)S(1)}, u32[]{:S(2)}, u32[]{:S(2)}) %all-to-all-start) | async-done | bytes 1048608 | tf_op jit(solution)/shard_map/all_to_all | solution.py:59
  115.2 1.3 %fusion.31 = f32[64,16,1,128]{3,2,1,0:T(1,128)S(1)} fusion(bf16[4,64,16,1]{0,3,2,1:T(2,128)(2,1)S(1)} %copy.114, bf16[4,64,16,128]{3,2,1,0:T(8,128)(2,1)S(1)} %bitcast.123), kind=kOutput, calls=%fused_computation.31 | convolution fusion | flops 1048576 | bytes 1581056 | tf_op jit(solution)/shard_map/sthd,sth->thd/dot_general | solution.py:63
  116.5 1.1 fusion.37
  (24 shorter events, 0.4 us)
Async XLA Ops:
  6.5 22.5 %all-gather.2.cloned.1.call-start = ((), (), s32[]{:S(2)}) async-start(), calls=%async_computation.2 | async-start | bytes 1310720 | tf_op jit(solution)/shard_map/all_gather | solution.py:33
  32.2 3.2 %copy-start = (f32[2,64,8,2048]{3,2,1,0:T(8,128)}, f32[2,64,8,2048]{3,2,1,0:T(8,128)S(1)}, u32[]{:S(2)}) copy-start(f32[2,64,8,2048]{3,2,1,0:T(8,128)S(1)} %get-tuple-element.196) | copy-start | bytes 25165828 | tf_op jit(solution)/shard_map/while
  46.8 3.2 %copy-start = (f32[2,64,8,2048]{3,2,1,0:T(8,128)}, f32[2,64,8,2048]{3,2,1,0:T(8,128)S(1)}, u32[]{:S(2)}) copy-start(f32[2,64,8,2048]{3,2,1,0:T(8,128)S(1)} %get-tuple-element.196) | copy-start | bytes 25165828 | tf_op jit(solution)/shard_map/while
  61.5 3.2 %copy-start = (f32[2,64,8,2048]{3,2,1,0:T(8,128)}, f32[2,64,8,2048]{3,2,1,0:T(8,128)S(1)}, u32[]{:S(2)}) copy-start(f32[2,64,8,2048]{3,2,1,0:T(8,128)S(1)} %get-tuple-element.196) | copy-start | bytes 25165828 | tf_op jit(solution)/shard_map/while
  76.1 3.2 %copy-start = (f32[2,64,8,2048]{3,2,1,0:T(8,128)}, f32[2,64,8,2048]{3,2,1,0:T(8,128)S(1)}, u32[]{:S(2)}) copy-start(f32[2,64,8,2048]{3,2,1,0:T(8,128)S(1)} %get-tuple-element.196) | copy-start | bytes 25165828 | tf_op jit(solution)/shard_map/while
  90.1 7.1 %all-to-all-start.1 = ((f32[4,1,1024]{2,1,0:T(1,128)}), f32[4,1,1024]{2,1,0:T(1,128)S(1)}, u32[]{:S(2)}, u32[]{:S(2)}) async-start(f32[4,1,1024]{2,1,0:T(1,128)} %reshape.128), calls=%async_computation.1 | async-start | bytes 32768 | tf_op jit(solution)/shard_map/all_to_all | solution.py:60
  97.2 18.0 %all-to-all-start = ((bf16[1,256,16,128]{3,2,0,1:T(8,128)(2,1)}), bf16[1,256,16,128]{3,2,0,1:T(8,128)(2,1)S(1)}, u32[]{:S(2)}, u32[]{:S(2)}) async-start(bf16[1,256,16,128]{3,2,0,1:T(8,128)(2,1)} %bitcast.2), calls=%async_computation | async-start | bytes 2097152 | tf_op jit(solution)/shard_map/all_to_all | solution.py:59
Sparse Core Ops, SparseCore 0:
  8.9 20.1 all-gather.1
where the time goes:
time: 125 us; the launch traced here: 124 us
  matrix products  33.2 us (27%)
  local copies, waits for them, and re-layouts  23.8 us (19%)
  waiting for transfers between devices  19.5 us (16%)
  other arithmetic  14.9 us (12%)
  between operations  13.5 us (11%)
  blocking collectives  12.5 us (10%)
  starting transfers between devices  6.77 us (5%)
    dot_general x5, matrix products, attend_block(): jnp.einsum('tkgs,skd->tkgd', expo.astype(jnp.bfloat16), values, preferred...  20.8 us
    while x8, local copies, waits for them, and re-layouts  12.9 us
    all_to_all x1, waiting for transfers between devices, per_device(): lax.all_to_all(norm[None], 'ctx', split_axis=1, concat_axis=0, tiled=True)  12.3 us
    dot_general x5, matrix products, attend_block(): jnp.einsum('tkgd,skd->tkgs', query_rows, keys, preferred_element_type=jnp...  11 us
    reduce_sum x5, other arithmetic, attend_block(): total = jnp.sum(expo, axis=-1)  9.28 us
    all_gather x1, blocking collectives, per_device(): lax.all_gather(new_keys, 'ctx', axis=0, tiled=True)  6.47 us
    all_gather x1, blocking collectives, per_device(): lax.all_gather(new_values, 'ctx', axis=0, tiled=True)  6.05 us
    unnamed x7, local copies, waits for them, and re-layouts  5.81 us
  transfers between devices with their start and end apart: 3, of which 3 were waited for; matrix products, arithmetic and copies ran while one was open for 7% of the time, Pallas kernels for 0%

commit v1 on v0

v1 whole, which is shorter than its diff:
```python
import functools
import math

import jax
import jax.numpy as jnp
from jax import lax
from jax.experimental import pallas as pl
from jax.experimental.pallas import tpu as pltpu
from jax.sharding import PartitionSpec as P

NEG_FILL = -1e30
LOG2E = 1.4426950408889634
LN2 = 0.6931471805599453
VMEM = pl.BlockSpec(memory_space=pltpu.VMEM)
SMEM = pl.BlockSpec(memory_space=pltpu.SMEM)
F32 = jnp.float32
BF16 = jnp.bfloat16


def params():
    return pltpu.CompilerParams(vmem_limit_bytes=40 * 2**20)


def pack_rows(column):
    rows = column.shape[0]
    flat = jnp.transpose(jnp.broadcast_to(column, (rows, 128)))[0:1, :]
    return jnp.concatenate([flat[:, i * 128 : (i + 1) * 128] for i in range(rows // 128)], axis=0)


def spread_rows(packed):
    return jnp.concatenate(
        [jnp.transpose(jnp.broadcast_to(packed[i : i + 1, :], (128, 128))) for i in range(packed.shape[0])], axis=0
    )


def prepare(info, k_ref, v_ref, nk_ref, nv_ref, keys, values):
    slots, kv, hd = k_ref.shape
    fresh = nk_ref.shape[0]
    filled = info[0]
    ok = lax.broadcasted_iota(jnp.int32, (slots, hd), 0) < filled
    all_k = jnp.swapaxes(k_ref[...], 0, 1)
    all_v = jnp.swapaxes(v_ref[...], 0, 1)
    new_k = jnp.swapaxes(nk_ref[...], 0, 1)
    new_v = jnp.swapaxes(nv_ref[...], 0, 1)
    ones = jnp.where(ok, 1.0, 0.0).astype(BF16)
    for h in range(kv):
        fill = jnp.where(filled > 0, all_k[h, 0:1, :].astype(F32), new_k[h, 0:1, :].astype(F32))
        keys[h, 0:slots] = jnp.where(ok, all_k[h].astype(F32), fill).astype(BF16)
        keys[h, slots:] = new_k[h]
        values[h, 0:slots, 0:hd] = jnp.where(ok, all_v[h].astype(F32), 0.0).astype(BF16)
        values[h, 0:slots, hd:] = ones
        values[h, slots:, 0:hd] = new_v[h]
        values[h, slots:, hd:] = jnp.ones((fresh, hd), BF16)


def attend(offset, q_ref, keys, values, o_ref, l_ref):
    tokens, heads, hd = q_ref.shape
    kv, span, _ = keys.shape
    group = heads // kv
    fresh = tokens
    slots = span - fresh
    scale = LOG2E / math.sqrt(hd)
    tile = min(tokens, 256 // group)
    rows = tile * group
    per = rows // 128
    for h in range(kv):
        for r in range(tokens // tile):
            q = q_ref[r * tile : (r + 1) * tile, h * group : (h + 1) * group, :].reshape(rows, hd)
            nt = (((1,), (1,)), ((), ()))
            s = lax.dot_general(q, keys[h, 0:slots], nt, preferred_element_type=F32)
            s2 = lax.dot_general(q, keys[h, slots:], nt, preferred_element_type=F32)
            token = r * tile + lax.broadcasted_iota(jnp.int32, (rows, fresh), 0) // group
            seen = token + offset >= lax.broadcasted_iota(jnp.int32, (rows, fresh), 1)
            s2 = jnp.where(seen, s2, NEG_FILL)
            peak = jnp.maximum(jnp.max(s, axis=-1, keepdims=True), jnp.max(s2, axis=-1, keepdims=True))
            w = jnp.exp2((s - peak) * scale).astype(BF16)
            w2 = jnp.where(seen, jnp.exp2((s2 - peak) * scale), 0.0).astype(BF16)
            out = jnp.dot(w, values[h, 0:slots], preferred_element_type=F32)
            out = out + jnp.dot(w2, values[h, slots:], preferred_element_type=F32)
            total = out[:, hd:]
            norm = out[:, 0:hd] / jnp.maximum(total, 1.0)
            o_ref[r * tile : (r + 1) * tile, h * group : (h + 1) * group, :] = norm.astype(BF16).reshape(tile, group, hd)
            total = total[:, 0:1]
            lse = jnp.where(total > 0.0, peak * (1.0 / math.sqrt(hd)) + jnp.log(jnp.maximum(total, 1.0)), NEG_FILL)
            at = h * (tokens * group // 128) + r * per
            l_ref[at : at + per, :] = pack_rows(lse)


def blend(group, parts, o_ref, l_ref=None):
    tokens, heads, hd = o_ref.shape
    lses = [l[...] for _, l in parts]
    top = functools.reduce(jnp.maximum, lses)
    scales = [jnp.exp(l - top) for l in lses]
    total = functools.reduce(jnp.add, scales)
    if l_ref is not None:
        l_ref[...] = jnp.where(top > 0.5 * NEG_FILL, top + jnp.log(total), NEG_FILL)
    inv = 1.0 / total
    kv = heads // group
    n = tokens * group // 128
    for h in range(kv):
        acc = None
        for (norm, _), s in zip(parts, scales):
            wide = spread_rows((s * inv)[h * n : (h + 1) * n, :])
            term = norm[:, h * group : (h + 1) * group, :].reshape(tokens * group, hd).astype(F32) * wide
            acc = term if acc is None else acc + term
        o_ref[:, h * group : (h + 1) * group, :] = acc.astype(BF16).reshape(tokens, group, hd)


def first_kernel(info, qa, qb, k, v, nk, nv, oa, la, ob, lb, keys, values):
    prepare(info, k, v, nk, nv, keys, values)
    attend(info[1], qa, keys, values, oa, la)
    attend(info[2], qb, keys, values, ob, lb)


def next_kernel(info, qa, keys, values, oa, la):
    attend(info[1], qa, keys, values, oa, la)


def blend2_kernel(group, a, la, b, lb, o, l):
    blend(group, [(a, la), (b, lb)], o, l)


def final_kernel(group, *refs):
    *ins, o = refs
    blend(group, [(ins[i], ins[i + 1]) for i in range(0, len(ins), 2)], o)


def per_device(cores, queries, new_keys, new_values, cache_keys, cache_values, cache_len):
    tokens, heads, hd = queries.shape
    slots, kv, _ = cache_keys.shape
    n = lax.axis_size("ctx")
    chips = n // cores
    place = lax.axis_index("ctx")
    filled = jnp.clip(cache_len[0] - place * slots, 0, slots)
    chip, core = place // cores, place % cores

    def info(owner):
        return (owner - place) * tokens

    def over_core(x):
        return lax.ppermute(x, "ctx", [(i, i ^ 1) for i in range(n)])

    def over_chip(x, step):
        return lax.ppermute(
            x, "ctx", [(i, (i // cores + step) % chips * cores + i % cores) for i in range(n)]
        )

    part = jax.ShapeDtypeStruct(queries.shape, BF16)
    lse = jax.ShapeDtypeStruct((tokens * heads // 128, 128), F32)
    span = slots + tokens
    flops = 4 * tokens * heads * span * hd
    cost = lambda k: pl.CostEstimate(flops=k * flops, bytes_accessed=2 * 2**20, transcendentals=k * tokens * heads * span)
    q_chip = [over_chip(queries, step) for step in range(1, chips)]
    q_core = over_core(queries)
    q_diag = [over_core(q) for q in q_chip]
    sibling = place ^ 1
    own_n, own_l, sib_n, sib_l, keys, values = pl.pallas_call(
        first_kernel,
        out_shape=(
            part, lse, part, lse,
            jax.ShapeDtypeStruct((kv, span, hd), BF16),
            jax.ShapeDtypeStruct((kv, span, 2 * hd), BF16),
        ),
        in_specs=[SMEM] + [VMEM] * 6,
        out_specs=[VMEM] * 6,
        compiler_params=params(),
        cost_estimate=cost(2),
        name="own_and_sibling",
    )(jnp.stack([filled, info(place), info(sibling)]), queries, q_core, cache_keys, cache_values, new_keys, new_values)
    got = [own_n, own_l, over_core(sib_n), over_core(sib_l)]

    def attend_one(q, owner):
        return pl.pallas_call(
            next_kernel,
            out_shape=(part, lse),
            in_specs=[SMEM] + [VMEM] * 3,
            out_specs=[VMEM] * 2,
            compiler_params=params(),
            cost_estimate=cost(1),
            name="other_chip",
        )(jnp.stack([filled, info(owner)]), q, keys, values)

    for step in range(1, chips):
        from_chip = (chip - step) % chips
        d_n, d_l = attend_one(q_diag[step - 1], from_chip * cores + (1 - core))
        r_n, r_l = over_core(d_n), over_core(d_l)
        x_n, x_l = attend_one(q_chip[step - 1], from_chip * cores + core)
        c_n, c_l = pl.pallas_call(
            functools.partial(blend2_kernel, heads // kv),
            out_shape=(part, lse),
            in_specs=[VMEM] * 4,
            out_specs=[VMEM] * 2,
            compiler_params=params(),
            cost_estimate=pl.CostEstimate(flops=2**20, bytes_accessed=2**20, transcendentals=2**14),
            name="chip_sum",
        )(x_n, x_l, r_n, r_l)
        got += [over_chip(c_n, chips - step), over_chip(c_l, chips - step)]
    return pl.pallas_call(
        functools.partial(final_kernel, heads // kv),
        out_shape=part,
        in_specs=[VMEM] * len(got),
        out_specs=VMEM,
        compiler_params=params(),
        cost_estimate=pl.CostEstimate(flops=2**20, bytes_accessed=2**20, transcendentals=2**14),
        name="final_sum",
    )(*got)


def solution(mesh):
    spec = P(("conv", "ctx"), "head", None)
    return jax.shard_map(
        functools.partial(per_device, 2),
        mesh=mesh,
        in_specs=(spec,) * 5 + (P("conv"),),
        out_specs=spec,
        check_vma=False,
    )
```

time: 125 us -> 44.8 us (0.36)
  matrix products: 33.2 us -> 0 us
  Pallas kernels: 0 us -> 19 us
  local copies, waits for them, and re-layouts: 23.8 us -> 6.16 us
  other arithmetic: 14.9 us -> 0.23 us
  between operations: 13.5 us -> 0.7 us
  blocking collectives: 12.5 us -> 0 us
  waiting for transfers between devices: 19.5 us -> 12.1 us
    dot_general x11 -> x0, matrix products: 33.2 us -> none  [the longest x5 20.8 us: attend_block(): jnp.einsum('tkgs,skd->tkgd', expo.astype(jnp.bfloat16), values, preferred...]
    pallas_call x0 -> x5, Pallas kernels: none -> 19 us  [the longest x2 9.26 us: attend_one(): pl.pallas_call(next_kernel, out_shape=(part, lse), in_specs=[SMEM] + [VME...]
    all_to_all x2 -> x0, waiting for transfers between devices: 15.7 us -> none  [the longest x1 12.3 us: per_device(): lax.all_to_all(norm[None], 'ctx', split_axis=1, concat_axis=0, tiled=True)]
    while x8 -> x0, local copies, waits for them, and re-layouts: 12.9 us -> none
    all_gather x2 -> x0, blocking collectives: 12.5 us -> none  [the longest x1 6.47 us: per_device(): lax.all_gather(new_keys, 'ctx', axis=0, tiled=True)]
    ppermute x0 -> x9, waiting for transfers between devices: none -> 12.1 us  [the longest x3 11.2 us: over_chip(): lax.ppermute(x, 'ctx', [(i, (i // cores + step) % chips * cores + i % cor...]
    reduce_sum x6 -> x0, other arithmetic: 9.32 us -> none  [the longest x5 9.28 us: attend_block(): total = jnp.sum(expo, axis=-1)]
    all_to_all x2 -> x0, starting transfers between devices: 6.77 us -> none  [the longest x1 3.52 us: per_device(): lax.all_to_all(norm[None], 'ctx', split_axis=1, concat_axis=0, tiled=True)]
  transfers between devices with their start and end apart: 3 -> 9, of which waited for: 3 -> 3; matrix products, arithmetic and copies ran while one was open for 7% -> 1% of each run, Pallas kernels for 0% -> 30%
where the time goes in v1:
time: 44.8 us; the launch traced here: 44.4 us
  Pallas kernels  19 us (42%)
  waiting for transfers between devices  12.1 us (27%)
  local copies, waits for them, and re-layouts  6.16 us (14%)
  starting transfers between devices  6.12 us (14%)
  between operations  0.7 us (2%)
    ppermute x3, waiting for transfers between devices, over_chip(): lax.ppermute(x, 'ctx', [(i, (i // cores + step) % chips * cores + i % cor...  11.2 us
    pallas_call x2, Pallas kernels, attend_one(): pl.pallas_call(next_kernel, out_shape=(part, lse), in_specs=[SMEM] + [VME...  9.26 us
    pallas_call x1, Pallas kernels, per_device(): pl.pallas_call(first_kernel, out_shape=(part, lse, part, lse, jax.ShapeDt...  8.19 us
    unnamed x14, local copies, waits for them, and re-layouts  6.16 us
    ppermute x3, starting transfers between devices, over_chip(): lax.ppermute(x, 'ctx', [(i, (i // cores + step) % chips * cores + i % cor...  5.03 us
    pallas_call x1, Pallas kernels, per_device(): pl.pallas_call(functools.partial(final_kernel, heads // kv), out_shape=pa...  1.2 us
    ppermute x6, starting transfers between devices, over_core(): return lax.ppermute(x, 'ctx', [(i, i ^ 1) for i in range(n)])  1.09 us
  transfers between devices with their start and end apart: 9, of which 3 were waited for; matrix products, arithmetic and copies ran while one was open for 1% of the time, Pallas kernels for 30%

profile of v1, /device:TPU:0, one launch (start us, length us, event | category | flops | bytes accessed | tf_op | source)
XLA Modules:
  0.0 44.4 jit_solution(6967790873910943777)
XLA Ops:
  0.0 2.9 %collective-permute-start.3 = (bf16[64,16,128]{2,1,0:T(8,128)(2,1)}, bf16[64,16,128]{2,1,0:T(8,128)(2,1)S(1)}, u32[]{:S(2)}, u32[]{:S(2)}) collective-permute-start(bf16[64,16,128]{2,1,0:T(8,128)(2,1)} %qa.1), channel_id=1, source_target_pairs={{0,8},{4,12},{8,0},{12,4},{1,9},{5,13},{9,1},{13,5},{2,10},{6,14},... | collective-permute-start | bytes 786440 | tf_op jit(solution)/shard_map/ppermute | solution.py:144
  2.9 0.0 collective-permute-start
  3.6 0.1 pad_add_fusion.2.info
  3.7 5.8 %collective-permute-done.3.qa = bf16[64,16,128]{2,1,0:T(8,128)(2,1)S(1)} collective-permute-done((bf16[64,16,128]{2,1,0:T(8,128)(2,1)}, bf16[64,16,128]{2,1,0:T(8,128)(2,1)S(1)}, u32[]{:S(2)}, u32[]{:S(2)}) %collective-permute-start.3) | collective-permute-done | bytes 262176 | tf_op jit(solution)/shard_map/ppermute | solution.py:144
  9.5 0.0 collective-permute-start.4
  9.5 0.1 pad_add_fusion.info
  9.5 0.0 collective-permute-done.qb
  9.5 0.0 copy-start
  9.5 1.2 %copy-done = bf16[2048,2,128]{2,1,0:T(2,128)(2,1)S(1)} copy-done((bf16[2048,2,128]{2,1,0:T(2,128)(2,1)S(1)}, bf16[2048,2,128]{2,1,0:T(2,128)(2,1)}, u32[]{:S(2)}) %copy-start) | copy-done | bytes 1048600
  10.8 0.0 copy-start.1
  10.8 1.2 %copy-done.1 = bf16[2048,2,128]{2,1,0:T(2,128)(2,1)S(1)} copy-done((bf16[2048,2,128]{2,1,0:T(2,128)(2,1)S(1)}, bf16[2048,2,128]{2,1,0:T(2,128)(2,1)}, u32[]{:S(2)}) %copy-start.1) | copy-done | bytes 1048600
  12.0 0.0 copy-start.2
  12.0 0.9 %copy-done.2 = bf16[64,16,128]{2,1,0:T(8,128)(2,1)S(1)} copy-done((bf16[64,16,128]{2,1,0:T(8,128)(2,1)S(1)}, bf16[64,16,128]{2,1,0:T(8,128)(2,1)}, u32[]{:S(2)}) %copy-start.2) | copy-done | bytes 262168
  12.9 0.0 copy-start.3
  12.9 0.8 %copy-done.3 = bf16[64,2,128]{2,1,0:T(2,128)(2,1)S(1)} copy-done((bf16[64,2,128]{2,1,0:T(2,128)(2,1)S(1)}, bf16[64,2,128]{2,1,0:T(2,128)(2,1)}, u32[]{:S(2)}) %copy-start.3) | copy-done | bytes 32792
  13.7 0.0 copy-start.4
  13.7 0.8 %copy-done.4 = bf16[64,2,128]{2,1,0:T(2,128)(2,1)S(1)} copy-done((bf16[64,2,128]{2,1,0:T(2,128)(2,1)S(1)}, bf16[64,2,128]{2,1,0:T(2,128)(2,1)}, u32[]{:S(2)}) %copy-start.4) | copy-done | bytes 32792
  14.5 8.2 %own_and_sibling.1 = (bf16[64,16,128]{2,1,0:T(8,128)(2,1)S(1)}, f32[8,128]{1,0:T(8,128)S(1)}, bf16[64,16,128]{2,1,0:T(8,128)(2,1)S(1)}, f32[8,128]{1,0:T(8,128)S...) custom-call(s32[3]{0:T(128)S(1)} %pad_add_fusion.info, bf16[64,16,128]{2,1,0:T(8,128)(2,1)S(1)} %copy-done.2, ...), custom_call_target="tpu_custom_call" | custom-call | flops 2214592512 | bytes 2097152 | tf_op jit(solution)/shard_map/own_and_sibling/pallas_call | solution.py:157
  22.6 0.0 copy-start.5
  22.6 0.0 collective-permute-done.4.qa
  22.7 4.6 %other_chip.3 = (bf16[64,16,128]{2,1,0:T(8,128)(2,1)S(1)}, f32[8,128]{1,0:T(8,128)S(1)}) custom-call(s32[2]{0:T(128)S(1)} %pad_add_fusion.2.info, bf16[64,16,128]{2,1,0:T(8,128)(2,1)S(1)} %collective-permute-done.4.qa, bf16[2,2112,128]{2,1,0:T(8,128)(2,1)S(1)} %get-tuple-element.21.keys, bf16[2,2112,256]{2,1,0:T(8,128)(2,1)S(1)} %get-tuple-element.22.values), custom_call_target="tpu_custom_call" | custom-call | flops 1107296256 | bytes 2097152 | tf_op jit(solution)/shard_map/other_chip/pallas_call | solution.py:173
  27.2 0.0 copy-done.5
  27.2 0.6 %collective-permute-start.5 = (bf16[64,16,128]{2,1,0:T(8,128)(2,1)S(1)}, bf16[64,16,128]{2,1,0:T(8,128)(2,1)S(1)}, u32[]{:S(2)}, u32[]{:S(2)}) collective-permute-start(bf16[64,16,128]{2,1,0:T(8,128)(2,1)S(1)} %get-tuple-element.25), channel_id=1, source_target_pairs={{0,4},{4,0},{8,12},{12,8},{1,5},{5,1},{9,13},{13,9},{2,6},{6,2},{1... | collective-permute-start | bytes 786440 | tf_op jit(solution)/shard_map/ppermute | solution.py:141
  27.8 0.1 pad_add_fusion.1.info
  27.9 0.0 collective-permute-start.1
  27.9 0.5 %collective-permute-start.6 = (f32[8,128]{1,0:T(8,128)S(1)}, f32[8,128]{1,0:T(8,128)S(1)}, u32[]{:S(2)}, u32[]{:S(2)}) collective-permute-start(f32[8,128]{1,0:T(8,128)S(1)} %get-tuple-element.26), channel_id=1, source_target_pairs={{0,4},{4,0},{8,12},{12,8},{1,5},{5,1},{9,13},{13,9},{2,6},{6,2},{1... | collective-permute-start | bytes 12296 | tf_op jit(solution)/shard_map/ppermute | solution.py:141
  28.4 0.0 copy-start.6
  28.4 1.2 %copy-done.6 = bf16[2,2112,128]{2,1,0:T(8,128)(2,1)S(1)} copy-done((bf16[2,2112,128]{2,1,0:T(8,128)(2,1)S(1)}, bf16[2,2112,128]{2,1,0:T(8,128)(2,1)}, u32[]{:S(2)}) %copy-start.6) | copy-done | bytes 1081368
  29.6 4.7 %other_chip.2 = (bf16[64,16,128]{2,1,0:T(8,128)(2,1)S(1)}, f32[8,128]{1,0:T(8,128)S(1)}) custom-call(s32[2]{0:T(128)S(1)} %pad_add_fusion.1.info, bf16[64,16,128]{2,1,0:T(8,128)(2,1)S(1)} %collective-permute-done.3.qa, bf16[2,2112,128]{2,1,0:T(8,128)(2,1)S(1)} %copy-done.6, bf16[2,2112,256]{2,1,0:T(8,128)(2,1)S(1)} %get-tuple-element.22.values), custom_call_target="tpu_custom_call" | custom-call | flops 1107296256 | bytes 2097152 | tf_op jit(solution)/shard_map/other_chip/pallas_call | solution.py:173
  34.3 0.0 collective-permute-done.6.lb
  34.3 0.0 collective-permute-done.5.b
  34.3 0.4 chip_sum.1
  34.7 1.8 %collective-permute-start.7 = (bf16[64,16,128]{2,1,0:T(8,128)(2,1)S(1)}, bf16[64,16,128]{2,1,0:T(8,128)(2,1)S(1)}, u32[]{:S(2)}, u32[]{:S(2)}) collective-permute-start(bf16[64,16,128]{2,1,0:T(8,128)(2,1)S(1)} %get-tuple-element.27), channel_id=1, source_target_pairs={{0,8},{4,12},{8,0},{12,4},{1,9},{5,13},{9,1},{13,5},{2,10},{6,14},... | collective-permute-start | bytes 786440 | tf_op jit(solution)/shard_map/ppermute | solution.py:144
  36.5 0.0 collective-permute-start.2
  36.5 0.3 collective-permute-start.8
  36.8 0.9 %collective-permute-done.2.refs_3_ = f32[8,128]{1,0:T(8,128)S(1)} collective-permute-done((f32[8,128]{1,0:T(8,128)S(1)}, f32[8,128]{1,0:T(8,128)S(1)}, u32[]{:S(2)}, u32[]{:S(2)}) %collective-permute-start.2) | collective-permute-done | bytes 4128 | tf_op jit(solution)/shard_map/ppermute | solution.py:141
  37.7 0.0 collective-permute-done.1.refs_2_
  37.7 5.5 %collective-permute-done.8.refs_5_ = f32[8,128]{1,0:T(8,128)S(1)} collective-permute-done((f32[8,128]{1,0:T(8,128)S(1)}, f32[8,128]{1,0:T(8,128)S(1)}, u32[]{:S(2)}, u32[]{:S(2)}) %collective-permute-start.8) | collective-permute-done | bytes 4128 | tf_op jit(solution)/shard_map/ppermute | solution.py:144
  43.2 0.0 collective-permute-done.7.refs_4_
  43.2 1.2 %final_sum.1 = bf16[64,16,128]{2,1,0:T(8,128)(2,1)} custom-call(bf16[64,16,128]{2,1,0:T(8,128)(2,1)S(1)} %get-tuple-element.17.refs_0_, f32[8,128]{1,0:T(8,128)S(1)} %get-tuple-element.18.refs_1_, bf16[64,16,128]{2,1,0:T(8,128)(2,1)S(1)} %collective-permute-done.1.refs_2_, f32[8,128]{1,0:T(8,128)S(1)} %collective-permute-done.2.refs_3_, ...), custom_call_target="tpu_custom_call" | custom-call | flops 1048576 | bytes 1048576 | tf_op jit(solution)/shard_map/final_sum/pallas_call | solution.py:198
Async XLA Ops:
  0.0 9.5 %collective-permute-start.3 = (bf16[64,16,128]{2,1,0:T(8,128)(2,1)}, bf16[64,16,128]{2,1,0:T(8,128)(2,1)S(1)}, u32[]{:S(2)}, u32[]{:S(2)}) collective-permute-start(bf16[64,16,128]{2,1,0:T(8,128)(2,1)} %qa.1), channel_id=1, source_target_pairs={{0,8},{4,12},{8,0},{12,4},{1,9},{5,13},{9,1},{13,5},{2,10},{6,14},... | collective-permute-start | bytes 786440 | tf_op jit(solution)/shard_map/ppermute | solution.py:144
  2.9 6.6 %collective-permute-start = (bf16[64,16,128]{2,1,0:T(8,128)(2,1)}, bf16[64,16,128]{2,1,0:T(8,128)(2,1)S(1)}, u32[]{:S(2)}, u32[]{:S(2)}) collective-permute-start(bf16[64,16,128]{2,1,0:T(8,128)(2,1)} %qa.1), channel_id=1, source_target_pairs={{0,4},{4,0},{8,12},{12,8},{1,5},{5,1},{9,13},{13,9},{2,6},{6,2},{1... | collective-permute-start | bytes 786440 | tf_op jit(solution)/shard_map/ppermute | solution.py:141
  9.5 13.2 %collective-permute-start.4 = (bf16[64,16,128]{2,1,0:T(8,128)(2,1)S(1)}, bf16[64,16,128]{2,1,0:T(8,128)(2,1)S(1)}, u32[]{:S(2)}, u32[]{:S(2)}) collective-permute-start(bf16[64,16,128]{2,1,0:T(8,128)(2,1)S(1)} %collective-permute-done.3.qa), channel_id=1, source_target_pairs={{0,4},{4,0},{8,12},{12,8},{1,5},{5,1},{9,13},{13,9},{2,6},{6,2},{1... | collective-permute-start | bytes 786440 | tf_op jit(solution)/shard_map/ppermute | solution.py:141
  9.5 1.2 %copy-start = (bf16[2048,2,128]{2,1,0:T(2,128)(2,1)S(1)}, bf16[2048,2,128]{2,1,0:T(2,128)(2,1)}, u32[]{:S(2)}) copy-start(bf16[2048,2,128]{2,1,0:T(2,128)(2,1)} %k.1) | copy-start | bytes 3145732
  10.8 1.2 %copy-start.1 = (bf16[2048,2,128]{2,1,0:T(2,128)(2,1)S(1)}, bf16[2048,2,128]{2,1,0:T(2,128)(2,1)}, u32[]{:S(2)}) copy-start(bf16[2048,2,128]{2,1,0:T(2,128)(2,1)} %v.1) | copy-start | bytes 3145732
  12.0 0.9 %copy-start.2 = (bf16[64,16,128]{2,1,0:T(8,128)(2,1)S(1)}, bf16[64,16,128]{2,1,0:T(8,128)(2,1)}, u32[]{:S(2)}) copy-start(bf16[64,16,128]{2,1,0:T(8,128)(2,1)} %qa.1) | copy-start | bytes 786436
  12.9 0.8 %copy-start.3 = (bf16[64,2,128]{2,1,0:T(2,128)(2,1)S(1)}, bf16[64,2,128]{2,1,0:T(2,128)(2,1)}, u32[]{:S(2)}) copy-start(bf16[64,2,128]{2,1,0:T(2,128)(2,1)} %nk.1) | copy-start | bytes 98308
  13.7 0.8 %copy-start.4 = (bf16[64,2,128]{2,1,0:T(2,128)(2,1)S(1)}, bf16[64,2,128]{2,1,0:T(2,128)(2,1)}, u32[]{:S(2)}) copy-start(bf16[64,2,128]{2,1,0:T(2,128)(2,1)} %nv.1) | copy-start | bytes 98308
  22.6 4.6 %copy-start.5 = (bf16[2,2112,128]{2,1,0:T(8,128)(2,1)}, bf16[2,2112,128]{2,1,0:T(8,128)(2,1)S(1)}, u32[]{:S(2)}) copy-start(bf16[2,2112,128]{2,1,0:T(8,128)(2,1)S(1)} %get-tuple-element.21.keys) | copy-start | bytes 3244036
  27.2 7.1 %collective-permute-start.5 = (bf16[64,16,128]{2,1,0:T(8,128)(2,1)S(1)}, bf16[64,16,128]{2,1,0:T(8,128)(2,1)S(1)}, u32[]{:S(2)}, u32[]{:S(2)}) collective-permute-start(bf16[64,16,128]{2,1,0:T(8,128)(2,1)S(1)} %get-tuple-element.25), channel_id=1, source_target_pairs={{0,4},{4,0},{8,12},{12,8},{1,5},{5,1},{9,13},{13,9},{2,6},{6,2},{1... | collective-permute-start | bytes 786440 | tf_op jit(solution)/shard_map/ppermute | solution.py:141
  27.9 9.8 %collective-permute-start.1 = (bf16[64,16,128]{2,1,0:T(8,128)(2,1)S(1)}, bf16[64,16,128]{2,1,0:T(8,128)(2,1)S(1)}, u32[]{:S(2)}, u32[]{:S(2)}) collective-permute-start(bf16[64,16,128]{2,1,0:T(8,128)(2,1)S(1)} %get-tuple-element.19), channel_id=1, source_target_pairs={{0,4},{4,0},{8,12},{12,8},{1,5},{5,1},{9,13},{13,9},{2,6},{6,2},{1... | collective-permute-start | bytes 786440 | tf_op jit(solution)/shard_map/ppermute | solution.py:141
  27.9 6.4 %collective-permute-start.6 = (f32[8,128]{1,0:T(8,128)S(1)}, f32[8,128]{1,0:T(8,128)S(1)}, u32[]{:S(2)}, u32[]{:S(2)}) collective-permute-start(f32[8,128]{1,0:T(8,128)S(1)} %get-tuple-element.26), channel_id=1, source_target_pairs={{0,4},{4,0},{8,12},{12,8},{1,5},{5,1},{9,13},{13,9},{2,6},{6,2},{1... | collective-permute-start | bytes 12296 | tf_op jit(solution)/shard_map/ppermute | solution.py:141
  28.4 1.2 %copy-start.6 = (bf16[2,2112,128]{2,1,0:T(8,128)(2,1)S(1)}, bf16[2,2112,128]{2,1,0:T(8,128)(2,1)}, u32[]{:S(2)}) copy-start(bf16[2,2112,128]{2,1,0:T(8,128)(2,1)} %copy-done.5) | copy-start | bytes 3244036
  34.7 8.4 %collective-permute-start.7 = (bf16[64,16,128]{2,1,0:T(8,128)(2,1)S(1)}, bf16[64,16,128]{2,1,0:T(8,128)(2,1)S(1)}, u32[]{:S(2)}, u32[]{:S(2)}) collective-permute-start(bf16[64,16,128]{2,1,0:T(8,128)(2,1)S(1)} %get-tuple-element.27), channel_id=1, source_target_pairs={{0,8},{4,12},{8,0},{12,4},{1,9},{5,13},{9,1},{13,5},{2,10},{6,14},... | collective-permute-start | bytes 786440 | tf_op jit(solution)/shard_map/ppermute | solution.py:144
  36.5 1.2 %collective-permute-start.2 = (f32[8,128]{1,0:T(8,128)S(1)}, f32[8,128]{1,0:T(8,128)S(1)}, u32[]{:S(2)}, u32[]{:S(2)}) collective-permute-start(f32[8,128]{1,0:T(8,128)S(1)} %get-tuple-element.20), channel_id=1, source_target_pairs={{0,4},{4,0},{8,12},{12,8},{1,5},{5,1},{9,13},{13,9},{2,6},{6,2},{1... | collective-permute-start | bytes 12296 | tf_op jit(solution)/shard_map/ppermute | solution.py:141
  36.5 6.6 %collective-permute-start.8 = (f32[8,128]{1,0:T(8,128)S(1)}, f32[8,128]{1,0:T(8,128)S(1)}, u32[]{:S(2)}, u32[]{:S(2)}) collective-permute-start(f32[8,128]{1,0:T(8,128)S(1)} %get-tuple-element.28), channel_id=1, source_target_pairs={{0,8},{4,12},{8,0},{12,4},{1,9},{5,13},{9,1},{13,5},{2,10},{6,14},... | collective-permute-start | bytes 12296 | tf_op jit(solution)/shard_map/ppermute | solution.py:144

commit v2 on v0

v2 whole, which is shorter than its diff:
```python
import functools
import math

import jax
import jax.numpy as jnp
from jax import lax
from jax.experimental import pallas as pl
from jax.experimental.pallas import tpu as pltpu
from jax.sharding import PartitionSpec as P

NEG_FILL = -1e30
LOG2E = 1.4426950408889634
VMEM = pl.BlockSpec(memory_space=pltpu.VMEM)
SMEM = pl.BlockSpec(memory_space=pltpu.SMEM)
HBM = pl.BlockSpec(memory_space=pltpu.HBM)
F32 = jnp.float32
BF16 = jnp.bfloat16
NT = (((1,), (1,)), ((), ()))
CORES = 2


def params():
    return pltpu.CompilerParams(vmem_limit_bytes=36 * 2**20)


def pack_rows(wide):
    eye = lax.broadcasted_iota(jnp.int32, (128, 128), 0) == lax.broadcasted_iota(jnp.int32, (128, 128), 1)
    return jnp.concatenate(
        [
            jnp.sum(jnp.where(eye, wide[i * 128 : (i + 1) * 128], 0.0), axis=0, keepdims=True)
            for i in range(wide.shape[0] // 128)
        ],
        axis=0,
    )


def spread_rows(packed):
    return jnp.concatenate(
        [jnp.transpose(jnp.broadcast_to(packed[i : i + 1, :], (128, 128))) for i in range(packed.shape[0])], axis=0
    )


def place_keys(filled, raw, new, keys):
    slots, kv, hd = raw.shape
    fresh = jnp.swapaxes(new[...], 0, 1)
    keys[:, slots:] = fresh

    @pl.when(filled == slots)
    def _():
        keys[:, 0:slots] = jnp.swapaxes(raw[...], 0, 1)

    @pl.when(filled < slots)
    def _():
        rows = jnp.swapaxes(raw[...], 0, 1)
        included = lax.broadcasted_iota(jnp.int32, (slots, hd), 0) < filled
        for h in range(kv):
            fill = jnp.where(filled > 0, rows[h, 0:1, :].astype(F32), fresh[h, 0:1, :].astype(F32))
            keys[h, 0:slots] = jnp.where(included, rows[h].astype(F32), fill).astype(BF16)


def place_values(filled, raw, new, values):
    slots, kv, hd = raw.shape
    fresh = new.shape[0]
    values[:, slots:, 0:hd] = jnp.swapaxes(new[...], 0, 1)
    values[:, slots:, hd:] = jnp.ones((kv, fresh, hd), BF16)

    @pl.when(filled == slots)
    def _():
        values[:, 0:slots, 0:hd] = jnp.swapaxes(raw[...], 0, 1)
        values[:, 0:slots, hd:] = jnp.ones((kv, slots, hd), BF16)

    @pl.when(filled < slots)
    def _():
        rows = jnp.swapaxes(raw[...], 0, 1)
        included = lax.broadcasted_iota(jnp.int32, (slots, hd), 0) < filled
        for h in range(kv):
            values[h, 0:slots, 0:hd] = jnp.where(included, rows[h].astype(F32), 0.0).astype(BF16)
            values[h, 0:slots, hd:] = jnp.where(included, 1.0, 0.0).astype(BF16)


def put_lse(ref, first, lse):
    heads = ref.shape[1]
    high = lse.astype(BF16).astype(F32)
    middle = (lse - high).astype(BF16).astype(F32)
    low = lse - high - middle
    extra = ref.shape[0] - first
    rest = jnp.zeros((extra * heads - 3 * lse.shape[0], 128), F32)
    rows = jnp.concatenate([high, middle, low, rest], axis=0)
    ref[first:] = rows.astype(BF16).reshape(extra, heads, 128)


def get_lse(ref, first):
    heads = ref.shape[1]
    n = first * heads // 128
    rows = ref[first:].astype(F32).reshape((ref.shape[0] - first) * heads, 128)
    return rows[0:n] + rows[n : 2 * n] + rows[2 * n : 3 * n]


def packed_shape(tokens, heads, hd):
    extra = -(-3 * (tokens * heads // 128) // heads)
    return jax.ShapeDtypeStruct((tokens + extra, heads, hd), BF16)


def attend(offset, fresh, q_ref, keys, values, parts, before_values=None):
    heads, hd = q_ref.shape[1:]
    kv, span, _ = keys.shape
    group = heads // kv
    slots = span - fresh
    scale = LOG2E / math.sqrt(hd)
    work = [(first, n, h, o) for first, n, o in parts for h in range(kv)]

    def scores(item):
        first, n, h, _ = item
        q = q_ref[first : first + n, h * group : (h + 1) * group, :].reshape(n * group, hd)
        s = lax.dot_general(q, keys[h, 0:slots], NT, preferred_element_type=F32)
        s2 = lax.dot_general(q, keys[h, slots:], NT, preferred_element_type=F32)
        return s, s2

    s, s2 = scores(work[0])
    if before_values is not None:
        before_values()
    lses = []
    for i, (first, n, h, o_ref) in enumerate(work):
        later = scores(work[i + 1]) if i + 1 < len(work) else (None, None)
        rows = n * group
        token = first + lax.broadcasted_iota(jnp.int32, (rows, fresh), 0) // group
        seen = token + offset >= lax.broadcasted_iota(jnp.int32, (rows, fresh), 1)
        s2 = jnp.where(seen, s2, NEG_FILL)
        peak = jnp.maximum(jnp.max(s, axis=-1, keepdims=True), jnp.max(s2, axis=-1, keepdims=True))
        w = jnp.exp2((s - peak) * scale).astype(BF16)
        w2 = jnp.where(seen, jnp.exp2((s2 - peak) * scale), 0.0).astype(BF16)
        out = jnp.dot(w, values[h, 0:slots], preferred_element_type=F32)
        out = out + jnp.dot(w2, values[h, slots:], preferred_element_type=F32)
        total = out[:, hd:]
        floored = jnp.maximum(total, 1.0)
        o_ref[0:n, h * group : (h + 1) * group, :] = (out[:, 0:hd] / floored).astype(BF16).reshape(n, group, hd)
        lses.append(pack_rows(jnp.where(total > 0.0, peak * (1.0 / math.sqrt(hd)) + jnp.log(floored), NEG_FILL)))
        if h == kv - 1:
            put_lse(o_ref, n, jnp.concatenate(lses, axis=0))
            lses = []
        s, s2 = later


def blend(parts, group):
    tokens, heads, hd = parts[0][0].shape
    top = functools.reduce(jnp.maximum, [lse for _, lse in parts])
    scales = [jnp.exp(lse - top) for _, lse in parts]
    total = functools.reduce(jnp.add, scales)
    lse = jnp.where(top > 0.5 * NEG_FILL, top + jnp.log(total), NEG_FILL)
    inv = 1.0 / total
    n = tokens * group // 128
    outs = []
    for h in range(heads // group):
        acc = None
        for (norm, _), s in zip(parts, scales):
            wide = spread_rows((s * inv)[h * n : (h + 1) * n, :])
            term = norm[:, h * group : (h + 1) * group, :].reshape(tokens * group, hd).astype(F32) * wide
            acc = term if acc is None else acc + term
        outs.append(acc)
    return outs, lse


def own_kernel(length, q, k, v, nk, nv, o, keys, values, q_in, k_in, v_in, nk_in, nv_in, sems):
    copies = [
        pltpu.make_async_copy(src, dst, sems.at[i])
        for i, (src, dst) in enumerate([(k, k_in), (nk, nk_in), (q, q_in), (v, v_in), (nv, nv_in)])
    ]
    for c in copies:
        c.start()
    slots = k.shape[0]
    filled = jnp.clip(length[0] - lax.axis_index("ctx") * slots, 0, slots)
    for c in copies[0:3]:
        c.wait()
    place_keys(filled, k_in, nk_in, keys)

    def fetch_values():
        for c in copies[3:]:
            c.wait()
        place_values(filled, v_in, nv_in, values)

    attend(0, nk.shape[0], q_in, keys, values, [(0, q.shape[0], o)], fetch_values)


def other_kernel(owner, first, n, q, keys, values, o):
    place = lax.axis_index("ctx")
    tokens = q.shape[0]
    attend((owner(place) - place) * tokens, tokens, q, keys, values, [(first, n, o)])


def chip_sum_kernel(group, first, n, tokens, a, b, o):
    heads, hd = a.shape[1:]
    lse_b = cut_lse(get_lse(b, tokens), heads // group, first, n, tokens)
    outs, lse = blend([(a[0:n], get_lse(a, n)), (b[first : first + n], lse_b)], group)
    for h, x in enumerate(outs):
        o[0:n, h * group : (h + 1) * group, :] = x.astype(BF16).reshape(n, group, hd)
    put_lse(o, n, lse)


def cut_lse(lse, kv, first, n, tokens):
    per = lse.shape[0] // kv
    a, b = first * per // tokens, (first + n) * per // tokens
    return jnp.concatenate([lse[h * per + a : h * per + b] for h in range(kv)], axis=0)


def near_kernel(group, own, sib, o, l):
    tokens, heads, hd = o.shape
    outs, lse = blend([(x[0:tokens], get_lse(x, tokens)) for x in (own, sib)], group)
    for h, x in enumerate(outs):
        o[:, h * group : (h + 1) * group, :] = x.reshape(tokens, group, hd)
    l[...] = lse


def final_kernel(group, halves, near, near_l, *refs):
    *far, o = refs
    tokens, heads, hd = o.shape
    n = tokens // halves
    for i in range(halves):
        first = i * n
        lse = cut_lse(near_l[...], heads // group, first, n, tokens)
        parts = [(near[first : first + n], lse)] + [(x[0:n], get_lse(x, n)) for x in far[i::halves]]
        outs, _ = blend(parts, group)
        for h, x in enumerate(outs):
            o[first : first + n, h * group : (h + 1) * group, :] = x.astype(BF16).reshape(n, group, hd)


def per_device(queries, new_keys, new_values, cache_keys, cache_values, cache_len):
    tokens, heads, hd = queries.shape
    slots, kv, _ = cache_keys.shape
    group = heads // kv
    n = lax.axis_size("ctx")
    chips = n // CORES
    halves = 2
    span = slots + tokens

    def over_core(x):
        return lax.ppermute(x, "ctx", [(i, i ^ 1) for i in range(n)])

    def over_chip(x, step):
        return lax.ppermute(x, "ctx", [(i, (i // CORES + step) % chips * CORES + i % CORES) for i in range(n)])

    def packed(m):
        return packed_shape(m, heads, hd)

    def cost(m):
        return pl.CostEstimate(
            flops=8 * m * heads * span * hd, bytes_accessed=4 * 2**20, transcendentals=m * heads * span
        )

    def call(name, kernel, out, args, estimate):
        return pl.pallas_call(
            kernel,
            out_shape=out,
            in_specs=[VMEM] * len(args),
            out_specs=jax.tree.map(lambda _: VMEM, out),
            compiler_params=params(),
            cost_estimate=estimate,
            name=name,
        )(*args)

    small = pl.CostEstimate(flops=2**20, bytes_accessed=2**20, transcendentals=2**14)
    q_chip = [over_chip(queries, step) for step in range(1, chips)]
    q_core = over_core(queries)
    pinned = [
        pltpu.with_memory_space_constraint(x, pltpu.HBM)
        for x in (queries, cache_keys, cache_values, new_keys, new_values)
    ]
    own, keys, values = pl.pallas_call(
        own_kernel,
        out_shape=[
            packed(tokens),
            jax.ShapeDtypeStruct((kv, span, hd), BF16),
            jax.ShapeDtypeStruct((kv, span, 2 * hd), BF16),
        ],
        in_specs=[SMEM] + [HBM] * 5,
        out_specs=[VMEM] * 3,
        scratch_shapes=[
            pltpu.VMEM(queries.shape, BF16),
            pltpu.VMEM(cache_keys.shape, BF16),
            pltpu.VMEM(cache_values.shape, BF16),
            pltpu.VMEM(new_keys.shape, BF16),
            pltpu.VMEM(new_values.shape, BF16),
            pltpu.SemaphoreType.DMA((5,)),
        ],
        compiler_params=params(),
        cost_estimate=cost(tokens),
        name="own",
    )(cache_len, *pinned)
    *q_chip, own = lax.optimization_barrier((*q_chip, own))
    q_diag = [over_core(q) for q in q_chip]

    def attend_other(name, q, owner, first, m):
        return call(name, functools.partial(other_kernel, owner, first, m), packed(m), (q, keys, values), cost(m))

    sib = over_core(attend_other("sibling", q_core, lambda i: i ^ 1, 0, tokens))
    m = tokens // halves
    far = []
    for step in range(1, chips):
        def same(i, step=step):
            return (i // CORES - step + chips) % chips * CORES + i % CORES

        diag = over_core(attend_other("diagonal", q_diag[step - 1], lambda i: same(i) ^ 1, 0, tokens))
        for i in range(halves):
            straight = attend_other("straight", q_chip[step - 1], same, i * m, m)
            both = call(
                "chip_sum", functools.partial(chip_sum_kernel, group, i * m, m, tokens), packed(m), (straight, diag), small
            )
            far.append(over_chip(both, chips - step))
    near = call(
        "near",
        functools.partial(near_kernel, group),
        [jax.ShapeDtypeStruct(queries.shape, F32), jax.ShapeDtypeStruct((tokens * heads // 128, 128), F32)],
        (own, sib),
        small,
    )
    return call(
        "final",
        functools.partial(final_kernel, group, halves),
        jax.ShapeDtypeStruct(queries.shape, BF16),
        (*near, *far),
        small,
    )


def solution(mesh):
    spec = P(("conv", "ctx"), "head", None)
    return jax.shard_map(
        per_device,
        mesh=mesh,
        in_specs=(spec,) * 5 + (P("conv"),),
        out_specs=spec,
        check_vma=False,
    )
```

time: 125 us -> 32.6 us (0.26)
  matrix products: 33.2 us -> 0 us
  local copies, waits for them, and re-layouts: 23.8 us -> 0.01 us
  Pallas kernels: 0 us -> 18.6 us
  other arithmetic: 14.9 us -> 0 us
  between operations: 13.5 us -> 0.72 us
  waiting for transfers between devices: 19.5 us -> 6.86 us
  blocking collectives: 12.5 us -> 0 us
    dot_general x11 -> x0, matrix products: 33.2 us -> none  [the longest x5 20.8 us: attend_block(): jnp.einsum('tkgs,skd->tkgd', expo.astype(jnp.bfloat16), values, preferred...]
    pallas_call x0 -> x9, Pallas kernels: none -> 18.6 us  [the longest x8 11.2 us: call(): pl.pallas_call(kernel, out_shape=out, in_specs=[VMEM] * len(args), out_sp...]
    all_to_all x2 -> x0, waiting for transfers between devices: 15.7 us -> none  [the longest x1 12.3 us: per_device(): lax.all_to_all(norm[None], 'ctx', split_axis=1, concat_axis=0, tiled=True)]
    while x8 -> x0, local copies, waits for them, and re-layouts: 12.9 us -> none
    all_gather x2 -> x0, blocking collectives: 12.5 us -> none  [the longest x1 6.47 us: per_device(): lax.all_gather(new_keys, 'ctx', axis=0, tiled=True)]
    reduce_sum x6 -> x0, other arithmetic: 9.32 us -> none  [the longest x5 9.28 us: attend_block(): total = jnp.sum(expo, axis=-1)]
    ppermute x0 -> x7, waiting for transfers between devices: none -> 6.86 us  [the longest x3 5.83 us: over_chip(): lax.ppermute(x, 'ctx', [(i, (i // CORES + step) % chips * CORES + i % COR...]
    all_to_all x2 -> x0, starting transfers between devices: 6.77 us -> none  [the longest x1 3.52 us: per_device(): lax.all_to_all(norm[None], 'ctx', split_axis=1, concat_axis=0, tiled=True)]
  transfers between devices with their start and end apart: 3 -> 7, of which waited for: 3 -> 3; matrix products, arithmetic and copies ran while one was open for 7% -> 0% of each run, Pallas kernels for 0% -> 54%
where the time goes in v2:
time: 32.6 us; the launch traced here: 32.5 us
  Pallas kernels  18.6 us (57%)
  waiting for transfers between devices  6.86 us (21%)
  starting transfers between devices  6.3 us (19%)
  between operations  0.72 us (2%)
    pallas_call x8, Pallas kernels, call(): pl.pallas_call(kernel, out_shape=out, in_specs=[VMEM] * len(args), out_sp...  11.2 us
    pallas_call x1, Pallas kernels, per_device(): pl.pallas_call(own_kernel, out_shape=[packed(tokens), jax.ShapeDtypeStruc...  7.38 us
    ppermute x3, waiting for transfers between devices, over_chip(): lax.ppermute(x, 'ctx', [(i, (i // CORES + step) % chips * CORES + i % COR...  5.83 us
    ppermute x3, starting transfers between devices, over_chip(): lax.ppermute(x, 'ctx', [(i, (i // CORES + step) % chips * CORES + i % COR...  5.09 us
    ppermute x4, starting transfers between devices, over_core(): return lax.ppermute(x, 'ctx', [(i, i ^ 1) for i in range(n)])  1.2 us
    ppermute x4, waiting for transfers between devices, over_core(): return lax.ppermute(x, 'ctx', [(i, i ^ 1) for i in range(n)])  1.03 us
  transfers between devices with their start and end apart: 7, of which 3 were waited for; matrix products, arithmetic and copies ran while one was open for 0% of the time, Pallas kernels for 54%

profile of v2, /device:TPU:0, one launch (start us, length us, event | category | flops | bytes accessed | tf_op | source)
XLA Modules:
  0.0 32.5 jit_solution(11362067417337136676)
XLA Ops:
  0.0 2.9 %collective-permute-start = (bf16[64,16,128]{2,1,0:T(8,128)(2,1)}, bf16[64,16,128]{2,1,0:T(8,128)(2,1)S(1)}, u32[]{:S(2)}, u32[]{:S(2)}) collective-permute-start(bf16[64,16,128]{2,1,0:T(8,128)(2,1)} %q.1), channel_id=1, source_target_pairs={{0,8},{4,12},{8,0},{12,4},{1,9},{5,13},{9,1},{13,5},{2,10},{6,14},... | collective-permute-start | bytes 786440 | tf_op jit(solution)/shard_map/ppermute | solution.py:239
  3.6 0.0 copy-start
  3.6 7.4 %own.1 = (bf16[66,16,128]{2,1,0:T(8,128)(2,1)S(1)}, bf16[2,2112,128]{2,1,0:T(8,128)(2,1)S(1)}, bf16[2,2112,256]{2,1,0:T(8,128)(2,1)S(1)}) custom-call(s32[1]{0:T(128)S(6)} %copy.7.length, bf16[64,16,128]{2,1,0:T(8,128)(2,1)} %q.1, bf16[2048,2,128]{2,1,0:T(2,128)(2,1)} %k.1, bf16[2048,2,128]{2,1,0:T(2,128)(2,1)} %v.1, bf16[64,2,128]{2,1,0:T(2,128)(2,1)} %nk.1, ...), custom_call_target="tpu_custom_call" | custom-call | flops 2214592512 | bytes 4194304 | tf_op jit(solution)/shard_map/own/pallas_call | solution.py:267
  11.0 0.0 collective-permute-done.q
  11.0 0.1 collective-permute-start.3
  11.1 0.0 copy-done
  11.1 0.5 %collective-permute-start.1 = (bf16[64,16,128]{2,1,0:T(8,128)(2,1)S(1)}, bf16[64,16,128]{2,1,0:T(8,128)(2,1)S(1)}, u32[]{:S(2)}, u32[]{:S(2)}) collective-permute-start(bf16[64,16,128]{2,1,0:T(8,128)(2,1)S(1)} %copy-done), channel_id=1, source_target_pairs={{0,4},{4,0},{8,12},{12,8},{1,5},{5,1},{9,13},{13,9},{2,6},{6,2},{1... | collective-permute-start | bytes 786440 | tf_op jit(solution)/shard_map/ppermute | solution.py:236
  11.6 1.0 %collective-permute-done.3.q = bf16[64,16,128]{2,1,0:T(8,128)(2,1)S(1)} collective-permute-done((bf16[64,16,128]{2,1,0:T(8,128)(2,1)S(1)}, bf16[64,16,128]{2,1,0:T(8,128)(2,1)S(1)}, u32[]{:S(2)}, u32[]{:S(2)}) %collective-permute-start.3) | collective-permute-done | bytes 262176 | tf_op jit(solution)/shard_map/ppermute | solution.py:236
  12.6 3.0 %diagonal.1 = bf16[66,16,128]{2,1,0:T(8,128)(2,1)S(1)} custom-call(bf16[64,16,128]{2,1,0:T(8,128)(2,1)S(1)} %collective-permute-done.3.q, bf16[2,2112,128]{2,1,0:T(8,128)(2,1)S(1)} %get-tuple-element.14.keys, bf16[2,2112,256]{2,1,0:T(8,128)(2,1)S(1)} %get-tuple-element.15.values), custom_call_target="tpu_custom_call" | custom-call | flops 2214592512 | bytes 4194304 | tf_op jit(solution)/shard_map/diagonal/pallas_call | solution.py:250
  15.6 0.2 collective-permute-start.4
  15.8 0.0 collective-permute-done.1.q
  15.8 3.0 %sibling.1 = bf16[66,16,128]{2,1,0:T(8,128)(2,1)S(1)} custom-call(bf16[64,16,128]{2,1,0:T(8,128)(2,1)S(1)} %collective-permute-done.1.q, bf16[2,2112,128]{2,1,0:T(8,128)(2,1)S(1)} %get-tuple-element.14.keys, bf16[2,2112,256]{2,1,0:T(8,128)(2,1)S(1)} %get-tuple-element.15.values), custom_call_target="tpu_custom_call" | custom-call | flops 2214592512 | bytes 4194304 | tf_op jit(solution)/shard_map/sibling/pallas_call | solution.py:250
  18.8 0.4 %collective-permute-start.2 = (bf16[66,16,128]{2,1,0:T(8,128)(2,1)S(1)}, bf16[66,16,128]{2,1,0:T(8,128)(2,1)S(1)}, u32[]{:S(2)}, u32[]{:S(2)}) collective-permute-start(bf16[66,16,128]{2,1,0:T(8,128)(2,1)S(1)} %sibling.1), channel_id=1, source_target_pairs={{0,4},{4,0},{8,12},{12,8},{1,5},{5,1},{9,13},{13,9},{2,6},{6,2},{1... | collective-permute-start | bytes 811016 | tf_op jit(solution)/shard_map/ppermute | solution.py:236
  19.2 1.7 %straight.3.a = bf16[33,16,128]{2,1,0:T(8,128)(2,1)S(1)} custom-call(bf16[64,16,128]{2,1,0:T(8,128)(2,1)S(1)} %collective-permute-done.q, bf16[2,2112,128]{2,1,0:T(8,128)(2,1)S(1)} %get-tuple-element.14.keys, bf16[2,2112,256]{2,1,0:T(8,128)(2,1)S(1)} %get-tuple-element.15.values), custom_call_target="tpu_custom_call" | custom-call | flops 1107296256 | bytes 4194304 | tf_op jit(solution)/shard_map/straight/pallas_call | solution.py:250
  20.9 1.7 %straight.2.a = bf16[33,16,128]{2,1,0:T(8,128)(2,1)S(1)} custom-call(bf16[64,16,128]{2,1,0:T(8,128)(2,1)S(1)} %collective-permute-done.q, bf16[2,2112,128]{2,1,0:T(8,128)(2,1)S(1)} %get-tuple-element.14.keys, bf16[2,2112,256]{2,1,0:T(8,128)(2,1)S(1)} %get-tuple-element.15.values), custom_call_target="tpu_custom_call" | custom-call | flops 1107296256 | bytes 4194304 | tf_op jit(solution)/shard_map/straight/pallas_call | solution.py:250
  22.6 0.0 collective-permute-done.4.b
  22.6 0.2 chip_sum.3
  22.8 0.2 collective-permute-start.6
  23.0 0.2 chip_sum.2
  23.2 2.0 %collective-permute-start.5 = (bf16[33,16,128]{2,1,0:T(8,128)(2,1)S(1)}, bf16[33,16,128]{2,1,0:T(8,128)(2,1)S(1)}, u32[]{:S(2)}, u32[]{:S(2)}) collective-permute-start(bf16[33,16,128]{2,1,0:T(8,128)(2,1)S(1)} %chip_sum.2), channel_id=1, source_target_pairs={{0,8},{4,12},{8,0},{12,4},{1,9},{5,13},{9,1},{13,5},{2,10},{6,14},... | collective-permute-start | bytes 405512 | tf_op jit(solution)/shard_map/ppermute | solution.py:239
  25.2 0.0 collective-permute-done.2.sib
  25.2 0.4 %near.1 = (f32[64,16,128]{2,1,0:T(8,128)S(1)}, f32[8,128]{1,0:T(8,128)S(1)}) custom-call(bf16[66,16,128]{2,1,0:T(8,128)(2,1)S(1)} %get-tuple-element.13.own, bf16[66,16,128]{2,1,0:T(8,128)(2,1)S(1)} %collective-permute-done.2.sib), custom_call_target="tpu_custom_call" | custom-call | flops 1048576 | bytes 1048576 | tf_op jit(solution)/shard_map/near/pallas_call | solution.py:250
  25.6 3.7 %collective-permute-done.6.refs_1_ = bf16[33,16,128]{2,1,0:T(8,128)(2,1)S(1)} collective-permute-done((bf16[33,16,128]{2,1,0:T(8,128)(2,1)S(1)}, bf16[33,16,128]{2,1,0:T(8,128)(2,1)S(1)}, u32[]{:S(2)}, u32[]{:S(2)}) %collective-permute-start.6) | collective-permute-done | bytes 135200 | tf_op jit(solution)/shard_map/ppermute | solution.py:239
  29.3 2.1 %collective-permute-done.5.refs_0_ = bf16[33,16,128]{2,1,0:T(8,128)(2,1)S(1)} collective-permute-done((bf16[33,16,128]{2,1,0:T(8,128)(2,1)S(1)}, bf16[33,16,128]{2,1,0:T(8,128)(2,1)S(1)}, u32[]{:S(2)}, u32[]{:S(2)}) %collective-permute-start.5) | collective-permute-done | bytes 135200 | tf_op jit(solution)/shard_map/ppermute | solution.py:239
  31.4 1.1 %final.1 = bf16[64,16,128]{2,1,0:T(8,128)(2,1)} custom-call(f32[64,16,128]{2,1,0:T(8,128)S(1)} %get-tuple-element.16.near, f32[8,128]{1,0:T(8,128)S(1)} %get-tuple-element.17.near_l, bf16[33,16,128]{2,1,0:T(8,128)(2,1)S(1)} %collective-permute-done.5.refs_0_, bf16[33,16,128]{2,1,0:T(8,128)(2,1)S(1)} %collective-permute-done.6.refs_1_), custom_call_target="tpu_custom_call" | custom-call | flops 1048576 | bytes 1048576 | tf_op jit(solution)/shard_map/final/pallas_call | solution.py:250
Async XLA Ops:
  0.0 11.0 %collective-permute-start = (bf16[64,16,128]{2,1,0:T(8,128)(2,1)}, bf16[64,16,128]{2,1,0:T(8,128)(2,1)S(1)}, u32[]{:S(2)}, u32[]{:S(2)}) collective-permute-start(bf16[64,16,128]{2,1,0:T(8,128)(2,1)} %q.1), channel_id=1, source_target_pairs={{0,8},{4,12},{8,0},{12,4},{1,9},{5,13},{9,1},{13,5},{2,10},{6,14},... | collective-permute-start | bytes 786440 | tf_op jit(solution)/shard_map/ppermute | solution.py:239
  3.6 7.5 %copy-start = (bf16[64,16,128]{2,1,0:T(8,128)(2,1)S(1)}, bf16[64,16,128]{2,1,0:T(8,128)(2,1)}, u32[]{:S(2)}) copy-start(bf16[64,16,128]{2,1,0:T(8,128)(2,1)} %q.1) | copy-start | bytes 786436
  11.0 1.6 %collective-permute-start.3 = (bf16[64,16,128]{2,1,0:T(8,128)(2,1)S(1)}, bf16[64,16,128]{2,1,0:T(8,128)(2,1)S(1)}, u32[]{:S(2)}, u32[]{:S(2)}) collective-permute-start(bf16[64,16,128]{2,1,0:T(8,128)(2,1)S(1)} %collective-permute-done.q), channel_id=1, source_target_pairs={{0,4},{4,0},{8,12},{12,8},{1,5},{5,1},{9,13},{13,9},{2,6},{6,2},{1... | collective-permute-start | bytes 786440 | tf_op jit(solution)/shard_map/ppermute | solution.py:236
  11.1 4.7 %collective-permute-start.1 = (bf16[64,16,128]{2,1,0:T(8,128)(2,1)S(1)}, bf16[64,16,128]{2,1,0:T(8,128)(2,1)S(1)}, u32[]{:S(2)}, u32[]{:S(2)}) collective-permute-start(bf16[64,16,128]{2,1,0:T(8,128)(2,1)S(1)} %copy-done), channel_id=1, source_target_pairs={{0,4},{4,0},{8,12},{12,8},{1,5},{5,1},{9,13},{13,9},{2,6},{6,2},{1... | collective-permute-start | bytes 786440 | tf_op jit(solution)/shard_map/ppermute | solution.py:236
  15.6 7.0 %collective-permute-start.4 = (bf16[66,16,128]{2,1,0:T(8,128)(2,1)S(1)}, bf16[66,16,128]{2,1,0:T(8,128)(2,1)S(1)}, u32[]{:S(2)}, u32[]{:S(2)}) collective-permute-start(bf16[66,16,128]{2,1,0:T(8,128)(2,1)S(1)} %diagonal.1), channel_id=1, source_target_pairs={{0,4},{4,0},{8,12},{12,8},{1,5},{5,1},{9,13},{13,9},{2,6},{6,2},{1... | collective-permute-start | bytes 811016 | tf_op jit(solution)/shard_map/ppermute | solution.py:236
  18.8 6.4 %collective-permute-start.2 = (bf16[66,16,128]{2,1,0:T(8,128)(2,1)S(1)}, bf16[66,16,128]{2,1,0:T(8,128)(2,1)S(1)}, u32[]{:S(2)}, u32[]{:S(2)}) collective-permute-start(bf16[66,16,128]{2,1,0:T(8,128)(2,1)S(1)} %sibling.1), channel_id=1, source_target_pairs={{0,4},{4,0},{8,12},{12,8},{1,5},{5,1},{9,13},{13,9},{2,6},{6,2},{1... | collective-permute-start | bytes 811016 | tf_op jit(solution)/shard_map/ppermute | solution.py:236
  22.8 6.5 %collective-permute-start.6 = (bf16[33,16,128]{2,1,0:T(8,128)(2,1)S(1)}, bf16[33,16,128]{2,1,0:T(8,128)(2,1)S(1)}, u32[]{:S(2)}, u32[]{:S(2)}) collective-permute-start(bf16[33,16,128]{2,1,0:T(8,128)(2,1)S(1)} %chip_sum.3), channel_id=1, source_target_pairs={{0,8},{4,12},{8,0},{12,4},{1,9},{5,13},{9,1},{13,5},{2,10},{6,14},... | collective-permute-start | bytes 405512 | tf_op jit(solution)/shard_map/ppermute | solution.py:239
  23.2 8.2 %collective-permute-start.5 = (bf16[33,16,128]{2,1,0:T(8,128)(2,1)S(1)}, bf16[33,16,128]{2,1,0:T(8,128)(2,1)S(1)}, u32[]{:S(2)}, u32[]{:S(2)}) collective-permute-start(bf16[33,16,128]{2,1,0:T(8,128)(2,1)S(1)} %chip_sum.2), channel_id=1, source_target_pairs={{0,8},{4,12},{8,0},{12,4},{1,9},{5,13},{9,1},{13,5},{2,10},{6,14},... | collective-permute-start | bytes 405512 | tf_op jit(solution)/shard_map/ppermute | solution.py:239

commit v3 on v2

v3 whole, which is shorter than its diff:
```python
import functools
import math

import jax
import jax.numpy as jnp
from jax import lax
from jax.experimental import pallas as pl
from jax.experimental.pallas import tpu as pltpu
from jax.sharding import PartitionSpec as P

NEG_FILL = -1e30
LOG2E = 1.4426950408889634
VMEM = pl.BlockSpec(memory_space=pltpu.VMEM)
SMEM = pl.BlockSpec(memory_space=pltpu.SMEM)
HBM = pl.BlockSpec(memory_space=pltpu.HBM)
F32 = jnp.float32
BF16 = jnp.bfloat16
NT = (((1,), (1,)), ((), ()))
CORES = 2


def params():
    return pltpu.CompilerParams(vmem_limit_bytes=36 * 2**20)


def pack_rows(wide):
    eye = lax.broadcasted_iota(jnp.int32, (128, 128), 0) == lax.broadcasted_iota(jnp.int32, (128, 128), 1)
    return jnp.concatenate(
        [
            jnp.sum(jnp.where(eye, wide[i * 128 : (i + 1) * 128], 0.0), axis=0, keepdims=True)
            for i in range(wide.shape[0] // 128)
        ],
        axis=0,
    )


def spread_rows(packed):
    return jnp.concatenate(
        [jnp.transpose(jnp.broadcast_to(packed[i : i + 1, :], (128, 128))) for i in range(packed.shape[0])], axis=0
    )


def load_kernel(length, *refs):
    n = (len(refs) - 2) // 2
    ins, outs, filled, sems = refs[:n], refs[n : 2 * n], refs[-2], refs[-1]
    copies = [pltpu.make_async_copy(ins[i], outs[i], sems.at[i]) for i in range(n)]
    for c in copies:
        c.start()
    slots = ins[0].shape[0]
    filled[...] = jnp.full(filled.shape, jnp.clip(length[0] - lax.axis_index("ctx") * slots, 0, slots), jnp.int32)
    for c in copies:
        c.wait()


def prepare_kernel(filled, k, v, nk, keys, values):
    slots, kv, hd = k.shape
    count = filled[0:1, :]
    included = lax.broadcasted_iota(jnp.int32, (slots, hd), 0) < count
    k_rows, v_rows, nk_rows = [jnp.swapaxes(x[...], 0, 1) for x in (k, v, nk)]
    for h in range(kv):
        fill = jnp.where(count > 0, k_rows[h, 0:1].astype(F32), nk_rows[h, 0:1].astype(F32))
        keys[h] = jnp.where(included, k_rows[h].astype(F32), fill).astype(BF16)
        values[h, :, 0:hd] = jnp.where(included, v_rows[h].astype(F32), 0.0).astype(BF16)
        values[h, :, hd:] = jnp.where(included, 1.0, 0.0).astype(BF16)


def put_lse(ref, first, lse):
    heads = ref.shape[1]
    high = lse.astype(BF16).astype(F32)
    middle = (lse - high).astype(BF16).astype(F32)
    low = lse - high - middle
    extra = lse_rows(lse.shape[0], heads)
    rest = jnp.zeros((extra * heads - 3 * lse.shape[0], 128), F32)
    rows = jnp.concatenate([high, middle, low, rest], axis=0)
    ref[first : first + extra] = rows.astype(BF16).reshape(extra, heads, 128)


def lse_rows(n, heads):
    return -(-3 * n // heads)


def get_lse(ref, first):
    heads = ref.shape[1]
    n = first * heads // 128
    extra = lse_rows(n, heads)
    rows = ref[first : first + extra].astype(F32).reshape(extra * heads, 128)
    return rows[0:n] + rows[n : 2 * n] + rows[2 * n : 3 * n]


def packed_shape(tokens, heads, hd):
    return jax.ShapeDtypeStruct((tokens + lse_rows(tokens * heads // 128, heads), heads, hd), BF16)


def extended(shape, rows):
    return jax.ShapeDtypeStruct((shape.shape[0] + rows,) + shape.shape[1:], shape.dtype)


def attend(q_ref, keys, values, first, n, o_ref, fresh=None, causal=None):
    heads, hd = q_ref.shape[1:]
    kv = keys.shape[0]
    group = heads // kv
    rows = n * group
    scale = LOG2E / math.sqrt(hd)
    if causal is not None:
        count = fresh[0].shape[1]
        token = causal + lax.broadcasted_iota(jnp.int32, (rows, count), 0) // group
        seen = token >= lax.broadcasted_iota(jnp.int32, (rows, count), 1)

    def scores(h):
        q = q_ref[first : first + n, h * group : (h + 1) * group, :].reshape(rows, hd)
        found = [lax.dot_general(q, keys[h], NT, preferred_element_type=F32)]
        if fresh is not None:
            s = lax.dot_general(q, fresh[0][h], NT, preferred_element_type=F32)
            found.append(s if causal is None else jnp.where(seen, s, NEG_FILL))
        return found

    now = scores(0)
    lses = []
    for h in range(kv):
        later = scores(h + 1) if h + 1 < kv else None
        peak = functools.reduce(jnp.maximum, [jnp.max(s, axis=-1, keepdims=True) for s in now])
        weights = [jnp.exp2((s - peak) * scale) for s in now]
        if causal is not None:
            weights[1] = jnp.where(seen, weights[1], 0.0)
        out = jnp.dot(weights[0].astype(BF16), values[h], preferred_element_type=F32)
        if fresh is not None:
            out = out + jnp.dot(weights[1].astype(BF16), fresh[1][h], preferred_element_type=F32)
        total = out[:, hd:]
        floored = jnp.maximum(total, 1.0)
        o_ref[0:n, h * group : (h + 1) * group, :] = (out[:, 0:hd] / floored).astype(BF16).reshape(n, group, hd)
        lses.append(pack_rows(jnp.where(total > 0.0, peak * (1.0 / math.sqrt(hd)) + jnp.log(floored), NEG_FILL)))
        now = later
    put_lse(o_ref, n, jnp.concatenate(lses, axis=0))


def fresh_kernel(nk, nv, nk_core, nv_core, keys, values):
    low = lax.axis_index("ctx") % CORES == 0
    tokens, kv, hd = nk.shape
    for mine, other, out in ((nk, nk_core, keys), (nv, nv_core, values)):
        mine, other = [jnp.swapaxes(x[...], 0, 1).astype(F32) for x in (mine, other)]
        out[:, 0:tokens, 0:hd] = jnp.where(low, mine, other).astype(BF16)
        out[:, tokens:, 0:hd] = jnp.where(low, other, mine).astype(BF16)
    values[:, :, hd:] = jnp.ones((kv, CORES * tokens, hd), BF16)


def blend(parts, group):
    tokens, heads, hd = parts[0][0].shape
    top = functools.reduce(jnp.maximum, [lse for _, lse in parts])
    scales = [jnp.exp(lse - top) for _, lse in parts]
    total = functools.reduce(jnp.add, scales)
    lse = jnp.where(top > 0.5 * NEG_FILL, top + jnp.log(total), NEG_FILL)
    inv = 1.0 / total
    n = tokens * group // 128
    outs = []
    for h in range(heads // group):
        norms = [
            norm[:, h * group : (h + 1) * group, :].reshape(tokens * group, hd).astype(F32) for norm, _ in parts
        ]
        acc = norms[0]
        for norm, s in zip(norms[1:], scales[1:]):
            acc = acc + (norm - norms[0]) * spread_rows((s * inv)[h * n : (h + 1) * n, :])
        outs.append(acc)
    return outs, lse


def shard_kernel(first, n, q, keys, values, *refs):
    o = refs[-1]
    attend(q, keys, values, first, n, o)
    if len(refs) > 1:
        o[o.shape[0] - refs[0].shape[0] :] = refs[0][...]


def straight_kernel(owner, first, n, q, keys, values, fresh_k, fresh_v, o):
    place = lax.axis_index("ctx")
    sees = owner(place) > place

    @pl.when(sees)
    def _():
        attend(q, keys, values, first, n, o, (fresh_k, fresh_v))

    @pl.when(jnp.logical_not(sees))
    def _():
        attend(q, keys, values, first, n, o)


def own_kernel(q, keys, values, fresh_k, fresh_v, o):
    tokens = q.shape[0]
    core = lax.axis_index("ctx") % CORES
    attend(q, keys, values, 0, tokens, o, (fresh_k, fresh_v), core * tokens)


def chip_sum_kernel(group, n, a, b, o):
    heads, hd = o.shape[1:]
    outs, lse = blend([(x[0:n], get_lse(x, n)) for x in (a, b)], group)
    for h, x in enumerate(outs):
        o[0:n, h * group : (h + 1) * group, :] = x.astype(BF16).reshape(n, group, hd)
    put_lse(o, n, lse)
    used = packed_shape(n, heads, hd).shape[0]
    if o.shape[0] > used:
        o[used:] = jnp.zeros((o.shape[0] - used, heads, hd), BF16)


def cut_lse(lse, kv, first, n, tokens):
    per = lse.shape[0] // kv
    a, b = first * per // tokens, (first + n) * per // tokens
    return jnp.concatenate([lse[h * per + a : h * per + b] for h in range(kv)], axis=0)


def near_kernel(group, own, sib, o, l):
    tokens, heads, hd = o.shape
    sib = sib.at[pl.ds(sib.shape[0] - own.shape[0], own.shape[0])]
    outs, lse = blend([(x[0:tokens], get_lse(x, tokens)) for x in (own, sib)], group)
    for h, x in enumerate(outs):
        o[:, h * group : (h + 1) * group, :] = x.reshape(tokens, group, hd)
    l[...] = lse


def final_kernel(group, shares, near, near_l, *refs):
    *far, o = refs
    tokens, heads, hd = o.shape
    for i, (first, n) in enumerate(shares):
        lse = cut_lse(near_l[...], heads // group, first, n, tokens)
        parts = [(near[first : first + n], lse)] + [(x[0:n], get_lse(x, n)) for x in far[i :: len(shares)]]
        outs, _ = blend(parts, group)
        for h, x in enumerate(outs):
            o[first : first + n, h * group : (h + 1) * group, :] = x.astype(BF16).reshape(n, group, hd)


def per_device(queries, new_keys, new_values, cache_keys, cache_values, cache_len):
    tokens, heads, hd = queries.shape
    slots, kv, _ = cache_keys.shape
    group = heads // kv
    n = lax.axis_size("ctx")
    chips = n // CORES
    unit = max(1, 128 // group)
    late = max(unit, tokens // 2 // unit * unit)
    shares = [(0, tokens - late), (tokens - late, late)]

    def over_core(x):
        return lax.ppermute(x, "ctx", [(i, i ^ 1) for i in range(n)])

    def over_chip(x, step):
        return lax.ppermute(x, "ctx", [(i, (i // CORES + step) % chips * CORES + i % CORES) for i in range(n)])

    def packed(m):
        return packed_shape(m, heads, hd)

    def cost(m):
        return pl.CostEstimate(
            flops=8 * m * heads * slots * hd, bytes_accessed=4 * 2**20, transcendentals=m * heads * slots
        )

    def call(name, kernel, out, args, estimate):
        return pl.pallas_call(
            kernel,
            out_shape=out,
            in_specs=[VMEM] * len(args),
            out_specs=jax.tree.map(lambda _: VMEM, out),
            compiler_params=params(),
            cost_estimate=estimate,
            name=name,
        )(*args)

    tiny = pl.CostEstimate(flops=0, bytes_accessed=0, transcendentals=0)
    small = pl.CostEstimate(flops=2**20, bytes_accessed=2**20, transcendentals=2**14)
    q_chip = [over_chip(queries, step) for step in range(1, chips)]
    moved = (cache_keys, cache_values, new_keys, new_values, queries)
    k, v, nk, nv, q_own, filled = pl.pallas_call(
        load_kernel,
        out_shape=[jax.ShapeDtypeStruct(x.shape, x.dtype) for x in moved]
        + [jax.ShapeDtypeStruct((8, hd), jnp.int32)],
        in_specs=[SMEM] + [HBM] * len(moved),
        out_specs=[VMEM] * (len(moved) + 1),
        scratch_shapes=[pltpu.SemaphoreType.DMA((len(moved),))],
        compiler_params=params(),
        cost_estimate=small,
        name="load",
    )(cache_len, *[pltpu.with_memory_space_constraint(x, pltpu.HBM) for x in moved])
    q_core, nk_core, nv_core = over_core(queries), over_core(new_keys), over_core(new_values)
    q_core, nk_core, nv_core = lax.optimization_barrier((q_core, nk_core, nv_core))
    keys, values = call(
        "prepare",
        prepare_kernel,
        [jax.ShapeDtypeStruct((kv, slots, hd), BF16), jax.ShapeDtypeStruct((kv, slots, 2 * hd), BF16)],
        (filled, k, v, nk),
        small,
    )
    shard = (keys, values)
    fresh = call(
        "fresh",
        fresh_kernel,
        [jax.ShapeDtypeStruct((kv, CORES * tokens, hd), BF16), jax.ShapeDtypeStruct((kv, CORES * tokens, 2 * hd), BF16)],
        (nk, nv, nk_core, nv_core),
        small,
    )
    q_core, *fresh = lax.optimization_barrier((q_core, *fresh))

    def attend_part(name, kernel, m, *args):
        return call(name, kernel, packed(m), args, cost(m))

    sib = attend_part("sibling", functools.partial(shard_kernel, 0, tokens), tokens, q_core, *shard)
    *q_chip, sib = lax.optimization_barrier((*q_chip, sib))
    q_diag = [over_core(q) for q in q_chip]
    far = []
    for step in range(1, chips):
        def owner(i, step=step):
            return (i // CORES - step + chips) % chips * CORES + i % CORES

        def straight_part(q, first, m):
            kernel = functools.partial(straight_kernel, owner, first, m)
            return call("straight", kernel, packed(m), (q, *shard, *fresh), tiny if first else cost(m))

        q_s, q_d = q_chip[step - 1], q_diag[step - 1]
        early = straight_part(q_s, *shares[0])
        q_d, early = lax.optimization_barrier((q_d, early))
        diag = []
        for first, m in shares:
            more = [sib] if first == 0 and step == 1 else []
            kernel = functools.partial(shard_kernel, first, m)
            shape = extended(packed(m), sum(x.shape[0] for x in more))
            diag.append(call("diagonal", kernel, shape, (q_d, *shard, *more), cost(m)))
            q_d, diag[-1] = lax.optimization_barrier((q_d, diag[-1]))
        q_s, diag[-1] = lax.optimization_barrier((q_s, diag[-1]))
        diag = [over_core(x) for x in diag]
        if step == 1:
            from_sib = diag[0]
        for i, (first, m) in enumerate(shares):
            straight = straight_part(q_s, first, m) if i else early
            shape = extended(packed(m), len(shares) - 1 - i)
            both = call("chip_sum", functools.partial(chip_sum_kernel, group, m), shape, (diag[i], straight), tiny)
            q_s, q_own, both = lax.optimization_barrier((q_s, q_own, both))
            far.append(over_chip(both, chips - step))
    own = call("own", own_kernel, packed(tokens), (q_own, *shard, *fresh), tiny)
    near = call(
        "near",
        functools.partial(near_kernel, group),
        [jax.ShapeDtypeStruct(queries.shape, F32), jax.ShapeDtypeStruct((tokens * heads // 128, 128), F32)],
        (own, from_sib),
        tiny,
    )
    return call(
        "final",
        functools.partial(final_kernel, group, shares),
        jax.ShapeDtypeStruct(queries.shape, BF16),
        (*near, *far),
        small,
    )


def solution(mesh):
    spec = P(("conv", "ctx"), "head", None)
    return jax.shard_map(
        per_device,
        mesh=mesh,
        in_specs=(spec,) * 5 + (P("conv"),),
        out_specs=spec,
        check_vma=False,
    )
```

time: 32.6 us -> 26.4 us (0.81)
  waiting for transfers between devices: 6.86 us -> 3.05 us
  Pallas kernels: 18.6 us -> 16.5 us
  starting transfers between devices: 6.3 us -> 5.9 us
    pallas_call x1, Pallas kernels: 7.38 us -> 1.66 us  [per_device(): pl.pallas_call(load_kernel, out_shape=[jax.ShapeDtypeStruct(x.shape, x.dt...]
    pallas_call x8 -> x12, Pallas kernels: 11.2 us -> 14.9 us  [call(): pl.pallas_call(kernel, out_shape=out, in_specs=[VMEM] * len(args), out_sp...]
    ppermute x3, waiting for transfers between devices: 5.83 us -> 3.03 us  [over_chip(): lax.ppermute(x, 'ctx', [(i, (i // CORES + step) % chips * CORES + i % COR...]
    ppermute x4 -> x6, waiting for transfers between devices: 1.03 us -> 0.02 us  [over_core(): return lax.ppermute(x, 'ctx', [(i, i ^ 1) for i in range(n)])]
    ppermute x3, starting transfers between devices: 5.09 us -> 4.29 us  [over_chip(): lax.ppermute(x, 'ctx', [(i, (i // CORES + step) % chips * CORES + i % COR...]
    ppermute x4 -> x6, starting transfers between devices: 1.2 us -> 1.61 us  [over_core(): return lax.ppermute(x, 'ctx', [(i, i ^ 1) for i in range(n)])]
  transfers between devices with their start and end apart: 7 -> 9, of which waited for: 3 -> 2; matrix products, arithmetic and copies ran while one was open for 0% -> 0% of each run, Pallas kernels for 54% -> 54%
where the time goes in v3:
time: 26.4 us; the launch traced here: 26.2 us
  Pallas kernels  16.5 us (62%)
  starting transfers between devices  5.9 us (22%)
  waiting for transfers between devices  3.05 us (12%)
  between operations  0.76 us (3%)
    pallas_call x12, Pallas kernels, call(): pl.pallas_call(kernel, out_shape=out, in_specs=[VMEM] * len(args), out_sp...  14.9 us
    ppermute x3, starting transfers between devices, over_chip(): lax.ppermute(x, 'ctx', [(i, (i // CORES + step) % chips * CORES + i % COR...  4.29 us
    ppermute x3, waiting for transfers between devices, over_chip(): lax.ppermute(x, 'ctx', [(i, (i // CORES + step) % chips * CORES + i % COR...  3.03 us
    pallas_call x1, Pallas kernels, per_device(): pl.pallas_call(load_kernel, out_shape=[jax.ShapeDtypeStruct(x.shape, x.dt...  1.66 us
    ppermute x6, starting transfers between devices, over_core(): return lax.ppermute(x, 'ctx', [(i, i ^ 1) for i in range(n)])  1.61 us
  transfers between devices with their start and end apart: 9, of which 2 were waited for; matrix products, arithmetic and copies ran while one was open for 0% of the time, Pallas kernels for 54%

profile of v3, /device:TPU:0, one launch (start us, length us, event | category | flops | bytes accessed | tf_op | source)
XLA Modules:
  0.0 26.2 jit_solution(3549605056488587013)
XLA Ops:
  0.0 0.5 %collective-permute-start.1 = (bf16[64,16,128]{2,1,0:T(8,128)(2,1)}, bf16[64,16,128]{2,1,0:T(8,128)(2,1)S(1)}, u32[]{:S(2)}, u32[]{:S(2)}) collective-permute-start(bf16[64,16,128]{2,1,0:T(8,128)(2,1)} %refs_4_.1), channel_id=1, source_target_pairs={{0,4},{4,0},{8,12},{12,8},{1,5},{5,1},{9,13},{13,9},{2,6},{6,2},{1... | collective-permute-start | bytes 786440 | tf_op jit(solution)/shard_map/ppermute | solution.py:240
  0.5 2.5 %collective-permute-start = (bf16[64,16,128]{2,1,0:T(8,128)(2,1)}, bf16[64,16,128]{2,1,0:T(8,128)(2,1)S(1)}, u32[]{:S(2)}, u32[]{:S(2)}) collective-permute-start(bf16[64,16,128]{2,1,0:T(8,128)(2,1)} %refs_4_.1), channel_id=1, source_target_pairs={{0,8},{4,12},{8,0},{12,4},{1,9},{5,13},{9,1},{13,5},{2,10},{6,14},... | collective-permute-start | bytes 786440 | tf_op jit(solution)/shard_map/ppermute | solution.py:243
  2.9 0.2 collective-permute-start.2
  3.2 0.3 %collective-permute-start.3 = (bf16[64,2,128]{2,1,0:T(2,128)(2,1)}, bf16[64,2,128]{2,1,0:T(2,128)(2,1)S(1)}, u32[]{:S(2)}, u32[]{:S(2)}) collective-permute-start(bf16[64,2,128]{2,1,0:T(2,128)(2,1)} %refs_3_.1), channel_id=1, source_target_pairs={{0,4},{4,0},{8,12},{12,8},{1,5},{5,1},{9,13},{13,9},{2,6},{6,2},{1... | collective-permute-start | bytes 98312 | tf_op jit(solution)/shard_map/ppermute | solution.py:240
  4.1 1.7 %load.1 = (bf16[2048,2,128]{2,1,0:T(2,128)(2,1)S(1)}, bf16[2048,2,128]{2,1,0:T(2,128)(2,1)S(1)}, bf16[64,2,128]{2,1,0:T(2,128)(2,1)S(1)}, bf16[64,2,128]{2,1,0:T...) custom-call(s32[1]{0:T(128)S(6)} %copy.7.length, bf16[2048,2,128]{2,1,0:T(2,128)(2,1)} %refs_0_.1, ...), custom_call_target="tpu_custom_call" | custom-call | flops 1048576 | bytes 1048576 | tf_op jit(solution)/shard_map/load/pallas_call | solution.py:268
  5.8 0.9 %prepare.1 = (bf16[2,2048,128]{2,1,0:T(8,128)(2,1)S(1)}, bf16[2,2048,256]{2,1,0:T(8,128)(2,1)S(1)}) custom-call(s32[8,128]{1,0:T(8,128)S(1)} %get-tuple-element.45.filled, bf16[2048,2,128]{2,1,0:T(2,128)(2,1)S(1)} %get-tuple-element.46.k, bf16[2048,2,128]{2,1,0:T(2,128)(2,1)S(1)} %get-tuple-element.47.v, bf16[64,2,128]{2,1,0:T(2,128)(2,1)S(1)} %get-tuple-element.38.nk), custom_call_target="tpu_custom_call" | custom-call | flops 1048576 | bytes 1048576 | tf_op jit(solution)/shard_map/prepare/pallas_call | solution.py:254
  6.7 0.0 collective-permute-done.2.nk_core
  6.7 0.0 collective-permute-done.3.nv_core
  6.7 0.0 collective-permute-done.1.q
  6.7 2.6 %sibling.1.refs_0_ = bf16[66,16,128]{2,1,0:T(8,128)(2,1)S(1)} custom-call(bf16[64,16,128]{2,1,0:T(8,128)(2,1)S(1)} %collective-permute-done.1.q, bf16[2,2048,128]{2,1,0:T(8,128)(2,1)S(1)} %get-tuple-element.48.keys, bf16[2,2048,256]{2,1,0:T(8,128)(2,1)S(1)} %get-tuple-element.49.values), custom_call_target="tpu_custom_call" | custom-call | flops 2147483648 | bytes 4194304 | tf_op jit(solution)/shard_map/sibling/pallas_call | solution.py:254
  9.4 0.7 %collective-permute-done.q = bf16[64,16,128]{2,1,0:T(8,128)(2,1)S(1)} collective-permute-done((bf16[64,16,128]{2,1,0:T(8,128)(2,1)}, bf16[64,16,128]{2,1,0:T(8,128)(2,1)S(1)}, u32[]{:S(2)}, u32[]{:S(2)}) %collective-permute-start) | collective-permute-done | bytes 262176 | tf_op jit(solution)/shard_map/ppermute | solution.py:243
  10.1 0.0 collective-permute-start.4
  10.1 1.7 %straight.2.b = bf16[33,16,128]{2,1,0:T(8,128)(2,1)S(1)} custom-call(bf16[64,16,128]{2,1,0:T(8,128)(2,1)S(1)} %collective-permute-done.q, bf16[2,2048,128]{2,1,0:T(8,128)(2,1)S(1)} %get-tuple-element.48.keys, bf16[2,2048,256]{2,1,0:T(8,128)(2,1)S(1)} %get-tuple-element.49.values, bf16[2,128,128]{2,1,0:T(8,128)(2,1)S(1)} %get-tuple-element.51.fresh_k, ...), custom_call_target="tpu_custom_call" | custom-call | flops 1073741824 | bytes 4194304 | tf_op jit(solution)/shard_map/straight/pallas_call | solution.py:254
  11.9 0.0 collective-permute-done.4.q
  11.9 1.6 %diagonal.2 = bf16[99,16,128]{2,1,0:T(8,128)(2,1)S(1)} custom-call(bf16[64,16,128]{2,1,0:T(8,128)(2,1)S(1)} %collective-permute-done.4.q, bf16[2,2048,128]{2,1,0:T(8,128)(2,1)S(1)} %get-tuple-element.48.keys, bf16[2,2048,256]{2,1,0:T(8,128)(2,1)S(1)} %get-tuple-element.49.values, bf16[66,16,128]{2,1,0:T(8,128)(2,1)S(1)} %sibling.1.refs_0_), custom_call_target="tpu_custom_call" | custom-call | flops 1073741824 | bytes 4194304 | tf_op jit(solution)/shard_map/diagonal/pallas_call | solution.py:254
  13.4 0.6 %collective-permute-start.5 = (bf16[99,16,128]{2,1,0:T(8,128)(2,1)S(1)}, bf16[99,16,128]{2,1,0:T(8,128)(2,1)S(1)}, u32[]{:S(2)}, u32[]{:S(2)}) collective-permute-start(bf16[99,16,128]{2,1,0:T(8,128)(2,1)S(1)} %diagonal.2), channel_id=1, source_target_pairs={{0,4},{4,0},{8,12},{12,8},{1,5},{5,1},{9,13},{13,9},{2,6},{6,2},{1... | collective-permute-start | bytes 1216520 | tf_op jit(solution)/shard_map/ppermute | solution.py:240
  14.0 1.5 %diagonal.3 = bf16[33,16,128]{2,1,0:T(8,128)(2,1)S(1)} custom-call(bf16[64,16,128]{2,1,0:T(8,128)(2,1)S(1)} %collective-permute-done.4.q, bf16[2,2048,128]{2,1,0:T(8,128)(2,1)S(1)} %get-tuple-element.48.keys, bf16[2,2048,256]{2,1,0:T(8,128)(2,1)S(1)} %get-tuple-element.49.values), custom_call_target="tpu_custom_call" | custom-call | flops 1073741824 | bytes 4194304 | tf_op jit(solution)/shard_map/diagonal/pallas_call | solution.py:254
  15.6 0.1 collective-permute-start.6
  15.6 0.0 collective-permute-done.5.a.sib
  15.6 0.2 chip_sum.2
  15.8 1.6 %collective-permute-start.7 = (bf16[34,16,128]{2,1,0:T(8,128)(2,1)S(1)}, bf16[34,16,128]{2,1,0:T(8,128)(2,1)S(1)}, u32[]{:S(2)}, u32[]{:S(2)}) collective-permute-start(bf16[34,16,128]{2,1,0:T(8,128)(2,1)S(1)} %chip_sum.2), channel_id=1, source_target_pairs={{0,8},{4,12},{8,0},{12,4},{1,9},{5,13},{9,1},{13,5},{2,10},{6,14},... | collective-permute-start | bytes 417800 | tf_op jit(solution)/shard_map/ppermute | solution.py:243
  17.5 1.9 %straight.3.b = bf16[33,16,128]{2,1,0:T(8,128)(2,1)S(1)} custom-call(bf16[64,16,128]{2,1,0:T(8,128)(2,1)S(1)} %collective-permute-done.q, bf16[2,2048,128]{2,1,0:T(8,128)(2,1)S(1)} %get-tuple-element.48.keys, bf16[2,2048,256]{2,1,0:T(8,128)(2,1)S(1)} %get-tuple-element.49.values, bf16[2,128,128]{2,1,0:T(8,128)(2,1)S(1)} %get-tuple-element.51.fresh_k, ...), custom_call_target="tpu_custom_call" | custom-call | tf_op jit(solution)/shard_map/straight/pallas_call | solution.py:254
  19.4 0.0 collective-permute-done.6.a
  19.4 0.2 chip_sum.3
  19.5 0.2 collective-permute-start.8
  19.7 3.1 %own.1 = bf16[66,16,128]{2,1,0:T(8,128)(2,1)S(1)} custom-call(bf16[64,16,128]{2,1,0:T(8,128)(2,1)S(1)} %get-tuple-element.64.q, bf16[2,2048,128]{2,1,0:T(8,128)(2,1)S(1)} %get-tuple-element.48.keys, bf16[2,2048,256]{2,1,0:T(8,128)(2,1)S(1)} %get-tuple-element.49.values, bf16[2,128,128]{2,1,0:T(8,128)(2,1)S(1)} %get-tuple-element.51.fresh_k, ...), custom_call_target="tpu_custom_call" | custom-call | tf_op jit(solution)/shard_map/own/pallas_call | solution.py:254
  22.8 0.2 near.1
  23.0 2.3 %collective-permute-done.8.refs_1_ = bf16[33,16,128]{2,1,0:T(8,128)(2,1)S(1)} collective-permute-done((bf16[33,16,128]{2,1,0:T(8,128)(2,1)S(1)}, bf16[33,16,128]{2,1,0:T(8,128)(2,1)S(1)}, u32[]{:S(2)}, u32[]{:S(2)}) %collective-permute-start.8) | collective-permute-done | bytes 135200 | tf_op jit(solution)/shard_map/ppermute | solution.py:243
  25.3 0.0 collective-permute-done.7.refs_0_
  25.3 0.9 %final.1 = bf16[64,16,128]{2,1,0:T(8,128)(2,1)} custom-call(f32[64,16,128]{2,1,0:T(8,128)S(1)} %get-tuple-element.65.near, f32[8,128]{1,0:T(8,128)S(1)} %get-tuple-element.66.near_l, bf16[34,16,128]{2,1,0:T(8,128)(2,1)S(1)} %collective-permute-done.7.refs_0_, bf16[33,16,128]{2,1,0:T(8,128)(2,1)S(1)} %collective-permute-done.8.refs_1_), custom_call_target="tpu_custom_call" | custom-call | flops 1048576 | bytes 1048576 | tf_op jit(solution)/shard_map/final/pallas_call | solution.py:254
  (1 shorter events, 0.0 us)
Async XLA Ops:
  0.0 6.7 %collective-permute-start.1 = (bf16[64,16,128]{2,1,0:T(8,128)(2,1)}, bf16[64,16,128]{2,1,0:T(8,128)(2,1)S(1)}, u32[]{:S(2)}, u32[]{:S(2)}) collective-permute-start(bf16[64,16,128]{2,1,0:T(8,128)(2,1)} %refs_4_.1), channel_id=1, source_target_pairs={{0,4},{4,0},{8,12},{12,8},{1,5},{5,1},{9,13},{13,9},{2,6},{6,2},{1... | collective-permute-start | bytes 786440 | tf_op jit(solution)/shard_map/ppermute | solution.py:240
  0.5 9.7 %collective-permute-start = (bf16[64,16,128]{2,1,0:T(8,128)(2,1)}, bf16[64,16,128]{2,1,0:T(8,128)(2,1)S(1)}, u32[]{:S(2)}, u32[]{:S(2)}) collective-permute-start(bf16[64,16,128]{2,1,0:T(8,128)(2,1)} %refs_4_.1), channel_id=1, source_target_pairs={{0,8},{4,12},{8,0},{12,4},{1,9},{5,13},{9,1},{13,5},{2,10},{6,14},... | collective-permute-start | bytes 786440 | tf_op jit(solution)/shard_map/ppermute | solution.py:243
  2.9 3.7 %collective-permute-start.2 = (bf16[64,2,128]{2,1,0:T(2,128)(2,1)}, bf16[64,2,128]{2,1,0:T(2,128)(2,1)S(1)}, u32[]{:S(2)}, u32[]{:S(2)}) collective-permute-start(bf16[64,2,128]{2,1,0:T(2,128)(2,1)} %refs_2_.1), channel_id=1, source_target_pairs={{0,4},{4,0},{8,12},{12,8},{1,5},{5,1},{9,13},{13,9},{2,6},{6,2},{1... | collective-permute-start | bytes 98312 | tf_op jit(solution)/shard_map/ppermute | solution.py:240
  3.2 3.5 %collective-permute-start.3 = (bf16[64,2,128]{2,1,0:T(2,128)(2,1)}, bf16[64,2,128]{2,1,0:T(2,128)(2,1)S(1)}, u32[]{:S(2)}, u32[]{:S(2)}) collective-permute-start(bf16[64,2,128]{2,1,0:T(2,128)(2,1)} %refs_3_.1), channel_id=1, source_target_pairs={{0,4},{4,0},{8,12},{12,8},{1,5},{5,1},{9,13},{13,9},{2,6},{6,2},{1... | collective-permute-start | bytes 98312 | tf_op jit(solution)/shard_map/ppermute | solution.py:240
  10.1 1.7 %collective-permute-start.4 = (bf16[64,16,128]{2,1,0:T(8,128)(2,1)S(1)}, bf16[64,16,128]{2,1,0:T(8,128)(2,1)S(1)}, u32[]{:S(2)}, u32[]{:S(2)}) collective-permute-start(bf16[64,16,128]{2,1,0:T(8,128)(2,1)S(1)} %collective-permute-done.q), channel_id=1, source_target_pairs={{0,4},{4,0},{8,12},{12,8},{1,5},{5,1},{9,13},{13,9},{2,6},{6,2},{1... | collective-permute-start | bytes 786440 | tf_op jit(solution)/shard_map/ppermute | solution.py:240
  13.4 2.2 %collective-permute-start.5 = (bf16[99,16,128]{2,1,0:T(8,128)(2,1)S(1)}, bf16[99,16,128]{2,1,0:T(8,128)(2,1)S(1)}, u32[]{:S(2)}, u32[]{:S(2)}) collective-permute-start(bf16[99,16,128]{2,1,0:T(8,128)(2,1)S(1)} %diagonal.2), channel_id=1, source_target_pairs={{0,4},{4,0},{8,12},{12,8},{1,5},{5,1},{9,13},{13,9},{2,6},{6,2},{1... | collective-permute-start | bytes 1216520 | tf_op jit(solution)/shard_map/ppermute | solution.py:240
  15.6 3.8 %collective-permute-start.6 = (bf16[33,16,128]{2,1,0:T(8,128)(2,1)S(1)}, bf16[33,16,128]{2,1,0:T(8,128)(2,1)S(1)}, u32[]{:S(2)}, u32[]{:S(2)}) collective-permute-start(bf16[33,16,128]{2,1,0:T(8,128)(2,1)S(1)} %diagonal.3), channel_id=1, source_target_pairs={{0,4},{4,0},{8,12},{12,8},{1,5},{5,1},{9,13},{13,9},{2,6},{6,2},{1... | collective-permute-start | bytes 405512 | tf_op jit(solution)/shard_map/ppermute | solution.py:240
  15.8 9.5 %collective-permute-start.7 = (bf16[34,16,128]{2,1,0:T(8,128)(2,1)S(1)}, bf16[34,16,128]{2,1,0:T(8,128)(2,1)S(1)}, u32[]{:S(2)}, u32[]{:S(2)}) collective-permute-start(bf16[34,16,128]{2,1,0:T(8,128)(2,1)S(1)} %chip_sum.2), channel_id=1, source_target_pairs={{0,8},{4,12},{8,0},{12,4},{1,9},{5,13},{9,1},{13,5},{2,10},{6,14},... | collective-permute-start | bytes 417800 | tf_op jit(solution)/shard_map/ppermute | solution.py:243
  19.5 5.8 %collective-permute-start.8 = (bf16[33,16,128]{2,1,0:T(8,128)(2,1)S(1)}, bf16[33,16,128]{2,1,0:T(8,128)(2,1)S(1)}, u32[]{:S(2)}, u32[]{:S(2)}) collective-permute-start(bf16[33,16,128]{2,1,0:T(8,128)(2,1)S(1)} %chip_sum.3), channel_id=1, source_target_pairs={{0,8},{4,12},{8,0},{12,4},{1,9},{5,13},{9,1},{13,5},{2,10},{6,14},... | collective-permute-start | bytes 405512 | tf_op jit(solution)/shard_map/ppermute | solution.py:243

commit v4 on v3

--- a/solution.py
+++ b/solution.py
@@ -40,15 +40,22 @@
     )
 
 
-def load_kernel(length, *refs):
-    n = (len(refs) - 2) // 2
-    ins, outs, filled, sems = refs[:n], refs[n : 2 * n], refs[-2], refs[-1]
-    copies = [pltpu.make_async_copy(ins[i], outs[i], sems.at[i]) for i in range(n)]
-    for c in copies:
+def load_kernel(pieces, *refs):
+    *refs, held, sems = refs
+    n = (len(refs) - 1 - pieces) // 2
+    length, ins, outs, filled = refs[0], refs[1 : n + 1], refs[n + 1 : -1], refs[-1]
+    moves = list(zip(ins[:-1], outs))
+    for i in range(pieces):
+        m = outs[-1].shape[0]
+        moves.append((ins[-1].at[i * m : (i + 1) * m], outs[len(ins) - 1 + i]))
+    moves.append((length, held))
+    copies = [pltpu.make_async_copy(a, b, sems.at[i]) for i, (a, b) in enumerate(moves)]
+    for c in copies[::-1]:
         c.start()
     slots = ins[0].shape[0]
-    filled[...] = jnp.full(filled.shape, jnp.clip(length[0] - lax.axis_index("ctx") * slots, 0, slots), jnp.int32)
-    for c in copies:
+    copies[-1].wait()
+    filled[...] = jnp.full(filled.shape, jnp.clip(held[0] - lax.axis_index("ctx") * slots, 0, slots), jnp.int32)
+    for c in copies[:-1]:
         c.wait()
 
 
@@ -95,8 +102,8 @@
     return jax.ShapeDtypeStruct((shape.shape[0] + rows,) + shape.shape[1:], shape.dtype)
 
 
-def attend(q_ref, keys, values, first, n, o_ref, fresh=None, causal=None):
-    heads, hd = q_ref.shape[1:]
+def attend(q_refs, keys, values, first, n, o_ref, fresh=None, causal=None):
+    heads, hd = q_refs[0].shape[1:]
     kv = keys.shape[0]
     group = heads // kv
     rows = n * group
@@ -107,7 +114,11 @@
         seen = token >= lax.broadcasted_iota(jnp.int32, (rows, count), 1)
 
     def scores(h):
-        q = q_ref[first : first + n, h * group : (h + 1) * group, :].reshape(rows, hd)
+        cut = slice(h * group, (h + 1) * group)
+        if len(q_refs) == 1:
+            q = q_refs[0][first : first + n, cut, :].reshape(rows, hd)
+        else:
+            q = jnp.concatenate([x[:, cut, :].reshape(x.shape[0] * group, hd) for x in q_refs], axis=0)
         found = [lax.dot_general(q, keys[h], NT, preferred_element_type=F32)]
         if fresh is not None:
             s = lax.dot_general(q, fresh[0][h], NT, preferred_element_type=F32)
@@ -165,7 +176,7 @@
 
 def shard_kernel(first, n, q, keys, values, *refs):
     o = refs[-1]
-    attend(q, keys, values, first, n, o)
+    attend([q], keys, values, first, n, o)
     if len(refs) > 1:
         o[o.shape[0] - refs[0].shape[0] :] = refs[0][...]
 
@@ -176,15 +187,21 @@
 
     @pl.when(sees)
     def _():
-        attend(q, keys, values, first, n, o, (fresh_k, fresh_v))
+        attend([q], keys, values, first, n, o, (fresh_k, fresh_v))
 
     @pl.when(jnp.logical_not(sees))
     def _():
-        attend(q, keys, values, first, n, o)
-
-
-def own_kernel(q, keys, values, fresh_k, fresh_v, o):
-    tokens = q.shape[0]
+        attend([q], keys, values, first, n, o)
+
+
+def sibling_kernel(*refs):
+    *q, keys, values, o = refs
+    attend(q, keys, values, 0, sum(x.shape[0] for x in q), o)
+
+
+def own_kernel(*refs):
+    *q, keys, values, fresh_k, fresh_v, o = refs
+    tokens = sum(x.shape[0] for x in q)
     core = lax.axis_index("ctx") % CORES
     attend(q, keys, values, 0, tokens, o, (fresh_k, fresh_v), core * tokens)
 
@@ -265,25 +282,28 @@
     small = pl.CostEstimate(flops=2**20, bytes_accessed=2**20, transcendentals=2**14)
     q_chip = [over_chip(queries, step) for step in range(1, chips)]
     moved = (cache_keys, cache_values, new_keys, new_values, queries)
-    k, v, nk, nv, q_own, filled = pl.pallas_call(
-        load_kernel,
-        out_shape=[jax.ShapeDtypeStruct(x.shape, x.dtype) for x in moved]
-        + [jax.ShapeDtypeStruct((8, hd), jnp.int32)],
-        in_specs=[SMEM] + [HBM] * len(moved),
-        out_specs=[VMEM] * (len(moved) + 1),
-        scratch_shapes=[pltpu.SemaphoreType.DMA((len(moved),))],
+    pieces = 2
+    out = [jax.ShapeDtypeStruct(x.shape, x.dtype) for x in moved[:-1]]
+    out += [jax.ShapeDtypeStruct((tokens // pieces, heads, hd), BF16)] * pieces
+    out += [jax.ShapeDtypeStruct((8, hd), jnp.int32)]
+    k, v, nk, nv, *q_own, filled = pl.pallas_call(
+        functools.partial(load_kernel, pieces),
+        out_shape=out,
+        in_specs=[pl.BlockSpec(memory_space=pl.ANY)] + [HBM] * len(moved),
+        out_specs=[VMEM] * len(out),
+        scratch_shapes=[pltpu.SMEM((1,), jnp.int32), pltpu.SemaphoreType.DMA((len(out),))],
         compiler_params=params(),
-        cost_estimate=small,
+        cost_estimate=tiny,
         name="load",
     )(cache_len, *[pltpu.with_memory_space_constraint(x, pltpu.HBM) for x in moved])
-    q_core, nk_core, nv_core = over_core(queries), over_core(new_keys), over_core(new_values)
-    q_core, nk_core, nv_core = lax.optimization_barrier((q_core, nk_core, nv_core))
+    q_core, nk_core, nv_core = [over_core(x) for x in q_own], over_core(nk), over_core(nv)
+    *q_core, nk_core, nv_core = lax.optimization_barrier((*q_core, nk_core, nv_core))
     keys, values = call(
         "prepare",
         prepare_kernel,
         [jax.ShapeDtypeStruct((kv, slots, hd), BF16), jax.ShapeDtypeStruct((kv, slots, 2 * hd), BF16)],
         (filled, k, v, nk),
-        small,
+        tiny,
     )
     shard = (keys, values)
     fresh = call(
@@ -291,14 +311,15 @@
         fresh_kernel,
         [jax.ShapeDtypeStruct((kv, CORES * tokens, hd), BF16), jax.ShapeDtypeStruct((kv, CORES * tokens, 2 * hd), BF16)],
         (nk, nv, nk_core, nv_core),
-        small,
-    )
-    q_core, *fresh = lax.optimization_barrier((q_core, *fresh))
+        tiny,
+    )
+    *q_core, fresh_k, fresh_v = lax.optimization_barrier((*q_core, *fresh))
+    fresh = (fresh_k, fresh_v)
 
     def attend_part(name, kernel, m, *args):
         return call(name, kernel, packed(m), args, cost(m))
 
-    sib = attend_part("sibling", functools.partial(shard_kernel, 0, tokens), tokens, q_core, *shard)
+    sib = call("sibling", sibling_kernel, packed(tokens), (*q_core, *shard), tiny)
     *q_chip, sib = lax.optimization_barrier((*q_chip, sib))
     q_diag = [over_core(q) for q in q_chip]
     far = []
@@ -328,9 +349,9 @@
             straight = straight_part(q_s, first, m) if i else early
             shape = extended(packed(m), len(shares) - 1 - i)
             both = call("chip_sum", functools.partial(chip_sum_kernel, group, m), shape, (diag[i], straight), tiny)
-            q_s, q_own, both = lax.optimization_barrier((q_s, q_own, both))
+            q_s, both, *q_own = lax.optimization_barrier((q_s, both, *q_own))
             far.append(over_chip(both, chips - step))
-    own = call("own", own_kernel, packed(tokens), (q_own, *shard, *fresh), tiny)
+    own = call("own", own_kernel, packed(tokens), (*q_own, *shard, *fresh), tiny)
     near = call(
         "near",
         functools.partial(near_kernel, group),

time: 26.4 us -> 26 us (0.985)
  waiting for transfers between devices: 3.05 us -> 1.53 us
  starting transfers between devices: 5.9 us -> 6.83 us
    ppermute x3, waiting for transfers between devices: 3.03 us -> 1.51 us  [over_chip(): lax.ppermute(x, 'ctx', [(i, (i // CORES + step) % chips * CORES + i % COR...]
    ppermute x6 -> x7, starting transfers between devices: 1.61 us -> 2.08 us  [over_core(): return lax.ppermute(x, 'ctx', [(i, i ^ 1) for i in range(n)])]
    ppermute x3, starting transfers between devices: 4.29 us -> 4.74 us  [over_chip(): lax.ppermute(x, 'ctx', [(i, (i // CORES + step) % chips * CORES + i % COR...]
  transfers between devices with their start and end apart: 9 -> 10, of which waited for: 2 -> 1; matrix products, arithmetic and copies ran while one was open for 0% -> 0% of each run, Pallas kernels for 54% -> 55%
where the time goes in v4:
time: 26 us; the launch traced here: 25.8 us
  Pallas kernels  16.7 us (64%)
  starting transfers between devices  6.83 us (26%)
  waiting for transfers between devices  1.53 us (6%)
  between operations  0.77 us (3%)
    pallas_call x12, Pallas kernels, call(): pl.pallas_call(kernel, out_shape=out, in_specs=[VMEM] * len(args), out_sp...  14.9 us
    ppermute x3, starting transfers between devices, over_chip(): lax.ppermute(x, 'ctx', [(i, (i // CORES + step) % chips * CORES + i % COR...  4.74 us
    ppermute x7, starting transfers between devices, over_core(): return lax.ppermute(x, 'ctx', [(i, i ^ 1) for i in range(n)])  2.08 us
    pallas_call x1, Pallas kernels, per_device(): pl.pallas_call(functools.partial(load_kernel, pieces), out_shape=out, in_...  1.8 us
    ppermute x3, waiting for transfers between devices, over_chip(): lax.ppermute(x, 'ctx', [(i, (i // CORES + step) % chips * CORES + i % COR...  1.51 us
  transfers between devices with their start and end apart: 10, of which 1 were waited for; matrix products, arithmetic and copies ran while one was open for 0% of the time, Pallas kernels for 55%

profile of v4, /device:TPU:0, one launch (start us, length us, event | category | flops | bytes accessed | tf_op | source)
XLA Modules:
  0.0 25.8 jit_solution(9271451117895009841)
XLA Ops:
  0.0 2.9 %collective-permute-start = (bf16[64,16,128]{2,1,0:T(8,128)(2,1)}, bf16[64,16,128]{2,1,0:T(8,128)(2,1)S(1)}, u32[]{:S(2)}, u32[]{:S(2)}) collective-permute-start(bf16[64,16,128]{2,1,0:T(8,128)(2,1)} %refs_5_.1), channel_id=1, source_target_pairs={{0,8},{4,12},{8,0},{12,4},{1,9},{5,13},{9,1},{13,5},{2,10},{6,14},... | collective-permute-start | bytes 786440 | tf_op jit(solution)/shard_map/ppermute | solution.py:260
  3.6 1.8 %load.1 = (bf16[2048,2,128]{2,1,0:T(2,128)(2,1)S(1)}, bf16[2048,2,128]{2,1,0:T(2,128)(2,1)S(1)}, bf16[64,2,128]{2,1,0:T(2,128)(2,1)S(1)}, bf16[64,2,128]{2,1,0:T...) custom-call(s32[1]{0:T(128)S(6)} %copy.7.refs_0_, ...), custom_call_target="tpu_custom_call" | custom-call | tf_op jit(solution)/shard_map/load/pallas_call | solution.py:289
  5.4 0.1 collective-permute-start.1
  5.5 0.5 %collective-permute-start.2 = (bf16[32,16,128]{2,1,0:T(8,128)(2,1)S(1)}, bf16[32,16,128]{2,1,0:T(8,128)(2,1)S(1)}, u32[]{:S(2)}, u32[]{:S(2)}) collective-permute-start(bf16[32,16,128]{2,1,0:T(8,128)(2,1)S(1)} %get-tuple-element.74.refs_1_), channel_id=1, source_target_pairs={{0,4},{4,0},{8,12},{12,8},{1,5},{5,1},{9,13},{13,9},{2,6},{6,2},{1... | collective-permute-start | bytes 393224 | tf_op jit(solution)/shard_map/ppermute | solution.py:257
  6.0 0.1 collective-permute-start.3
  6.0 0.4 %collective-permute-start.4 = (bf16[64,2,128]{2,1,0:T(2,128)(2,1)S(1)}, bf16[64,2,128]{2,1,0:T(2,128)(2,1)S(1)}, u32[]{:S(2)}, u32[]{:S(2)}) collective-permute-start(bf16[64,2,128]{2,1,0:T(2,128)(2,1)S(1)} %get-tuple-element.45.nv), channel_id=1, source_target_pairs={{0,4},{4,0},{8,12},{12,8},{1,5},{5,1},{9,13},{13,9},{2,6},{6,2},{1... | collective-permute-start | bytes 98312 | tf_op jit(solution)/shard_map/ppermute | solution.py:257
  6.5 0.9 %prepare.1 = (bf16[2,2048,128]{2,1,0:T(8,128)(2,1)S(1)}, bf16[2,2048,256]{2,1,0:T(8,128)(2,1)S(1)}) custom-call(s32[8,128]{1,0:T(8,128)S(1)} %get-tuple-element.54.filled, bf16[2048,2,128]{2,1,0:T(2,128)(2,1)S(1)} %get-tuple-element.55.k, bf16[2048,2,128]{2,1,0:T(2,128)(2,1)S(1)} %get-tuple-element.56.v, bf16[64,2,128]{2,1,0:T(2,128)(2,1)S(1)} %get-tuple-element.44.nk), custom_call_target="tpu_custom_call" | custom-call | tf_op jit(solution)/shard_map/prepare/pallas_call | solution.py:271
  7.4 0.0 collective-permute-done.3.nk_core
  7.4 0.0 collective-permute-done.4.nv_core
  7.4 0.0 collective-permute-done.1.refs_0_
  7.4 0.0 collective-permute-done.2.refs_1_
  7.5 2.6 %sibling.1.refs_0_ = bf16[66,16,128]{2,1,0:T(8,128)(2,1)S(1)} custom-call(bf16[32,16,128]{2,1,0:T(8,128)(2,1)S(1)} %collective-permute-done.1.refs_0_, bf16[32,16,128]{2,1,0:T(8,128)(2,1)S(1)} %collective-permute-done.2.refs_1_, bf16[2,2048,128]{2,1,0:T(8,128)(2,1)S(1)} %get-tuple-element.57.refs_2_.keys, ...), custom_call_target="tpu_custom_call" | custom-call | tf_op jit(solution)/shard_map/sibling/pallas_call | solution.py:271
  10.1 0.0 collective-permute-done.q
  10.1 0.4 %collective-permute-start.5 = (bf16[64,16,128]{2,1,0:T(8,128)(2,1)S(1)}, bf16[64,16,128]{2,1,0:T(8,128)(2,1)S(1)}, u32[]{:S(2)}, u32[]{:S(2)}) collective-permute-start(bf16[64,16,128]{2,1,0:T(8,128)(2,1)S(1)} %collective-permute-done.q), channel_id=1, source_target_pairs={{0,4},{4,0},{8,12},{12,8},{1,5},{5,1},{9,13},{13,9},{2,6},{6,2},{1... | collective-permute-start | bytes 786440 | tf_op jit(solution)/shard_map/ppermute | solution.py:257
  10.5 1.7 %straight.2.b = bf16[33,16,128]{2,1,0:T(8,128)(2,1)S(1)} custom-call(bf16[64,16,128]{2,1,0:T(8,128)(2,1)S(1)} %collective-permute-done.q, bf16[2,2048,128]{2,1,0:T(8,128)(2,1)S(1)} %get-tuple-element.57.refs_2_.keys, bf16[2,2048,256]{2,1,0:T(8,128)(2,1)S(1)} %get-tuple-element.58.refs_3_.values, bf16[2,128,128]{2,1,0:T(8,128)(2,1)S(1)} %get-tuple-element.60.fresh_k.refs_4_, ...), custom_call_target="tpu_custom_call" | custom-call | flops 1073741824 | bytes 4194304 | tf_op jit(solution)/shard_map/straight/pallas_call | solution.py:271
  12.2 0.0 collective-permute-done.5.q
  12.2 1.6 %diagonal.2 = bf16[99,16,128]{2,1,0:T(8,128)(2,1)S(1)} custom-call(bf16[64,16,128]{2,1,0:T(8,128)(2,1)S(1)} %collective-permute-done.5.q, bf16[2,2048,128]{2,1,0:T(8,128)(2,1)S(1)} %get-tuple-element.57.refs_2_.keys, bf16[2,2048,256]{2,1,0:T(8,128)(2,1)S(1)} %get-tuple-element.58.refs_3_.values, bf16[66,16,128]{2,1,0:T(8,128)(2,1)S(1)} %sibling.1.refs_0_), custom_call_target="tpu_custom_call" | custom-call | flops 1073741824 | bytes 4194304 | tf_op jit(solution)/shard_map/diagonal/pallas_call | solution.py:271
  13.8 0.3 %collective-permute-start.6 = (bf16[99,16,128]{2,1,0:T(8,128)(2,1)S(1)}, bf16[99,16,128]{2,1,0:T(8,128)(2,1)S(1)}, u32[]{:S(2)}, u32[]{:S(2)}) collective-permute-start(bf16[99,16,128]{2,1,0:T(8,128)(2,1)S(1)} %diagonal.2), channel_id=1, source_target_pairs={{0,4},{4,0},{8,12},{12,8},{1,5},{5,1},{9,13},{13,9},{2,6},{6,2},{1... | collective-permute-start | bytes 1216520 | tf_op jit(solution)/shard_map/ppermute | solution.py:257
  14.0 1.5 %diagonal.3 = bf16[33,16,128]{2,1,0:T(8,128)(2,1)S(1)} custom-call(bf16[64,16,128]{2,1,0:T(8,128)(2,1)S(1)} %collective-permute-done.5.q, bf16[2,2048,128]{2,1,0:T(8,128)(2,1)S(1)} %get-tuple-element.57.refs_2_.keys, bf16[2,2048,256]{2,1,0:T(8,128)(2,1)S(1)} %get-tuple-element.58.refs_3_.values), custom_call_target="tpu_custom_call" | custom-call | flops 1073741824 | bytes 4194304 | tf_op jit(solution)/shard_map/diagonal/pallas_call | solution.py:271
  15.6 0.4 %collective-permute-start.7 = (bf16[33,16,128]{2,1,0:T(8,128)(2,1)S(1)}, bf16[33,16,128]{2,1,0:T(8,128)(2,1)S(1)}, u32[]{:S(2)}, u32[]{:S(2)}) collective-permute-start(bf16[33,16,128]{2,1,0:T(8,128)(2,1)S(1)} %diagonal.3), channel_id=1, source_target_pairs={{0,4},{4,0},{8,12},{12,8},{1,5},{5,1},{9,13},{13,9},{2,6},{6,2},{1... | collective-permute-start | bytes 405512 | tf_op jit(solution)/shard_map/ppermute | solution.py:257
  16.0 0.0 collective-permute-done.6.a.sib
  16.0 0.2 chip_sum.2
  16.1 0.6 %collective-permute-start.8 = (bf16[34,16,128]{2,1,0:T(8,128)(2,1)S(1)}, bf16[34,16,128]{2,1,0:T(8,128)(2,1)S(1)}, u32[]{:S(2)}, u32[]{:S(2)}) collective-permute-start(bf16[34,16,128]{2,1,0:T(8,128)(2,1)S(1)} %chip_sum.2), channel_id=1, source_target_pairs={{0,8},{4,12},{8,0},{12,4},{1,9},{5,13},{9,1},{13,5},{2,10},{6,14},... | collective-permute-start | bytes 417800 | tf_op jit(solution)/shard_map/ppermute | solution.py:260
  16.8 1.9 %straight.3.b = bf16[33,16,128]{2,1,0:T(8,128)(2,1)S(1)} custom-call(bf16[64,16,128]{2,1,0:T(8,128)(2,1)S(1)} %collective-permute-done.q, bf16[2,2048,128]{2,1,0:T(8,128)(2,1)S(1)} %get-tuple-element.57.refs_2_.keys, bf16[2,2048,256]{2,1,0:T(8,128)(2,1)S(1)} %get-tuple-element.58.refs_3_.values, bf16[2,128,128]{2,1,0:T(8,128)(2,1)S(1)} %get-tuple-element.60.fresh_k.refs_4_, ...), custom_call_target="tpu_custom_call" | custom-call | tf_op jit(solution)/shard_map/straight/pallas_call | solution.py:271
  18.7 0.0 collective-permute-done.7.a
  18.7 0.2 chip_sum.3
  18.9 1.2 %collective-permute-start.9 = (bf16[33,16,128]{2,1,0:T(8,128)(2,1)S(1)}, bf16[33,16,128]{2,1,0:T(8,128)(2,1)S(1)}, u32[]{:S(2)}, u32[]{:S(2)}) collective-permute-start(bf16[33,16,128]{2,1,0:T(8,128)(2,1)S(1)} %chip_sum.3), channel_id=1, source_target_pairs={{0,8},{4,12},{8,0},{12,4},{1,9},{5,13},{9,1},{13,5},{2,10},{6,14},... | collective-permute-start | bytes 405512 | tf_op jit(solution)/shard_map/ppermute | solution.py:260
  20.0 3.1 %own.1 = bf16[66,16,128]{2,1,0:T(8,128)(2,1)S(1)} custom-call(bf16[32,16,128]{2,1,0:T(8,128)(2,1)S(1)} %get-tuple-element.73.refs_0_, bf16[32,16,128]{2,1,0:T(8,128)(2,1)S(1)} %get-tuple-element.74.refs_1_, bf16[2,2048,128]{2,1,0:T(8,128)(2,1)S(1)} %get-tuple-element.57.refs_2_.keys, bf16[2,2048,256]{2,1,0:T(8,128)(2,1)S(1)} %get-tuple-element.58.refs_3_.values, ...), custom_call_target="tpu_custom_call" | custom-call | tf_op jit(solution)/shard_map/own/pallas_call | solution.py:271
  23.1 0.2 near.1
  23.4 1.5 %collective-permute-done.9.refs_1_ = bf16[33,16,128]{2,1,0:T(8,128)(2,1)S(1)} collective-permute-done((bf16[33,16,128]{2,1,0:T(8,128)(2,1)S(1)}, bf16[33,16,128]{2,1,0:T(8,128)(2,1)S(1)}, u32[]{:S(2)}, u32[]{:S(2)}) %collective-permute-start.9) | collective-permute-done | bytes 135200 | tf_op jit(solution)/shard_map/ppermute | solution.py:260
  24.9 0.0 collective-permute-done.8.refs_0_
  24.9 0.9 %final.1 = bf16[64,16,128]{2,1,0:T(8,128)(2,1)} custom-call(f32[64,16,128]{2,1,0:T(8,128)S(1)} %get-tuple-element.75.near, f32[8,128]{1,0:T(8,128)S(1)} %get-tuple-element.76.near_l, bf16[34,16,128]{2,1,0:T(8,128)(2,1)S(1)} %collective-permute-done.8.refs_0_, bf16[33,16,128]{2,1,0:T(8,128)(2,1)S(1)} %collective-permute-done.9.refs_1_), custom_call_target="tpu_custom_call" | custom-call | flops 1048576 | bytes 1048576 | tf_op jit(solution)/shard_map/final/pallas_call | solution.py:271
  (1 shorter events, 0.0 us)
Async XLA Ops:
  0.0 10.1 %collective-permute-start = (bf16[64,16,128]{2,1,0:T(8,128)(2,1)}, bf16[64,16,128]{2,1,0:T(8,128)(2,1)S(1)}, u32[]{:S(2)}, u32[]{:S(2)}) collective-permute-start(bf16[64,16,128]{2,1,0:T(8,128)(2,1)} %refs_5_.1), channel_id=1, source_target_pairs={{0,8},{4,12},{8,0},{12,4},{1,9},{5,13},{9,1},{13,5},{2,10},{6,14},... | collective-permute-start | bytes 786440 | tf_op jit(solution)/shard_map/ppermute | solution.py:260
  5.4 2.0 %collective-permute-start.1 = (bf16[32,16,128]{2,1,0:T(8,128)(2,1)S(1)}, bf16[32,16,128]{2,1,0:T(8,128)(2,1)S(1)}, u32[]{:S(2)}, u32[]{:S(2)}) collective-permute-start(bf16[32,16,128]{2,1,0:T(8,128)(2,1)S(1)} %get-tuple-element.73.refs_0_), channel_id=1, source_target_pairs={{0,4},{4,0},{8,12},{12,8},{1,5},{5,1},{9,13},{13,9},{2,6},{6,2},{1... | collective-permute-start | bytes 393224 | tf_op jit(solution)/shard_map/ppermute | solution.py:257
  5.5 1.9 %collective-permute-start.2 = (bf16[32,16,128]{2,1,0:T(8,128)(2,1)S(1)}, bf16[32,16,128]{2,1,0:T(8,128)(2,1)S(1)}, u32[]{:S(2)}, u32[]{:S(2)}) collective-permute-start(bf16[32,16,128]{2,1,0:T(8,128)(2,1)S(1)} %get-tuple-element.74.refs_1_), channel_id=1, source_target_pairs={{0,4},{4,0},{8,12},{12,8},{1,5},{5,1},{9,13},{13,9},{2,6},{6,2},{1... | collective-permute-start | bytes 393224 | tf_op jit(solution)/shard_map/ppermute | solution.py:257
  6.0 1.4 %collective-permute-start.3 = (bf16[64,2,128]{2,1,0:T(2,128)(2,1)S(1)}, bf16[64,2,128]{2,1,0:T(2,128)(2,1)S(1)}, u32[]{:S(2)}, u32[]{:S(2)}) collective-permute-start(bf16[64,2,128]{2,1,0:T(2,128)(2,1)S(1)} %get-tuple-element.44.nk), channel_id=1, source_target_pairs={{0,4},{4,0},{8,12},{12,8},{1,5},{5,1},{9,13},{13,9},{2,6},{6,2},{1... | collective-permute-start | bytes 98312 | tf_op jit(solution)/shard_map/ppermute | solution.py:257
  6.0 1.3 %collective-permute-start.4 = (bf16[64,2,128]{2,1,0:T(2,128)(2,1)S(1)}, bf16[64,2,128]{2,1,0:T(2,128)(2,1)S(1)}, u32[]{:S(2)}, u32[]{:S(2)}) collective-permute-start(bf16[64,2,128]{2,1,0:T(2,128)(2,1)S(1)} %get-tuple-element.45.nv), channel_id=1, source_target_pairs={{0,4},{4,0},{8,12},{12,8},{1,5},{5,1},{9,13},{13,9},{2,6},{6,2},{1... | collective-permute-start | bytes 98312 | tf_op jit(solution)/shard_map/ppermute | solution.py:257
  10.1 2.1 %collective-permute-start.5 = (bf16[64,16,128]{2,1,0:T(8,128)(2,1)S(1)}, bf16[64,16,128]{2,1,0:T(8,128)(2,1)S(1)}, u32[]{:S(2)}, u32[]{:S(2)}) collective-permute-start(bf16[64,16,128]{2,1,0:T(8,128)(2,1)S(1)} %collective-permute-done.q), channel_id=1, source_target_pairs={{0,4},{4,0},{8,12},{12,8},{1,5},{5,1},{9,13},{13,9},{2,6},{6,2},{1... | collective-permute-start | bytes 786440 | tf_op jit(solution)/shard_map/ppermute | solution.py:257
  13.8 2.2 %collective-permute-start.6 = (bf16[99,16,128]{2,1,0:T(8,128)(2,1)S(1)}, bf16[99,16,128]{2,1,0:T(8,128)(2,1)S(1)}, u32[]{:S(2)}, u32[]{:S(2)}) collective-permute-start(bf16[99,16,128]{2,1,0:T(8,128)(2,1)S(1)} %diagonal.2), channel_id=1, source_target_pairs={{0,4},{4,0},{8,12},{12,8},{1,5},{5,1},{9,13},{13,9},{2,6},{6,2},{1... | collective-permute-start | bytes 1216520 | tf_op jit(solution)/shard_map/ppermute | solution.py:257
  15.6 3.1 %collective-permute-start.7 = (bf16[33,16,128]{2,1,0:T(8,128)(2,1)S(1)}, bf16[33,16,128]{2,1,0:T(8,128)(2,1)S(1)}, u32[]{:S(2)}, u32[]{:S(2)}) collective-permute-start(bf16[33,16,128]{2,1,0:T(8,128)(2,1)S(1)} %diagonal.3), channel_id=1, source_target_pairs={{0,4},{4,0},{8,12},{12,8},{1,5},{5,1},{9,13},{13,9},{2,6},{6,2},{1... | collective-permute-start | bytes 405512 | tf_op jit(solution)/shard_map/ppermute | solution.py:257
  16.1 8.8 %collective-permute-start.8 = (bf16[34,16,128]{2,1,0:T(8,128)(2,1)S(1)}, bf16[34,16,128]{2,1,0:T(8,128)(2,1)S(1)}, u32[]{:S(2)}, u32[]{:S(2)}) collective-permute-start(bf16[34,16,128]{2,1,0:T(8,128)(2,1)S(1)} %chip_sum.2), channel_id=1, source_target_pairs={{0,8},{4,12},{8,0},{12,4},{1,9},{5,13},{9,1},{13,5},{2,10},{6,14},... | collective-permute-start | bytes 417800 | tf_op jit(solution)/shard_map/ppermute | solution.py:260
  18.9 6.0 %collective-permute-start.9 = (bf16[33,16,128]{2,1,0:T(8,128)(2,1)S(1)}, bf16[33,16,128]{2,1,0:T(8,128)(2,1)S(1)}, u32[]{:S(2)}, u32[]{:S(2)}) collective-permute-start(bf16[33,16,128]{2,1,0:T(8,128)(2,1)S(1)} %chip_sum.3), channel_id=1, source_target_pairs={{0,8},{4,12},{8,0},{12,4},{1,9},{5,13},{9,1},{13,5},{2,10},{6,14},... | collective-permute-start | bytes 405512 | tf_op jit(solution)/shard_map/ppermute | solution.py:260

commit v5 on v4

--- a/solution.py
+++ b/solution.py
@@ -40,35 +40,38 @@
     )
 
 
-def load_kernel(pieces, *refs):
-    *refs, held, sems = refs
-    n = (len(refs) - 1 - pieces) // 2
-    length, ins, outs, filled = refs[0], refs[1 : n + 1], refs[n + 1 : -1], refs[-1]
-    moves = list(zip(ins[:-1], outs))
-    for i in range(pieces):
-        m = outs[-1].shape[0]
-        moves.append((ins[-1].at[i * m : (i + 1) * m], outs[len(ins) - 1 + i]))
+def load_kernel(length, k, v, q, nk, nv, k_out, v_out, qk, qv, filled, held, sems):
+    m = q.shape[0] // 2
+    moves = [(k, k_out), (v, v_out)]
+    for i, (new, out) in enumerate(((nk, qk), (nv, qv))):
+        moves += [(q.at[i * m : (i + 1) * m], out.at[0:m]), (new, out.at[m:])]
     moves.append((length, held))
     copies = [pltpu.make_async_copy(a, b, sems.at[i]) for i, (a, b) in enumerate(moves)]
     for c in copies[::-1]:
         c.start()
-    slots = ins[0].shape[0]
+    slots = k.shape[0]
     copies[-1].wait()
     filled[...] = jnp.full(filled.shape, jnp.clip(held[0] - lax.axis_index("ctx") * slots, 0, slots), jnp.int32)
     for c in copies[:-1]:
         c.wait()
 
 
-def prepare_kernel(filled, k, v, nk, keys, values):
+def prepare_kernel(new, filled, k, v, qk, keys, values):
     slots, kv, hd = k.shape
-    count = filled[0:1, :]
-    included = lax.broadcasted_iota(jnp.int32, (slots, hd), 0) < count
-    k_rows, v_rows, nk_rows = [jnp.swapaxes(x[...], 0, 1) for x in (k, v, nk)]
-    for h in range(kv):
-        fill = jnp.where(count > 0, k_rows[h, 0:1].astype(F32), nk_rows[h, 0:1].astype(F32))
-        keys[h] = jnp.where(included, k_rows[h].astype(F32), fill).astype(BF16)
-        values[h, :, 0:hd] = jnp.where(included, v_rows[h].astype(F32), 0.0).astype(BF16)
-        values[h, :, hd:] = jnp.where(included, 1.0, 0.0).astype(BF16)
+    keys[...] = jnp.swapaxes(k[...], 0, 1)
+    values[:, :, 0:hd] = jnp.swapaxes(v[...], 0, 1)
+    values[:, :, hd:] = jnp.ones((kv, slots, hd), BF16)
+
+    @pl.when(filled[0, 0] < slots)
+    def _():
+        count = filled[0:1, :]
+        included = lax.broadcasted_iota(jnp.int32, (slots, hd), 0) < count
+        first = qk[new].astype(F32)
+        for h in range(kv):
+            fill = jnp.where(count > 0, keys[h, 0:1, :].astype(F32), first[h : h + 1])
+            keys[h] = jnp.where(included, keys[h].astype(F32), fill).astype(BF16)
+            values[h, :, 0:hd] = jnp.where(included, values[h, :, 0:hd].astype(F32), 0.0).astype(BF16)
+            values[h, :, hd:] = jnp.where(included, 1.0, 0.0).astype(BF16)
 
 
 def put_lse(ref, first, lse):
@@ -118,7 +121,8 @@
         if len(q_refs) == 1:
             q = q_refs[0][first : first + n, cut, :].reshape(rows, hd)
         else:
-            q = jnp.concatenate([x[:, cut, :].reshape(x.shape[0] * group, hd) for x in q_refs], axis=0)
+            m = n // len(q_refs)
+            q = jnp.concatenate([x[0:m, cut, :].reshape(m * group, hd) for x in q_refs], axis=0)
         found = [lax.dot_general(q, keys[h], NT, preferred_element_type=F32)]
         if fresh is not None:
             s = lax.dot_general(q, fresh[0][h], NT, preferred_element_type=F32)
@@ -144,14 +148,17 @@
     put_lse(o_ref, n, jnp.concatenate(lses, axis=0))
 
 
-def fresh_kernel(nk, nv, nk_core, nv_core, keys, values):
+def fresh_kernel(m, qk, qv, qk_core, qv_core, keys, values, rows):
     low = lax.axis_index("ctx") % CORES == 0
-    tokens, kv, hd = nk.shape
-    for mine, other, out in ((nk, nk_core, keys), (nv, nv_core, values)):
-        mine, other = [jnp.swapaxes(x[...], 0, 1).astype(F32) for x in (mine, other)]
-        out[:, 0:tokens, 0:hd] = jnp.where(low, mine, other).astype(BF16)
-        out[:, tokens:, 0:hd] = jnp.where(low, other, mine).astype(BF16)
-    values[:, :, hd:] = jnp.ones((kv, CORES * tokens, hd), BF16)
+    kv, count, hd = keys.shape
+    tokens = count // CORES
+    for mine, other, out in ((qk, qk_core, keys), (qv, qv_core, values)):
+        mine, other = mine[m:].astype(F32), other[m:].astype(F32)
+        for i, x in enumerate((jnp.where(low, mine, other), jnp.where(low, other, mine))):
+            rows[...] = x.reshape(tokens * kv, hd)
+            for h in range(kv):
+                out[h, i * tokens : (i + 1) * tokens, 0:hd] = rows[pl.ds(h, tokens, stride=kv), :].astype(BF16)
+    values[:, :, hd:] = jnp.ones((kv, count, hd), BF16)
 
 
 def blend(parts, group):
@@ -194,16 +201,13 @@
         attend([q], keys, values, first, n, o)
 
 
-def sibling_kernel(*refs):
-    *q, keys, values, o = refs
-    attend(q, keys, values, 0, sum(x.shape[0] for x in q), o)
-
-
-def own_kernel(*refs):
-    *q, keys, values, fresh_k, fresh_v, o = refs
-    tokens = sum(x.shape[0] for x in q)
+def sibling_kernel(tokens, qk, qv, keys, values, o):
+    attend([qk, qv], keys, values, 0, tokens, o)
+
+
+def own_kernel(tokens, qk, qv, keys, values, fresh_k, fresh_v, o):
     core = lax.axis_index("ctx") % CORES
-    attend(q, keys, values, 0, tokens, o, (fresh_k, fresh_v), core * tokens)
+    attend([qk, qv], keys, values, 0, tokens, o, (fresh_k, fresh_v), core * tokens)
 
 
 def chip_sum_kernel(group, n, a, b, o):
@@ -232,15 +236,18 @@
     l[...] = lse
 
 
-def final_kernel(group, shares, near, near_l, *refs):
-    *far, o = refs
+def final_kernel(group, first, n, near, near_l, *refs):
+    *far, o, rows, sem = refs
+    far = far[: len(far) - (first > 0)]
     tokens, heads, hd = o.shape
-    for i, (first, n) in enumerate(shares):
-        lse = cut_lse(near_l[...], heads // group, first, n, tokens)
-        parts = [(near[first : first + n], lse)] + [(x[0:n], get_lse(x, n)) for x in far[i :: len(shares)]]
-        outs, _ = blend(parts, group)
-        for h, x in enumerate(outs):
-            o[first : first + n, h * group : (h + 1) * group, :] = x.astype(BF16).reshape(n, group, hd)
+    lse = cut_lse(near_l[...], heads // group, first, n, tokens)
+    parts = [(near[first : first + n], lse)] + [(x[0:n], get_lse(x, n)) for x in far]
+    outs, _ = blend(parts, group)
+    for h, x in enumerate(outs):
+        rows[:, h * group : (h + 1) * group, :] = x.astype(BF16).reshape(n, group, hd)
+    copy = pltpu.make_async_copy(rows, o.at[first : first + n], sem)
+    copy.start()
+    copy.wait()
 
 
 def per_device(queries, new_keys, new_values, cache_keys, cache_values, cache_len):
@@ -281,45 +288,55 @@
     tiny = pl.CostEstimate(flops=0, bytes_accessed=0, transcendentals=0)
     small = pl.CostEstimate(flops=2**20, bytes_accessed=2**20, transcendentals=2**14)
     q_chip = [over_chip(queries, step) for step in range(1, chips)]
-    moved = (cache_keys, cache_values, new_keys, new_values, queries)
-    pieces = 2
-    out = [jax.ShapeDtypeStruct(x.shape, x.dtype) for x in moved[:-1]]
-    out += [jax.ShapeDtypeStruct((tokens // pieces, heads, hd), BF16)] * pieces
-    out += [jax.ShapeDtypeStruct((8, hd), jnp.int32)]
-    k, v, nk, nv, *q_own, filled = pl.pallas_call(
-        functools.partial(load_kernel, pieces),
-        out_shape=out,
+    fresh_rows = (tokens * kv // heads, heads, hd)
+    moved = (cache_keys, cache_values, queries, new_keys.reshape(fresh_rows), new_values.reshape(fresh_rows))
+    m = tokens // 2
+    piece = jax.ShapeDtypeStruct((m + fresh_rows[0], heads, hd), BF16)
+    k, v, qk, qv, filled = pl.pallas_call(
+        load_kernel,
+        out_shape=[
+            jax.ShapeDtypeStruct(cache_keys.shape, BF16),
+            jax.ShapeDtypeStruct(cache_values.shape, BF16),
+            piece,
+            piece,
+            jax.ShapeDtypeStruct((8, hd), jnp.int32),
+        ],
         in_specs=[pl.BlockSpec(memory_space=pl.ANY)] + [HBM] * len(moved),
-        out_specs=[VMEM] * len(out),
-        scratch_shapes=[pltpu.SMEM((1,), jnp.int32), pltpu.SemaphoreType.DMA((len(out),))],
+        out_specs=[VMEM] * 5,
+        scratch_shapes=[pltpu.SMEM((1,), jnp.int32), pltpu.SemaphoreType.DMA((7,))],
         compiler_params=params(),
         cost_estimate=tiny,
         name="load",
     )(cache_len, *[pltpu.with_memory_space_constraint(x, pltpu.HBM) for x in moved])
-    q_core, nk_core, nv_core = [over_core(x) for x in q_own], over_core(nk), over_core(nv)
-    *q_core, nk_core, nv_core = lax.optimization_barrier((*q_core, nk_core, nv_core))
+    qk_core, qv_core = over_core(qk), over_core(qv)
     keys, values = call(
         "prepare",
-        prepare_kernel,
+        functools.partial(prepare_kernel, m),
         [jax.ShapeDtypeStruct((kv, slots, hd), BF16), jax.ShapeDtypeStruct((kv, slots, 2 * hd), BF16)],
-        (filled, k, v, nk),
+        (filled, k, v, qk),
         tiny,
     )
     shard = (keys, values)
-    fresh = call(
-        "fresh",
-        fresh_kernel,
-        [jax.ShapeDtypeStruct((kv, CORES * tokens, hd), BF16), jax.ShapeDtypeStruct((kv, CORES * tokens, 2 * hd), BF16)],
-        (nk, nv, nk_core, nv_core),
-        tiny,
-    )
-    *q_core, fresh_k, fresh_v = lax.optimization_barrier((*q_core, *fresh))
-    fresh = (fresh_k, fresh_v)
+    fresh = pl.pallas_call(
+        functools.partial(fresh_kernel, m),
+        out_shape=[
+            jax.ShapeDtypeStruct((kv, CORES * tokens, hd), BF16),
+            jax.ShapeDtypeStruct((kv, CORES * tokens, 2 * hd), BF16),
+        ],
+        in_specs=[VMEM] * 4,
+        out_specs=[VMEM] * 2,
+        scratch_shapes=[pltpu.VMEM((tokens * kv, hd), F32)],
+        compiler_params=params(),
+        cost_estimate=tiny,
+        name="fresh",
+    )(qk, qv, qk_core, qv_core)
+    qk_core, *fresh = lax.optimization_barrier((qk_core, *fresh))
 
     def attend_part(name, kernel, m, *args):
         return call(name, kernel, packed(m), args, cost(m))
 
-    sib = call("sibling", sibling_kernel, packed(tokens), (*q_core, *shard), tiny)
+    kernel = functools.partial(sibling_kernel, tokens)
+    sib = call("sibling", kernel, packed(tokens), (qk_core, qv_core, *shard), tiny)
     *q_chip, sib = lax.optimization_barrier((*q_chip, sib))
     q_diag = [over_core(q) for q in q_chip]
     far = []
@@ -349,9 +366,9 @@
             straight = straight_part(q_s, first, m) if i else early
             shape = extended(packed(m), len(shares) - 1 - i)
             both = call("chip_sum", functools.partial(chip_sum_kernel, group, m), shape, (diag[i], straight), tiny)
-            q_s, both, *q_own = lax.optimization_barrier((q_s, both, *q_own))
+            q_s, both, qk = lax.optimization_barrier((q_s, both, qk))
             far.append(over_chip(both, chips - step))
-    own = call("own", own_kernel, packed(tokens), (*q_own, *shard, *fresh), tiny)
+    own = call("own", functools.partial(own_kernel, tokens), packed(tokens), (qk, qv, *shard, *fresh), tiny)
     near = call(
         "near",
         functools.partial(near_kernel, group),
@@ -359,13 +376,23 @@
         (own, from_sib),
         tiny,
     )
-    return call(
-        "final",
-        functools.partial(final_kernel, group, shares),
-        jax.ShapeDtypeStruct(queries.shape, BF16),
-        (*near, *far),
-        small,
-    )
+    out = []
+    for i, (first, n_tokens) in enumerate(shares):
+        args = (*near, *far[i :: len(shares)], *out)
+        out = [
+            pl.pallas_call(
+                functools.partial(final_kernel, group, first, n_tokens),
+                out_shape=jax.ShapeDtypeStruct(queries.shape, BF16),
+                in_specs=[VMEM] * (len(args) - len(out)) + [HBM] * len(out),
+                out_specs=HBM,
+                scratch_shapes=[pltpu.VMEM((n_tokens, heads, hd), BF16), pltpu.SemaphoreType.DMA],
+                input_output_aliases={len(args) - 1: 0} if out else {},
+                compiler_params=params(),
+                cost_estimate=tiny,
+                name="final",
+            )(*args)
+        ]
+    return out[0]
 
 
 def solution(mesh):

time: 26 us -> 25.7 us (0.988)
  starting transfers between devices: 6.83 us -> 6.48 us
  waiting for transfers between devices: 1.53 us -> 1.24 us
    pallas_call x1 -> x4, Pallas kernels: 1.8 us -> 3.5 us  [the longest x1 1.79 us: per_device(): pl.pallas_call(load_kernel, out_shape=[jax.ShapeDtypeStruct(cache_keys.sh...]
    pallas_call x12 -> x10, Pallas kernels: 14.9 us -> 13.4 us  [call(): pl.pallas_call(kernel, out_shape=out, in_specs=[VMEM] * len(args), out_sp...]
    ppermute x3, waiting for transfers between devices: 1.51 us -> 0.7 us  [over_chip(): lax.ppermute(x, 'ctx', [(i, (i // CORES + step) % chips * CORES + i % COR...]
    ppermute x7 -> x5, starting transfers between devices: 2.08 us -> 1.55 us  [over_core(): return lax.ppermute(x, 'ctx', [(i, i ^ 1) for i in range(n)])]
    ppermute x7 -> x5, waiting for transfers between devices: 0.02 us -> 0.54 us  [over_core(): return lax.ppermute(x, 'ctx', [(i, i ^ 1) for i in range(n)])]
  transfers between devices with their start and end apart: 10 -> 8, of which waited for: 1 -> 3; matrix products, arithmetic and copies ran while one was open for 0% -> 0% of each run, Pallas kernels for 55% -> 57%
where the time goes in v5:
time: 25.7 us; the launch traced here: 25.5 us
  Pallas kernels  16.9 us (66%)
  starting transfers between devices  6.48 us (25%)
  waiting for transfers between devices  1.24 us (5%)
  between operations  0.91 us (4%)
    pallas_call x10, Pallas kernels, call(): pl.pallas_call(kernel, out_shape=out, in_specs=[VMEM] * len(args), out_sp...  13.4 us
    ppermute x3, starting transfers between devices, over_chip(): lax.ppermute(x, 'ctx', [(i, (i // CORES + step) % chips * CORES + i % COR...  4.93 us
    pallas_call x1, Pallas kernels, per_device(): pl.pallas_call(load_kernel, out_shape=[jax.ShapeDtypeStruct(cache_keys.sh...  1.79 us
    pallas_call x2, Pallas kernels, per_device(): pl.pallas_call(functools.partial(final_kernel, group, first, n_tokens), o...  1.65 us
    ppermute x5, starting transfers between devices, over_core(): return lax.ppermute(x, 'ctx', [(i, i ^ 1) for i in range(n)])  1.55 us
    ppermute x3, waiting for transfers between devices, over_chip(): lax.ppermute(x, 'ctx', [(i, (i // CORES + step) % chips * CORES + i % COR...  0.7 us
    ppermute x5, waiting for transfers between devices, over_core(): return lax.ppermute(x, 'ctx', [(i, i ^ 1) for i in range(n)])  0.54 us
  transfers between devices with their start and end apart: 8, of which 3 were waited for; matrix products, arithmetic and copies ran while one was open for 0% of the time, Pallas kernels for 57%

profile of v5, /device:TPU:0, one launch (start us, length us, event | category | flops | bytes accessed | tf_op | source)
XLA Modules:
  0.0 25.5 jit_solution(10766127246262198306)
XLA Ops:
  0.0 2.9 %collective-permute-start = (bf16[64,16,128]{2,1,0:T(8,128)(2,1)}, bf16[64,16,128]{2,1,0:T(8,128)(2,1)S(1)}, u32[]{:S(2)}, u32[]{:S(2)}) collective-permute-start(bf16[64,16,128]{2,1,0:T(8,128)(2,1)} %q.1), channel_id=1, source_target_pairs={{0,8},{4,12},{8,0},{12,4},{1,9},{5,13},{9,1},{13,5},{2,10},{6,14},... | collective-permute-start | bytes 786440 | tf_op jit(solution)/shard_map/ppermute | solution.py:267
  3.6 1.8 %load.1 = (bf16[2048,2,128]{2,1,0:T(2,128)(2,1)S(1)}, bf16[2048,2,128]{2,1,0:T(2,128)(2,1)S(1)}, bf16[40,16,128]{2,1,0:T(8,128)(2,1)S(1)}, bf16[40,16,128]{2,1,0:T(8,128)(2,1)S(1)}, s32[8,128]{1,0:T(8,128)S(1)}) custom-call(s32[1]{0:T(128)S(6)} %copy.9.length, bf16[2048,2,128]{2,1,0:T(2,128)(2,1)} %k.1, bf16[2048,2,128]{2,1,0:T(2,128)(2,1)} %v.1, ...), custom_call_target="tpu_custom_call" | custom-call | tf_op jit(solution)/shard_map/load/pallas_call | solution.py:295
  5.4 0.1 collective-permute-start.1
  5.5 0.5 %collective-permute-start.2 = (bf16[40,16,128]{2,1,0:T(8,128)(2,1)S(1)}, bf16[40,16,128]{2,1,0:T(8,128)(2,1)S(1)}, u32[]{:S(2)}, u32[]{:S(2)}) collective-permute-start(bf16[40,16,128]{2,1,0:T(8,128)(2,1)S(1)} %get-tuple-element.34.qv), channel_id=1, source_target_pairs={{0,4},{4,0},{8,12},{12,8},{1,5},{5,1},{9,13},{13,9},{2,6},{6,2},{1... | collective-permute-start | bytes 491528 | tf_op jit(solution)/shard_map/ppermute | solution.py:264
  6.0 0.6 %prepare.1 = (bf16[2,2048,128]{2,1,0:T(8,128)(2,1)S(1)}, bf16[2,2048,256]{2,1,0:T(8,128)(2,1)S(1)}) custom-call(s32[8,128]{1,0:T(8,128)S(1)} %get-tuple-element.38.filled, bf16[2048,2,128]{2,1,0:T(2,128)(2,1)S(1)} %get-tuple-element.39.k, bf16[2048,2,128]{2,1,0:T(2,128)(2,1)S(1)} %get-tuple-element.40.v, bf16[40,16,128]{2,1,0:T(8,128)(2,1)S(1)} %get-tuple-element.56.qk), custom_call_target="tpu_custom_call" | custom-call | tf_op jit(solution)/shard_map/prepare/pallas_call | solution.py:278
  6.5 0.3 %collective-permute-done.1.qk_core.qk = bf16[40,16,128]{2,1,0:T(8,128)(2,1)S(1)} collective-permute-done((bf16[40,16,128]{2,1,0:T(8,128)(2,1)S(1)}, bf16[40,16,128]{2,1,0:T(8,128)(2,1)S(1)}, u32[]{:S(2)}, u32[]{:S(2)}) %collective-permute-start.1) | collective-permute-done | bytes 163872 | tf_op jit(solution)/shard_map/ppermute | solution.py:264
  6.8 0.2 collective-permute-done.2.qv_core.qv
  7.1 0.1 fresh.1
  7.1 2.6 %sibling.1.refs_0_ = bf16[66,16,128]{2,1,0:T(8,128)(2,1)S(1)} custom-call(bf16[40,16,128]{2,1,0:T(8,128)(2,1)S(1)} %collective-permute-done.1.qk_core.qk, bf16[40,16,128]{2,1,0:T(8,128)(2,1)S(1)} %collective-permute-done.2.qv_core.qv, bf16[2,2048,128]{2,1,0:T(8,128)(2,1)S(1)} %get-tuple-element.41.keys, bf16[2,2048,256]{2,1,0:T(8,128)(2,1)S(1)} %get-tuple-element.42.values), custom_call_target="tpu_custom_call" | custom-call | tf_op jit(solution)/shard_map/sibling/pallas_call | solution.py:278
  9.8 0.0 collective-permute-done.q
  9.8 0.3 %collective-permute-start.3 = (bf16[64,16,128]{2,1,0:T(8,128)(2,1)S(1)}, bf16[64,16,128]{2,1,0:T(8,128)(2,1)S(1)}, u32[]{:S(2)}, u32[]{:S(2)}) collective-permute-start(bf16[64,16,128]{2,1,0:T(8,128)(2,1)S(1)} %collective-permute-done.q), channel_id=1, source_target_pairs={{0,4},{4,0},{8,12},{12,8},{1,5},{5,1},{9,13},{13,9},{2,6},{6,2},{1... | collective-permute-start | bytes 786440 | tf_op jit(solution)/shard_map/ppermute | solution.py:264
  10.1 1.7 %straight.2.b = bf16[33,16,128]{2,1,0:T(8,128)(2,1)S(1)} custom-call(bf16[64,16,128]{2,1,0:T(8,128)(2,1)S(1)} %collective-permute-done.q, bf16[2,2048,128]{2,1,0:T(8,128)(2,1)S(1)} %get-tuple-element.41.keys, bf16[2,2048,256]{2,1,0:T(8,128)(2,1)S(1)} %get-tuple-element.42.values, bf16[2,128,128]{2,1,0:T(8,128)(2,1)S(1)} %get-tuple-element.44.fresh_k, ...), custom_call_target="tpu_custom_call" | custom-call | flops 1073741824 | bytes 4194304 | tf_op jit(solution)/shard_map/straight/pallas_call | solution.py:278
  11.9 0.0 collective-permute-done.3.q
  11.9 1.6 %diagonal.2 = bf16[99,16,128]{2,1,0:T(8,128)(2,1)S(1)} custom-call(bf16[64,16,128]{2,1,0:T(8,128)(2,1)S(1)} %collective-permute-done.3.q, bf16[2,2048,128]{2,1,0:T(8,128)(2,1)S(1)} %get-tuple-element.41.keys, bf16[2,2048,256]{2,1,0:T(8,128)(2,1)S(1)} %get-tuple-element.42.values, bf16[66,16,128]{2,1,0:T(8,128)(2,1)S(1)} %sibling.1.refs_0_), custom_call_target="tpu_custom_call" | custom-call | flops 1073741824 | bytes 4194304 | tf_op jit(solution)/shard_map/diagonal/pallas_call | solution.py:278
  13.4 0.3 %collective-permute-start.4 = (bf16[99,16,128]{2,1,0:T(8,128)(2,1)S(1)}, bf16[99,16,128]{2,1,0:T(8,128)(2,1)S(1)}, u32[]{:S(2)}, u32[]{:S(2)}) collective-permute-start(bf16[99,16,128]{2,1,0:T(8,128)(2,1)S(1)} %diagonal.2), channel_id=1, source_target_pairs={{0,4},{4,0},{8,12},{12,8},{1,5},{5,1},{9,13},{13,9},{2,6},{6,2},{1... | collective-permute-start | bytes 1216520 | tf_op jit(solution)/shard_map/ppermute | solution.py:264
  13.7 1.5 %diagonal.3 = bf16[33,16,128]{2,1,0:T(8,128)(2,1)S(1)} custom-call(bf16[64,16,128]{2,1,0:T(8,128)(2,1)S(1)} %collective-permute-done.3.q, bf16[2,2048,128]{2,1,0:T(8,128)(2,1)S(1)} %get-tuple-element.41.keys, bf16[2,2048,256]{2,1,0:T(8,128)(2,1)S(1)} %get-tuple-element.42.values), custom_call_target="tpu_custom_call" | custom-call | flops 1073741824 | bytes 4194304 | tf_op jit(solution)/shard_map/diagonal/pallas_call | solution.py:278
  15.3 0.3 %collective-permute-start.5 = (bf16[33,16,128]{2,1,0:T(8,128)(2,1)S(1)}, bf16[33,16,128]{2,1,0:T(8,128)(2,1)S(1)}, u32[]{:S(2)}, u32[]{:S(2)}) collective-permute-start(bf16[33,16,128]{2,1,0:T(8,128)(2,1)S(1)} %diagonal.3), channel_id=1, source_target_pairs={{0,4},{4,0},{8,12},{12,8},{1,5},{5,1},{9,13},{13,9},{2,6},{6,2},{1... | collective-permute-start | bytes 405512 | tf_op jit(solution)/shard_map/ppermute | solution.py:264
  15.6 0.0 collective-permute-done.4.a.sib
  15.6 0.2 chip_sum.2
  15.8 1.0 %collective-permute-start.7 = (bf16[34,16,128]{2,1,0:T(8,128)(2,1)S(1)}, bf16[34,16,128]{2,1,0:T(8,128)(2,1)S(1)}, u32[]{:S(2)}, u32[]{:S(2)}) collective-permute-start(bf16[34,16,128]{2,1,0:T(8,128)(2,1)S(1)} %chip_sum.2), channel_id=1, source_target_pairs={{0,8},{4,12},{8,0},{12,4},{1,9},{5,13},{9,1},{13,5},{2,10},{6,14},... | collective-permute-start | bytes 417800 | tf_op jit(solution)/shard_map/ppermute | solution.py:267
  16.8 1.7 %straight.3.b = bf16[33,16,128]{2,1,0:T(8,128)(2,1)S(1)} custom-call(bf16[64,16,128]{2,1,0:T(8,128)(2,1)S(1)} %collective-permute-done.q, bf16[2,2048,128]{2,1,0:T(8,128)(2,1)S(1)} %get-tuple-element.41.keys, bf16[2,2048,256]{2,1,0:T(8,128)(2,1)S(1)} %get-tuple-element.42.values, bf16[2,128,128]{2,1,0:T(8,128)(2,1)S(1)} %get-tuple-element.44.fresh_k, ...), custom_call_target="tpu_custom_call" | custom-call | tf_op jit(solution)/shard_map/straight/pallas_call | solution.py:278
  18.5 0.0 collective-permute-done.5.a
  18.5 0.2 chip_sum.3
  18.7 1.0 %collective-permute-start.6 = (bf16[33,16,128]{2,1,0:T(8,128)(2,1)S(1)}, bf16[33,16,128]{2,1,0:T(8,128)(2,1)S(1)}, u32[]{:S(2)}, u32[]{:S(2)}) collective-permute-start(bf16[33,16,128]{2,1,0:T(8,128)(2,1)S(1)} %chip_sum.3), channel_id=1, source_target_pairs={{0,8},{4,12},{8,0},{12,4},{1,9},{5,13},{9,1},{13,5},{2,10},{6,14},... | collective-permute-start | bytes 405512 | tf_op jit(solution)/shard_map/ppermute | solution.py:267
  19.7 3.1 %own.1 = bf16[66,16,128]{2,1,0:T(8,128)(2,1)S(1)} custom-call(bf16[40,16,128]{2,1,0:T(8,128)(2,1)S(1)} %get-tuple-element.56.qk, bf16[40,16,128]{2,1,0:T(8,128)(2,1)S(1)} %get-tuple-element.34.qv, bf16[2,2048,128]{2,1,0:T(8,128)(2,1)S(1)} %get-tuple-element.41.keys, bf16[2,2048,256]{2,1,0:T(8,128)(2,1)S(1)} %get-tuple-element.42.values, ...), custom_call_target="tpu_custom_call" | custom-call | tf_op jit(solution)/shard_map/own/pallas_call | solution.py:278
  22.8 0.2 near.1
  23.0 0.0 collective-permute-done.7.refs_0_
  23.0 0.8 %final.2.refs_1_ = bf16[64,16,128]{2,1,0:T(8,128)(2,1)} custom-call(f32[64,16,128]{2,1,0:T(8,128)S(1)} %get-tuple-element.57.near, f32[8,128]{1,0:T(8,128)S(1)} %get-tuple-element.58.near_l, bf16[34,16,128]{2,1,0:T(8,128)(2,1)S(1)} %collective-permute-done.7.refs_0_), custom_call_target="tpu_custom_call" | custom-call | tf_op jit(solution)/shard_map/final/pallas_call | solution.py:383
  23.9 0.7 %collective-permute-done.6.refs_0_ = bf16[33,16,128]{2,1,0:T(8,128)(2,1)S(1)} collective-permute-done((bf16[33,16,128]{2,1,0:T(8,128)(2,1)S(1)}, bf16[33,16,128]{2,1,0:T(8,128)(2,1)S(1)}, u32[]{:S(2)}, u32[]{:S(2)}) %collective-permute-start.6) | collective-permute-done | bytes 135200 | tf_op jit(solution)/shard_map/ppermute | solution.py:267
  24.6 0.8 %final.3 = bf16[64,16,128]{2,1,0:T(8,128)(2,1)} custom-call(f32[64,16,128]{2,1,0:T(8,128)S(1)} %get-tuple-element.57.near, f32[8,128]{1,0:T(8,128)S(1)} %get-tuple-element.58.near_l, bf16[33,16,128]{2,1,0:T(8,128)(2,1)S(1)} %collective-permute-done.6.refs_0_, bf16[64,16,128]{2,1,0:T(8,128)(2,1)} %final.2.refs_1_), custom_call_target="tpu_custom_call", output_to_operand_aliasing={{}: (3, {})} | custom-call | tf_op jit(solution)/shard_map/final/pallas_call | solution.py:383
Async XLA Ops:
  0.0 9.8 %collective-permute-start = (bf16[64,16,128]{2,1,0:T(8,128)(2,1)}, bf16[64,16,128]{2,1,0:T(8,128)(2,1)S(1)}, u32[]{:S(2)}, u32[]{:S(2)}) collective-permute-start(bf16[64,16,128]{2,1,0:T(8,128)(2,1)} %q.1), channel_id=1, source_target_pairs={{0,8},{4,12},{8,0},{12,4},{1,9},{5,13},{9,1},{13,5},{2,10},{6,14},... | collective-permute-start | bytes 786440 | tf_op jit(solution)/shard_map/ppermute | solution.py:267
  5.4 1.5 %collective-permute-start.1 = (bf16[40,16,128]{2,1,0:T(8,128)(2,1)S(1)}, bf16[40,16,128]{2,1,0:T(8,128)(2,1)S(1)}, u32[]{:S(2)}, u32[]{:S(2)}) collective-permute-start(bf16[40,16,128]{2,1,0:T(8,128)(2,1)S(1)} %get-tuple-element.56.qk), channel_id=1, source_target_pairs={{0,4},{4,0},{8,12},{12,8},{1,5},{5,1},{9,13},{13,9},{2,6},{6,2},{1... | collective-permute-start | bytes 491528 | tf_op jit(solution)/shard_map/ppermute | solution.py:264
  5.5 1.6 %collective-permute-start.2 = (bf16[40,16,128]{2,1,0:T(8,128)(2,1)S(1)}, bf16[40,16,128]{2,1,0:T(8,128)(2,1)S(1)}, u32[]{:S(2)}, u32[]{:S(2)}) collective-permute-start(bf16[40,16,128]{2,1,0:T(8,128)(2,1)S(1)} %get-tuple-element.34.qv), channel_id=1, source_target_pairs={{0,4},{4,0},{8,12},{12,8},{1,5},{5,1},{9,13},{13,9},{2,6},{6,2},{1... | collective-permute-start | bytes 491528 | tf_op jit(solution)/shard_map/ppermute | solution.py:264
  9.8 2.1 %collective-permute-start.3 = (bf16[64,16,128]{2,1,0:T(8,128)(2,1)S(1)}, bf16[64,16,128]{2,1,0:T(8,128)(2,1)S(1)}, u32[]{:S(2)}, u32[]{:S(2)}) collective-permute-start(bf16[64,16,128]{2,1,0:T(8,128)(2,1)S(1)} %collective-permute-done.q), channel_id=1, source_target_pairs={{0,4},{4,0},{8,12},{12,8},{1,5},{5,1},{9,13},{13,9},{2,6},{6,2},{1... | collective-permute-start | bytes 786440 | tf_op jit(solution)/shard_map/ppermute | solution.py:264
  13.4 2.2 %collective-permute-start.4 = (bf16[99,16,128]{2,1,0:T(8,128)(2,1)S(1)}, bf16[99,16,128]{2,1,0:T(8,128)(2,1)S(1)}, u32[]{:S(2)}, u32[]{:S(2)}) collective-permute-start(bf16[99,16,128]{2,1,0:T(8,128)(2,1)S(1)} %diagonal.2), channel_id=1, source_target_pairs={{0,4},{4,0},{8,12},{12,8},{1,5},{5,1},{9,13},{13,9},{2,6},{6,2},{1... | collective-permute-start | bytes 1216520 | tf_op jit(solution)/shard_map/ppermute | solution.py:264
  15.3 3.2 %collective-permute-start.5 = (bf16[33,16,128]{2,1,0:T(8,128)(2,1)S(1)}, bf16[33,16,128]{2,1,0:T(8,128)(2,1)S(1)}, u32[]{:S(2)}, u32[]{:S(2)}) collective-permute-start(bf16[33,16,128]{2,1,0:T(8,128)(2,1)S(1)} %diagonal.3), channel_id=1, source_target_pairs={{0,4},{4,0},{8,12},{12,8},{1,5},{5,1},{9,13},{13,9},{2,6},{6,2},{1... | collective-permute-start | bytes 405512 | tf_op jit(solution)/shard_map/ppermute | solution.py:264
  15.8 7.2 %collective-permute-start.7 = (bf16[34,16,128]{2,1,0:T(8,128)(2,1)S(1)}, bf16[34,16,128]{2,1,0:T(8,128)(2,1)S(1)}, u32[]{:S(2)}, u32[]{:S(2)}) collective-permute-start(bf16[34,16,128]{2,1,0:T(8,128)(2,1)S(1)} %chip_sum.2), channel_id=1, source_target_pairs={{0,8},{4,12},{8,0},{12,4},{1,9},{5,13},{9,1},{13,5},{2,10},{6,14},... | collective-permute-start | bytes 417800 | tf_op jit(solution)/shard_map/ppermute | solution.py:267
  18.7 5.9 %collective-permute-start.6 = (bf16[33,16,128]{2,1,0:T(8,128)(2,1)S(1)}, bf16[33,16,128]{2,1,0:T(8,128)(2,1)S(1)}, u32[]{:S(2)}, u32[]{:S(2)}) collective-permute-start(bf16[33,16,128]{2,1,0:T(8,128)(2,1)S(1)} %chip_sum.3), channel_id=1, source_target_pairs={{0,8},{4,12},{8,0},{12,4},{1,9},{5,13},{9,1},{13,5},{2,10},{6,14},... | collective-permute-start | bytes 405512 | tf_op jit(solution)/shard_map/ppermute | solution.py:267

commit v6 on v5

v6 whole, which is shorter than its diff:
```python
import functools
import math

import jax
import jax.numpy as jnp
from jax import lax
from jax.experimental import pallas as pl
from jax.experimental.pallas import tpu as pltpu
from jax.sharding import PartitionSpec as P

NEG_FILL = -1e30
LOG2E = 1.4426950408889634
VMEM = pl.BlockSpec(memory_space=pltpu.VMEM)
SMEM = pl.BlockSpec(memory_space=pltpu.SMEM)
HBM = pl.BlockSpec(memory_space=pltpu.HBM)
F32 = jnp.float32
BF16 = jnp.bfloat16
NT = (((1,), (1,)), ((), ()))
CORES = 2


def params():
    return pltpu.CompilerParams(vmem_limit_bytes=36 * 2**20)


def pack_rows(wide):
    eye = lax.broadcasted_iota(jnp.int32, (128, 128), 0) == lax.broadcasted_iota(jnp.int32, (128, 128), 1)
    return jnp.concatenate(
        [
            jnp.sum(jnp.where(eye, wide[i * 128 : (i + 1) * 128], 0.0), axis=0, keepdims=True)
            for i in range(wide.shape[0] // 128)
        ],
        axis=0,
    )


def spread_rows(packed):
    return jnp.concatenate(
        [jnp.transpose(jnp.broadcast_to(packed[i : i + 1, :], (128, 128))) for i in range(packed.shape[0])], axis=0
    )


def load_kernel(k, v, q, nk, nv, k_out, v_out, q_out, new, sems):
    m = nk.shape[0]
    moves = [(k, k_out), (v, v_out), (q, q_out), (nk, new.at[0:m]), (nv, new.at[m:])]
    copies = [pltpu.make_async_copy(a, b, sems.at[i]) for i, (a, b) in enumerate(moves)]
    for c in copies[::-1]:
        c.start()
    for c in copies:
        c.wait()


def prepare_kernel(k, v, keys, values, at=0):
    slots, kv, hd = k.shape
    keys[:, at : at + slots] = jnp.swapaxes(k[...], 0, 1)
    values[:, at : at + slots, 0:hd] = jnp.swapaxes(v[...], 0, 1)
    values[:, at : at + slots, hd:] = jnp.ones((kv, slots, hd), BF16)


def exclude(count, at, slots, fill, keys, values):
    kv, _, hd = keys.shape
    cut = slice(at, at + slots)

    @pl.when(count < slots)
    def _():
        included = lax.broadcasted_iota(jnp.int32, (slots, hd), 0) < count
        for h in range(kv):
            keys[h, cut] = jnp.where(included, keys[h, cut].astype(F32), fill(h)).astype(BF16)
            values[h, cut, 0:hd] = jnp.where(included, values[h, cut, 0:hd].astype(F32), 0.0).astype(BF16)
            values[h, cut, hd:] = jnp.where(included, 1.0, 0.0).astype(BF16)


def own_shard_kernel(slots, length, new, _k, _v, keys, values):
    count = jnp.clip(length[0] - lax.axis_index("ctx") * slots, 0, slots)
    first_new = new[0].astype(F32)

    def fill(h):
        return jnp.where(count > 0, keys[h, 0:1, :].astype(F32), first_new[h : h + 1])

    exclude(count, 0, slots, fill, keys, values)


def other_shard_kernel(length, k, v, new, new_core, _k, _v, keys, values, rows):
    slots, kv, hd = k.shape
    prepare_kernel(k, v, keys, values, slots)
    place = lax.axis_index("ctx")
    low = place % CORES == 0
    m = new.shape[0] // 2
    tokens = rows.shape[0] // kv
    end = 2 * slots
    for j, out in enumerate((keys, values)):
        mine, other = [x[j * m : (j + 1) * m].astype(F32) for x in (new, new_core)]
        for i, x in enumerate((jnp.where(low, mine, other), jnp.where(low, other, mine))):
            rows[...] = x.reshape(tokens * kv, hd)
            first = end + i * tokens
            for h in range(kv):
                out[h, first : first + tokens, 0:hd] = rows[pl.ds(h, tokens, stride=kv), :].astype(BF16)
    values[:, end:, hd:] = jnp.ones((kv, CORES * tokens, hd), BF16)
    count = jnp.clip(length[0] - place * slots, 0, slots)
    other_count = jnp.clip(length[0] - (place ^ 1) * slots, 0, slots)

    def fill(h):
        own, other, new_key = [keys[h, i : i + 1, :].astype(F32) for i in (0, slots, end)]
        return jnp.where(other_count > 0, other, jnp.where(count > 0, own, new_key))

    exclude(other_count, slots, slots, fill, keys, values)

    @pl.when(count == 0)
    def _():
        for h in range(kv):
            keys[h, 0:slots] = jnp.broadcast_to(fill(h), (slots, hd)).astype(BF16)


def put_lse(ref, first, lse):
    heads = ref.shape[1]
    high = lse.astype(BF16).astype(F32)
    middle = (lse - high).astype(BF16).astype(F32)
    low = lse - high - middle
    extra = lse_rows(lse.shape[0], heads)
    rest = jnp.zeros((extra * heads - 3 * lse.shape[0], 128), F32)
    rows = jnp.concatenate([high, middle, low, rest], axis=0)
    ref[first : first + extra] = rows.astype(BF16).reshape(extra, heads, 128)


def lse_rows(n, heads):
    return -(-3 * n // heads)


def get_lse(ref, first):
    heads = ref.shape[1]
    n = first * heads // 128
    extra = lse_rows(n, heads)
    rows = ref[first : first + extra].astype(F32).reshape(extra * heads, 128)
    return rows[0:n] + rows[n : 2 * n] + rows[2 * n : 3 * n]


def packed_shape(tokens, heads, hd):
    return jax.ShapeDtypeStruct((tokens + lse_rows(tokens * heads // 128, heads), heads, hd), BF16)


def extended(shape, rows):
    return jax.ShapeDtypeStruct((shape.shape[0] + rows,) + shape.shape[1:], shape.dtype)


def attend(q_ref, keys, values, cuts, first, n, o_ref, causal=None):
    heads, hd = q_ref.shape[1:]
    kv = keys.shape[0]
    group = heads // kv
    rows = n * group
    scale = LOG2E / math.sqrt(hd)
    if causal is not None:
        count = cuts[-1].stop - cuts[-1].start
        token = causal + lax.broadcasted_iota(jnp.int32, (rows, count), 0) // group
        seen = token >= lax.broadcasted_iota(jnp.int32, (rows, count), 1)

    def scores(h):
        q = q_ref[first : first + n, h * group : (h + 1) * group, :].reshape(rows, hd)
        found = [lax.dot_general(q, keys[h, cut], NT, preferred_element_type=F32) for cut in cuts]
        if causal is not None:
            found[-1] = jnp.where(seen, found[-1], NEG_FILL)
        return found

    now = scores(0)
    lses = []
    for h in range(kv):
        later = scores(h + 1) if h + 1 < kv else None
        peak = functools.reduce(jnp.maximum, [jnp.max(s, axis=-1, keepdims=True) for s in now])
        weights = [jnp.exp2((s - peak) * scale) for s in now]
        if causal is not None:
            weights[-1] = jnp.where(seen, weights[-1], 0.0)
        out = None
        for w, cut in zip(weights, cuts):
            term = jnp.dot(w.astype(BF16), values[h, cut], preferred_element_type=F32)
            out = term if out is None else out + term
        total = out[:, hd:]
        floored = jnp.maximum(total, 1.0)
        o_ref[0:n, h * group : (h + 1) * group, :] = (out[:, 0:hd] / floored).astype(BF16).reshape(n, group, hd)
        lses.append(pack_rows(jnp.where(total > 0.0, peak * (1.0 / math.sqrt(hd)) + jnp.log(floored), NEG_FILL)))
        now = later
    put_lse(o_ref, n, jnp.concatenate(lses, axis=0))
    used = packed_shape(n, heads, hd).shape[0]
    if o_ref.shape[0] > used:
        o_ref[used:] = jnp.zeros((o_ref.shape[0] - used, heads, hd), BF16)


def blend(parts, group):
    tokens, heads, hd = parts[0][0].shape
    top = functools.reduce(jnp.maximum, [lse for _, lse in parts])
    scales = [jnp.exp(lse - top) for _, lse in parts]
    total = functools.reduce(jnp.add, scales)
    lse = jnp.where(top > 0.5 * NEG_FILL, top + jnp.log(total), NEG_FILL)
    inv = 1.0 / total
    n = tokens * group // 128
    outs = []
    for h in range(heads // group):
        norms = [
            norm[:, h * group : (h + 1) * group, :].reshape(tokens * group, hd).astype(F32) for norm, _ in parts
        ]
        acc = norms[0]
        for norm, s in zip(norms[1:], scales[1:]):
            acc = acc + (norm - norms[0]) * spread_rows((s * inv)[h * n : (h + 1) * n, :])
        outs.append(acc)
    return outs, lse


def own_near_kernel(slots, q, keys, values, o):
    attend(q, keys, values, [slice(0, slots)], 0, q.shape[0], o)


def own_rest_kernel(slots, length, q, keys, values, o):
    tokens = q.shape[0]
    place = lax.axis_index("ctx")
    other, fresh = slice(slots, 2 * slots), slice(2 * slots, keys.shape[1])
    filled = length[0] > (place ^ 1) * slots

    @pl.when(filled)
    def _():
        attend(q, keys, values, [other, fresh], 0, tokens, o, place % CORES * tokens)

    @pl.when(jnp.logical_not(filled))
    def _():
        attend(q, keys, values, [fresh], 0, tokens, o, place % CORES * tokens)


def visitor_kernel(owner, slots, first, n, q, keys, values, o):
    place = lax.axis_index("ctx")
    sees = owner(place) > place

    @pl.when(sees)
    def _():
        attend(q, keys, values, [slice(0, keys.shape[1])], first, n, o)

    @pl.when(jnp.logical_not(sees))
    def _():
        attend(q, keys, values, [slice(0, 2 * slots)], first, n, o)


def cut_lse(lse, kv, first, n, tokens):
    per = lse.shape[0] // kv
    a, b = first * per // tokens, (first + n) * per // tokens
    return jnp.concatenate([lse[h * per + a : h * per + b] for h in range(kv)], axis=0)


def near_kernel(group, near, rest, o, l):
    tokens, heads, hd = o.shape
    outs, lse = blend([(x[0:tokens], get_lse(x, tokens)) for x in (near, rest)], group)
    for h, x in enumerate(outs):
        o[:, h * group : (h + 1) * group, :] = x.reshape(tokens, group, hd)
    l[...] = lse


def final_kernel(group, first, n, near, near_l, *refs):
    *far, o, rows, sem = refs
    far = far[: len(far) - (first > 0)]
    tokens, heads, hd = o.shape
    lse = cut_lse(near_l[...], heads // group, first, n, tokens)
    parts = [(near[first : first + n], lse)] + [(x[0:n], get_lse(x, n)) for x in far]
    outs, _ = blend(parts, group)
    for h, x in enumerate(outs):
        rows[:, h * group : (h + 1) * group, :] = x.astype(BF16).reshape(n, group, hd)
    copy = pltpu.make_async_copy(rows, o.at[first : first + n], sem)
    copy.start()
    copy.wait()


def per_device(queries, new_keys, new_values, cache_keys, cache_values, cache_len):
    tokens, heads, hd = queries.shape
    slots, kv, _ = cache_keys.shape
    group = heads // kv
    n = lax.axis_size("ctx")
    chips = n // CORES
    unit = max(1, 128 // group)
    late = max(unit, tokens // 2 // unit * unit)
    shares = [(0, tokens - late), (tokens - late, late)]

    def over_core(x):
        return lax.ppermute(x, "ctx", [(i, i ^ 1) for i in range(n)])

    def over_chip(x, step):
        return lax.ppermute(x, "ctx", [(i, (i // CORES + step) % chips * CORES + i % CORES) for i in range(n)])

    def packed(m):
        return packed_shape(m, heads, hd)

    def cost(m):
        return pl.CostEstimate(
            flops=8 * m * heads * slots * hd, bytes_accessed=4 * 2**20, transcendentals=m * heads * slots
        )

    def call(name, kernel, out, args, estimate):
        return pl.pallas_call(
            kernel,
            out_shape=out,
            in_specs=[VMEM] * len(args),
            out_specs=jax.tree.map(lambda _: VMEM, out),
            compiler_params=params(),
            cost_estimate=estimate,
            name=name,
        )(*args)

    tiny = pl.CostEstimate(flops=0, bytes_accessed=0, transcendentals=0)
    small = pl.CostEstimate(flops=2**20, bytes_accessed=2**20, transcendentals=2**14)
    q_chip = [over_chip(queries, step) for step in range(1, chips)]
    k_core, v_core = over_core(cache_keys), over_core(cache_values)
    new_rows = (tokens * kv // heads, heads, hd)
    moved = (cache_keys, cache_values, queries, new_keys.reshape(new_rows), new_values.reshape(new_rows))
    out = [jax.ShapeDtypeStruct(x.shape, BF16) for x in moved[:3]]
    out.append(jax.ShapeDtypeStruct((2 * new_rows[0], heads, hd), BF16))
    k, v, q_own, new = pl.pallas_call(
        load_kernel,
        out_shape=out,
        in_specs=[HBM] * len(moved),
        out_specs=[VMEM] * len(out),
        scratch_shapes=[pltpu.SemaphoreType.DMA((len(moved),))],
        compiler_params=params(),
        cost_estimate=tiny,
        name="load",
    )(*[pltpu.with_memory_space_constraint(x, pltpu.HBM) for x in moved])
    new_core = over_core(new)
    places = 2 * slots + CORES * tokens
    both = [jax.ShapeDtypeStruct((kv, places, hd), BF16), jax.ShapeDtypeStruct((kv, places, 2 * hd), BF16)]
    keys, values = call("prepare", prepare_kernel, both, (k, v), tiny)
    keys, values = pl.pallas_call(
        functools.partial(own_shard_kernel, slots),
        out_shape=both,
        in_specs=[SMEM] + [VMEM] * 3,
        out_specs=[VMEM] * 2,
        input_output_aliases={2: 0, 3: 1},
        compiler_params=params(),
        cost_estimate=tiny,
        name="own_shard",
    )(cache_len, new, keys, values)
    kernel = functools.partial(own_near_kernel, slots)
    own_near = call("own_near", kernel, packed(tokens), (q_own, keys, values), tiny)
    k_core, v_core, own_near = lax.optimization_barrier((k_core, v_core, own_near))
    keys, values = pl.pallas_call(
        other_shard_kernel,
        out_shape=both,
        in_specs=[SMEM] + [VMEM] * 6,
        out_specs=[VMEM] * 2,
        scratch_shapes=[pltpu.VMEM((tokens * kv, hd), F32)],
        input_output_aliases={5: 0, 6: 1},
        compiler_params=params(),
        cost_estimate=tiny,
        name="other_shard",
    )(cache_len, k_core, v_core, new, new_core, keys, values)
    far = []
    for step in range(1, chips):
        def owner(i, step=step):
            return (i // CORES - step + chips) % chips * CORES + i % CORES

        q = q_chip[step - 1]
        for i, (first, m) in enumerate(shares):
            kernel = functools.partial(visitor_kernel, owner, slots, first, m)
            shape = extended(packed(m), len(shares) - 1 - i)
            part = call("visitor", kernel, shape, (q, keys, values), tiny if i else cost(m))
            q, q_own, part = lax.optimization_barrier((q, q_own, part))
            far.append(over_chip(part, chips - step))
    own_rest = pl.pallas_call(
        functools.partial(own_rest_kernel, slots),
        out_shape=packed(tokens),
        in_specs=[SMEM] + [VMEM] * 3,
        out_specs=VMEM,
        compiler_params=params(),
        cost_estimate=tiny,
        name="own_rest",
    )(cache_len, q_own, keys, values)
    near = call(
        "near",
        functools.partial(near_kernel, group),
        [jax.ShapeDtypeStruct(queries.shape, F32), jax.ShapeDtypeStruct((tokens * heads // 128, 128), F32)],
        (own_near, own_rest),
        tiny,
    )
    out = []
    for i, (first, n_tokens) in enumerate(shares):
        args = (*near, *far[i :: len(shares)], *out)
        out = [
            pl.pallas_call(
                functools.partial(final_kernel, group, first, n_tokens),
                out_shape=jax.ShapeDtypeStruct(queries.shape, BF16),
                in_specs=[VMEM] * (len(args) - len(out)) + [HBM] * len(out),
                out_specs=HBM,
                scratch_shapes=[pltpu.VMEM((n_tokens, heads, hd), BF16), pltpu.SemaphoreType.DMA],
                input_output_aliases={len(args) - 1: 0} if out else {},
                compiler_params=params(),
                cost_estimate=tiny,
                name="final",
            )(*args)
        ]
    return out[0]


def solution(mesh):
    spec = P(("conv", "ctx"), "head", None)
    return jax.shard_map(
        per_device,
        mesh=mesh,
        in_specs=(spec,) * 5 + (P("conv"),),
        out_specs=spec,
        check_vma=False,
    )
```

time: 25.7 us -> 23.5 us (0.914)
  Pallas kernels: 16.9 us -> 15.7 us
  starting transfers between devices: 6.48 us -> 5.53 us
    pallas_call x10 -> x5, Pallas kernels: 13.4 us -> 8.71 us  [call(): pl.pallas_call(kernel, out_shape=out, in_specs=[VMEM] * len(args), out_sp...]
    pallas_call x2 -> x4, Pallas kernels: 1.85 us -> 5.33 us  [the longest x1 2.99 us: per_device(): pl.pallas_call(functools.partial(own_rest_kernel, slots), out_shape=packe...]
    ppermute x5 -> x3, starting transfers between devices: 1.55 us -> 0.58 us  [over_core(): return lax.ppermute(x, 'ctx', [(i, i ^ 1) for i in range(n)])]
    ppermute x5 -> x3, waiting for transfers between devices: 0.54 us -> 0.01 us  [over_core(): return lax.ppermute(x, 'ctx', [(i, i ^ 1) for i in range(n)])]
    ppermute x3, waiting for transfers between devices: 0.7 us -> 1.19 us  [over_chip(): lax.ppermute(x, 'ctx', [(i, (i // CORES + step) % chips * CORES + i % COR...]
  transfers between devices with their start and end apart: 8 -> 6, of which waited for: 3 -> 2; matrix products, arithmetic and copies ran while one was open for 0% -> 0% of each run, Pallas kernels for 57% -> 52%
where the time goes in v6:
time: 23.5 us; the launch traced here: 23.3 us
  Pallas kernels  15.7 us (67%)
  starting transfers between devices  5.53 us (24%)
  waiting for transfers between devices  1.2 us (5%)
  between operations  0.92 us (4%)
    pallas_call x5, Pallas kernels, call(): pl.pallas_call(kernel, out_shape=out, in_specs=[VMEM] * len(args), out_sp...  8.71 us
    ppermute x3, starting transfers between devices, over_chip(): lax.ppermute(x, 'ctx', [(i, (i // CORES + step) % chips * CORES + i % COR...  4.95 us
    pallas_call x1, Pallas kernels, per_device(): pl.pallas_call(functools.partial(own_rest_kernel, slots), out_shape=packe...  2.99 us
    pallas_call x1, Pallas kernels, per_device(): pl.pallas_call(load_kernel, out_shape=out, in_specs=[HBM] * len(moved), o...  1.71 us
    pallas_call x2, Pallas kernels, per_device(): pl.pallas_call(functools.partial(final_kernel, group, first, n_tokens), o...  1.65 us
    ppermute x3, waiting for transfers between devices, over_chip(): lax.ppermute(x, 'ctx', [(i, (i // CORES + step) % chips * CORES + i % COR...  1.19 us
    pallas_call x1, Pallas kernels, per_device(): pl.pallas_call(other_shard_kernel, out_shape=both, in_specs=[SMEM] + [VME...  0.62 us
    ppermute x3, starting transfers between devices, over_core(): return lax.ppermute(x, 'ctx', [(i, i ^ 1) for i in range(n)])  0.58 us
  transfers between devices with their start and end apart: 6, of which 2 were waited for; matrix products, arithmetic and copies ran while one was open for 0% of the time, Pallas kernels for 52%

profile of v6, /device:TPU:0, one launch (start us, length us, event | category | flops | bytes accessed | tf_op | source)
XLA Modules:
  0.0 23.3 jit_solution(4324221675540509595)
XLA Ops:
  0.0 0.5 %collective-permute-start = (bf16[2048,2,128]{2,1,0:T(2,128)(2,1)}, bf16[2048,2,128]{2,1,0:T(2,128)(2,1)S(1)}, u32[]{:S(2)}, u32[]{:S(2)}) collective-permute-start(bf16[2048,2,128]{2,1,0:T(2,128)(2,1)} %k.1), channel_id=1, source_target_pairs={{0,4},{4,0},{8,12},{12,8},{1,5},{5,1},{9,13},{13,9},{2,6},{6,2},{1... | collective-permute-start | bytes 3145736 | tf_op jit(solution)/shard_map/ppermute | solution.py:277
  0.5 0.1 collective-permute-start.1
  0.5 2.9 %collective-permute-start.2 = (bf16[64,16,128]{2,1,0:T(8,128)(2,1)}, bf16[64,16,128]{2,1,0:T(8,128)(2,1)S(1)}, u32[]{:S(2)}, u32[]{:S(2)}) collective-permute-start(bf16[64,16,128]{2,1,0:T(8,128)(2,1)} %q.1), channel_id=1, source_target_pairs={{0,8},{4,12},{8,0},{12,4},{1,9},{5,13},{9,1},{13,5},{2,10},{6,14},... | collective-permute-start | bytes 786440 | tf_op jit(solution)/shard_map/ppermute | solution.py:280
  3.5 1.7 %load.1 = (bf16[2048,2,128]{2,1,0:T(2,128)(2,1)S(1)}, bf16[2048,2,128]{2,1,0:T(2,128)(2,1)S(1)}, bf16[64,16,128]{2,1,0:T(8,128)(2,1)S(1)}, bf16[16,16,128]{2,1,0:T(8,128)(2,1)S(1)}) custom-call(bf16[2048,2,128]{2,1,0:T(2,128)(2,1)} %k.1, bf16[2048,2,128]{2,1,0:T(2,128)(2,1)} %v.1, bf16[64,16,128]{2,1,0:T(8,128)(2,1)} %q.1, bf16[8,16,128]{2,1,0:T(8,128)(2,1)} %bitcast.2, ...), custom_call_target="tpu_custom_call" | custom-call | tf_op jit(solution)/shard_map/load/pallas_call | solution.py:309
  5.2 0.1 collective-permute-start.3
  5.9 0.5 %prepare.1 = (bf16[2,4224,128]{2,1,0:T(8,128)(2,1)S(1)}, bf16[2,4224,256]{2,1,0:T(8,128)(2,1)S(1)}) custom-call(bf16[2048,2,128]{2,1,0:T(2,128)(2,1)S(1)} %get-tuple-element.27.k, bf16[2048,2,128]{2,1,0:T(2,128)(2,1)S(1)} %get-tuple-element.28.v), custom_call_target="tpu_custom_call" | custom-call | tf_op jit(solution)/shard_map/prepare/pallas_call | solution.py:291
  6.4 2.6 %own_near.1.near = bf16[66,16,128]{2,1,0:T(8,128)(2,1)S(1)} custom-call(bf16[64,16,128]{2,1,0:T(8,128)(2,1)S(1)} %get-tuple-element.40.q, bf16[2,4224,128]{2,1,0:T(8,128)(2,1)S(1)} %get-tuple-element.31.keys._k, bf16[2,4224,256]{2,1,0:T(8,128)(2,1)S(1)} %get-tuple-element.32.values._v), custom_call_target="tpu_custom_call" | custom-call | tf_op jit(solution)/shard_map/own_near/pallas_call | solution.py:291
  8.9 0.0 collective-permute-done.k
  8.9 0.0 collective-permute-done.1.v
  9.0 0.0 collective-permute-done.3.new_core
  9.0 0.6 %other_shard.1 = (bf16[2,4224,128]{2,1,0:T(8,128)(2,1)S(1)}, bf16[2,4224,256]{2,1,0:T(8,128)(2,1)S(1)}) custom-call(s32[1]{0:T(128)S(6)} %copy.17.length, bf16[2048,2,128]{2,1,0:T(2,128)(2,1)S(1)} %collective-permute-done.k, bf16[2048,2,128]{2,1,0:T(2,128)(2,1)S(1)} %collective-permute-done.1.v, ...), custom_call_target="tpu_custom_call", output_to_operand_aliasing={{0}: (5, {}), {1}: (6, {})} | custom-call | tf_op jit(solution)/shard_map/other_shard/pallas_call | solution.py:336
  9.6 0.5 %collective-permute-done.2.q = bf16[64,16,128]{2,1,0:T(8,128)(2,1)S(1)} collective-permute-done((bf16[64,16,128]{2,1,0:T(8,128)(2,1)}, bf16[64,16,128]{2,1,0:T(8,128)(2,1)S(1)}, u32[]{:S(2)}, u32[]{:S(2)}) %collective-permute-start.2) | collective-permute-done | bytes 262176 | tf_op jit(solution)/shard_map/ppermute | solution.py:280
  10.1 2.7 %visitor.2 = bf16[34,16,128]{2,1,0:T(8,128)(2,1)S(1)} custom-call(bf16[64,16,128]{2,1,0:T(8,128)(2,1)S(1)} %collective-permute-done.2.q, bf16[2,4224,128]{2,1,0:T(8,128)(2,1)S(1)} %get-tuple-element.36.keys, bf16[2,4224,256]{2,1,0:T(8,128)(2,1)S(1)} %get-tuple-element.37.values), custom_call_target="tpu_custom_call" | custom-call | flops 1073741824 | bytes 4194304 | tf_op jit(solution)/shard_map/visitor/pallas_call | solution.py:291
  12.9 1.7 %collective-permute-start.5 = (bf16[34,16,128]{2,1,0:T(8,128)(2,1)S(1)}, bf16[34,16,128]{2,1,0:T(8,128)(2,1)S(1)}, u32[]{:S(2)}, u32[]{:S(2)}) collective-permute-start(bf16[34,16,128]{2,1,0:T(8,128)(2,1)S(1)} %visitor.2), channel_id=1, source_target_pairs={{0,8},{4,12},{8,0},{12,4},{1,9},{5,13},{9,1},{13,5},{2,10},{6,14},... | collective-permute-start | bytes 417800 | tf_op jit(solution)/shard_map/ppermute | solution.py:280
  14.5 2.7 %visitor.3 = bf16[33,16,128]{2,1,0:T(8,128)(2,1)S(1)} custom-call(bf16[64,16,128]{2,1,0:T(8,128)(2,1)S(1)} %collective-permute-done.2.q, bf16[2,4224,128]{2,1,0:T(8,128)(2,1)S(1)} %get-tuple-element.36.keys, bf16[2,4224,256]{2,1,0:T(8,128)(2,1)S(1)} %get-tuple-element.37.values), custom_call_target="tpu_custom_call" | custom-call | tf_op jit(solution)/shard_map/visitor/pallas_call | solution.py:291
  17.3 0.4 %collective-permute-start.4 = (bf16[33,16,128]{2,1,0:T(8,128)(2,1)S(1)}, bf16[33,16,128]{2,1,0:T(8,128)(2,1)S(1)}, u32[]{:S(2)}, u32[]{:S(2)}) collective-permute-start(bf16[33,16,128]{2,1,0:T(8,128)(2,1)S(1)} %visitor.3), channel_id=1, source_target_pairs={{0,8},{4,12},{8,0},{12,4},{1,9},{5,13},{9,1},{13,5},{2,10},{6,14},... | collective-permute-start | bytes 405512 | tf_op jit(solution)/shard_map/ppermute | solution.py:280
  17.6 3.0 %own_rest.1.rest = bf16[66,16,128]{2,1,0:T(8,128)(2,1)S(1)} custom-call(s32[1]{0:T(128)S(6)} %copy.17.length, bf16[64,16,128]{2,1,0:T(8,128)(2,1)S(1)} %get-tuple-element.40.q, bf16[2,4224,128]{2,1,0:T(8,128)(2,1)S(1)} %get-tuple-element.36.keys, bf16[2,4224,256]{2,1,0:T(8,128)(2,1)S(1)} %get-tuple-element.37.values), custom_call_target="tpu_custom_call" | custom-call | tf_op jit(solution)/shard_map/own_rest/pallas_call | solution.py:359
  20.6 0.2 near.1
  20.9 0.0 collective-permute-done.5.refs_0_
  20.9 0.8 %final.2.refs_1_ = bf16[64,16,128]{2,1,0:T(8,128)(2,1)} custom-call(f32[64,16,128]{2,1,0:T(8,128)S(1)} %get-tuple-element.41.near, f32[8,128]{1,0:T(8,128)S(1)} %get-tuple-element.42.near_l, bf16[34,16,128]{2,1,0:T(8,128)(2,1)S(1)} %collective-permute-done.5.refs_0_), custom_call_target="tpu_custom_call" | custom-call | tf_op jit(solution)/shard_map/final/pallas_call | solution.py:379
  21.7 0.7 %collective-permute-done.4.refs_0_ = bf16[33,16,128]{2,1,0:T(8,128)(2,1)S(1)} collective-permute-done((bf16[33,16,128]{2,1,0:T(8,128)(2,1)S(1)}, bf16[33,16,128]{2,1,0:T(8,128)(2,1)S(1)}, u32[]{:S(2)}, u32[]{:S(2)}) %collective-permute-start.4) | collective-permute-done | bytes 135200 | tf_op jit(solution)/shard_map/ppermute | solution.py:280
  22.4 0.8 %final.3 = bf16[64,16,128]{2,1,0:T(8,128)(2,1)} custom-call(f32[64,16,128]{2,1,0:T(8,128)S(1)} %get-tuple-element.41.near, f32[8,128]{1,0:T(8,128)S(1)} %get-tuple-element.42.near_l, bf16[33,16,128]{2,1,0:T(8,128)(2,1)S(1)} %collective-permute-done.4.refs_0_, bf16[64,16,128]{2,1,0:T(8,128)(2,1)} %final.2.refs_1_), custom_call_target="tpu_custom_call", output_to_operand_aliasing={{}: (3, {})} | custom-call | tf_op jit(solution)/shard_map/final/pallas_call | solution.py:379
  (1 shorter events, 0.0 us)
Async XLA Ops:
  0.0 8.9 %collective-permute-start = (bf16[2048,2,128]{2,1,0:T(2,128)(2,1)}, bf16[2048,2,128]{2,1,0:T(2,128)(2,1)S(1)}, u32[]{:S(2)}, u32[]{:S(2)}) collective-permute-start(bf16[2048,2,128]{2,1,0:T(2,128)(2,1)} %k.1), channel_id=1, source_target_pairs={{0,4},{4,0},{8,12},{12,8},{1,5},{5,1},{9,13},{13,9},{2,6},{6,2},{1... | collective-permute-start | bytes 3145736 | tf_op jit(solution)/shard_map/ppermute | solution.py:277
  0.5 8.5 %collective-permute-start.1 = (bf16[2048,2,128]{2,1,0:T(2,128)(2,1)}, bf16[2048,2,128]{2,1,0:T(2,128)(2,1)S(1)}, u32[]{:S(2)}, u32[]{:S(2)}) collective-permute-start(bf16[2048,2,128]{2,1,0:T(2,128)(2,1)} %v.1), channel_id=1, source_target_pairs={{0,4},{4,0},{8,12},{12,8},{1,5},{5,1},{9,13},{13,9},{2,6},{6,2},{1... | collective-permute-start | bytes 3145736 | tf_op jit(solution)/shard_map/ppermute | solution.py:277
  0.5 9.6 %collective-permute-start.2 = (bf16[64,16,128]{2,1,0:T(8,128)(2,1)}, bf16[64,16,128]{2,1,0:T(8,128)(2,1)S(1)}, u32[]{:S(2)}, u32[]{:S(2)}) collective-permute-start(bf16[64,16,128]{2,1,0:T(8,128)(2,1)} %q.1), channel_id=1, source_target_pairs={{0,8},{4,12},{8,0},{12,4},{1,9},{5,13},{9,1},{13,5},{2,10},{6,14},... | collective-permute-start | bytes 786440 | tf_op jit(solution)/shard_map/ppermute | solution.py:280
  5.2 3.8 %collective-permute-start.3 = (bf16[16,16,128]{2,1,0:T(8,128)(2,1)S(1)}, bf16[16,16,128]{2,1,0:T(8,128)(2,1)S(1)}, u32[]{:S(2)}, u32[]{:S(2)}) collective-permute-start(bf16[16,16,128]{2,1,0:T(8,128)(2,1)S(1)} %get-tuple-element.26.new), channel_id=1, source_target_pairs={{0,4},{4,0},{8,12},{12,8},{1,5},{5,1},{9,13},{13,9},{2,6},{6,2},{1... | collective-permute-start | bytes 196616 | tf_op jit(solution)/shard_map/ppermute | solution.py:277
  12.9 8.0 %collective-permute-start.5 = (bf16[34,16,128]{2,1,0:T(8,128)(2,1)S(1)}, bf16[34,16,128]{2,1,0:T(8,128)(2,1)S(1)}, u32[]{:S(2)}, u32[]{:S(2)}) collective-permute-start(bf16[34,16,128]{2,1,0:T(8,128)(2,1)S(1)} %visitor.2), channel_id=1, source_target_pairs={{0,8},{4,12},{8,0},{12,4},{1,9},{5,13},{9,1},{13,5},{2,10},{6,14},... | collective-permute-start | bytes 417800 | tf_op jit(solution)/shard_map/ppermute | solution.py:280
  17.3 5.1 %collective-permute-start.4 = (bf16[33,16,128]{2,1,0:T(8,128)(2,1)S(1)}, bf16[33,16,128]{2,1,0:T(8,128)(2,1)S(1)}, u32[]{:S(2)}, u32[]{:S(2)}) collective-permute-start(bf16[33,16,128]{2,1,0:T(8,128)(2,1)S(1)} %visitor.3), channel_id=1, source_target_pairs={{0,8},{4,12},{8,0},{12,4},{1,9},{5,13},{9,1},{13,5},{2,10},{6,14},... | collective-permute-start | bytes 405512 | tf_op jit(solution)/shard_map/ppermute | solution.py:280

commit v7 on v6

--- a/solution.py
+++ b/solution.py
@@ -301,7 +301,6 @@
     tiny = pl.CostEstimate(flops=0, bytes_accessed=0, transcendentals=0)
     small = pl.CostEstimate(flops=2**20, bytes_accessed=2**20, transcendentals=2**14)
     q_chip = [over_chip(queries, step) for step in range(1, chips)]
-    k_core, v_core = over_core(cache_keys), over_core(cache_values)
     new_rows = (tokens * kv // heads, heads, hd)
     moved = (cache_keys, cache_values, queries, new_keys.reshape(new_rows), new_values.reshape(new_rows))
     out = [jax.ShapeDtypeStruct(x.shape, BF16) for x in moved[:3]]
@@ -316,6 +315,7 @@
         cost_estimate=tiny,
         name="load",
     )(*[pltpu.with_memory_space_constraint(x, pltpu.HBM) for x in moved])
+    k_core, v_core = over_core(k), over_core(v)
     new_core = over_core(new)
     places = 2 * slots + CORES * tokens
     both = [jax.ShapeDtypeStruct((kv, places, hd), BF16), jax.ShapeDtypeStruct((kv, places, 2 * hd), BF16)]
@@ -331,7 +331,7 @@
         name="own_shard",
     )(cache_len, new, keys, values)
     kernel = functools.partial(own_near_kernel, slots)
-    own_near = call("own_near", kernel, packed(tokens), (q_own, keys, values), tiny)
+    own_near = call("own_near", kernel, packed(tokens), (q_own, keys, values), cost(tokens * 50))
     k_core, v_core, own_near = lax.optimization_barrier((k_core, v_core, own_near))
     keys, values = pl.pallas_call(
         other_shard_kernel,

time: 23.5 us -> 22.8 us (0.970)
  waiting for transfers between devices: 1.2 us -> 0.44 us
    ppermute x3, waiting for transfers between devices: 1.19 us -> 0.43 us  [over_chip(): lax.ppermute(x, 'ctx', [(i, (i // CORES + step) % chips * CORES + i % COR...]
  transfers between devices with their start and end apart: 6 -> 6, of which waited for: 2 -> 1; matrix products, arithmetic and copies ran while one was open for 0% -> 0% of each run, Pallas kernels for 52% -> 53%
where the time goes in v7:
time: 22.8 us; the launch traced here: 22.7 us
  Pallas kernels  15.7 us (69%)
  starting transfers between devices  5.6 us (25%)
  between operations  0.92 us (4%)
  waiting for transfers between devices  0.44 us (2%)
    pallas_call x5, Pallas kernels, call(): pl.pallas_call(kernel, out_shape=out, in_specs=[VMEM] * len(args), out_sp...  8.73 us
    ppermute x3, starting transfers between devices, over_chip(): lax.ppermute(x, 'ctx', [(i, (i // CORES + step) % chips * CORES + i % COR...  4.95 us
    pallas_call x1, Pallas kernels, per_device(): pl.pallas_call(functools.partial(own_rest_kernel, slots), out_shape=packe...  2.99 us
    pallas_call x1, Pallas kernels, per_device(): pl.pallas_call(load_kernel, out_shape=out, in_specs=[HBM] * len(moved), o...  1.71 us
    pallas_call x2, Pallas kernels, per_device(): pl.pallas_call(functools.partial(final_kernel, group, first, n_tokens), o...  1.65 us
    ppermute x3, starting transfers between devices, over_core(): return lax.ppermute(x, 'ctx', [(i, i ^ 1) for i in range(n)])  0.65 us
    pallas_call x1, Pallas kernels, per_device(): pl.pallas_call(other_shard_kernel, out_shape=both, in_specs=[SMEM] + [VME...  0.62 us
  transfers between devices with their start and end apart: 6, of which 1 were waited for; matrix products, arithmetic and copies ran while one was open for 0% of the time, Pallas kernels for 53%

profile of v7, /device:TPU:0, one launch (start us, length us, event | category | flops | bytes accessed | tf_op | source)
XLA Modules:
  0.0 22.7 jit_solution(10078335905767222236)
XLA Ops:
  0.0 2.9 %collective-permute-start.2 = (bf16[64,16,128]{2,1,0:T(8,128)(2,1)}, bf16[64,16,128]{2,1,0:T(8,128)(2,1)S(1)}, u32[]{:S(2)}, u32[]{:S(2)}) collective-permute-start(bf16[64,16,128]{2,1,0:T(8,128)(2,1)} %q.1), channel_id=1, source_target_pairs={{0,8},{4,12},{8,0},{12,4},{1,9},{5,13},{9,1},{13,5},{2,10},{6,14},... | collective-permute-start | bytes 786440 | tf_op jit(solution)/shard_map/ppermute | solution.py:280
  2.9 1.7 %load.1 = (bf16[2048,2,128]{2,1,0:T(2,128)(2,1)S(1)}, bf16[2048,2,128]{2,1,0:T(2,128)(2,1)S(1)}, bf16[64,16,128]{2,1,0:T(8,128)(2,1)S(1)}, bf16[16,16,128]{2,1,0:T(8,128)(2,1)S(1)}) custom-call(bf16[2048,2,128]{2,1,0:T(2,128)(2,1)} %k.1, bf16[2048,2,128]{2,1,0:T(2,128)(2,1)} %v.1, bf16[64,16,128]{2,1,0:T(8,128)(2,1)} %q.1, bf16[8,16,128]{2,1,0:T(8,128)(2,1)} %bitcast.2, ...), custom_call_target="tpu_custom_call" | custom-call | tf_op jit(solution)/shard_map/load/pallas_call | solution.py:308
  4.7 0.1 collective-permute-start
  4.7 0.5 %collective-permute-start.1 = (bf16[2048,2,128]{2,1,0:T(2,128)(2,1)S(1)}, bf16[2048,2,128]{2,1,0:T(2,128)(2,1)S(1)}, u32[]{:S(2)}, u32[]{:S(2)}) collective-permute-start(bf16[2048,2,128]{2,1,0:T(2,128)(2,1)S(1)} %get-tuple-element.26.v), channel_id=1, source_target_pairs={{0,4},{4,0},{8,12},{12,8},{1,5},{5,1},{9,13},{13,9},{2,6},{6,2},{1... | collective-permute-start | bytes 3145736 | tf_op jit(solution)/shard_map/ppermute | solution.py:277
  5.2 0.1 collective-permute-start.3
  5.3 0.4 %prepare.1 = (bf16[2,4224,128]{2,1,0:T(8,128)(2,1)S(1)}, bf16[2,4224,256]{2,1,0:T(8,128)(2,1)S(1)}) custom-call(bf16[2048,2,128]{2,1,0:T(2,128)(2,1)S(1)} %get-tuple-element.25.k, bf16[2048,2,128]{2,1,0:T(2,128)(2,1)S(1)} %get-tuple-element.26.v), custom_call_target="tpu_custom_call" | custom-call | tf_op jit(solution)/shard_map/prepare/pallas_call | solution.py:291
  6.4 2.6 %own_near.1.near = bf16[66,16,128]{2,1,0:T(8,128)(2,1)S(1)} custom-call(bf16[64,16,128]{2,1,0:T(8,128)(2,1)S(1)} %get-tuple-element.40.q, bf16[2,4224,128]{2,1,0:T(8,128)(2,1)S(1)} %get-tuple-element.31.keys._k, bf16[2,4224,256]{2,1,0:T(8,128)(2,1)S(1)} %get-tuple-element.32.values._v), custom_call_target="tpu_custom_call" | custom-call | flops 107374182400 | bytes 4194304 | tf_op jit(solution)/shard_map/own_near/pallas_call | solution.py:291
  9.0 0.0 collective-permute-done.k
  9.0 0.0 collective-permute-done.1.v
  9.0 0.0 collective-permute-done.3.new_core
  9.0 0.6 %other_shard.1 = (bf16[2,4224,128]{2,1,0:T(8,128)(2,1)S(1)}, bf16[2,4224,256]{2,1,0:T(8,128)(2,1)S(1)}) custom-call(s32[1]{0:T(128)S(6)} %copy.17.length, bf16[2048,2,128]{2,1,0:T(2,128)(2,1)S(1)} %collective-permute-done.k, bf16[2048,2,128]{2,1,0:T(2,128)(2,1)S(1)} %collective-permute-done.1.v, ...), custom_call_target="tpu_custom_call", output_to_operand_aliasing={{0}: (5, {}), {1}: (6, {})} | custom-call | tf_op jit(solution)/shard_map/other_shard/pallas_call | solution.py:336
  9.7 0.0 collective-permute-done.2.q
  9.7 2.8 %visitor.2 = bf16[34,16,128]{2,1,0:T(8,128)(2,1)S(1)} custom-call(bf16[64,16,128]{2,1,0:T(8,128)(2,1)S(1)} %collective-permute-done.2.q, bf16[2,4224,128]{2,1,0:T(8,128)(2,1)S(1)} %get-tuple-element.36.keys, bf16[2,4224,256]{2,1,0:T(8,128)(2,1)S(1)} %get-tuple-element.37.values), custom_call_target="tpu_custom_call" | custom-call | flops 1073741824 | bytes 4194304 | tf_op jit(solution)/shard_map/visitor/pallas_call | solution.py:291
  12.4 1.4 %collective-permute-start.5 = (bf16[34,16,128]{2,1,0:T(8,128)(2,1)S(1)}, bf16[34,16,128]{2,1,0:T(8,128)(2,1)S(1)}, u32[]{:S(2)}, u32[]{:S(2)}) collective-permute-start(bf16[34,16,128]{2,1,0:T(8,128)(2,1)S(1)} %visitor.2), channel_id=1, source_target_pairs={{0,8},{4,12},{8,0},{12,4},{1,9},{5,13},{9,1},{13,5},{2,10},{6,14},... | collective-permute-start | bytes 417800 | tf_op jit(solution)/shard_map/ppermute | solution.py:280
  13.9 2.7 %visitor.3 = bf16[33,16,128]{2,1,0:T(8,128)(2,1)S(1)} custom-call(bf16[64,16,128]{2,1,0:T(8,128)(2,1)S(1)} %collective-permute-done.2.q, bf16[2,4224,128]{2,1,0:T(8,128)(2,1)S(1)} %get-tuple-element.36.keys, bf16[2,4224,256]{2,1,0:T(8,128)(2,1)S(1)} %get-tuple-element.37.values), custom_call_target="tpu_custom_call" | custom-call | tf_op jit(solution)/shard_map/visitor/pallas_call | solution.py:291
  16.6 0.6 %collective-permute-start.4 = (bf16[33,16,128]{2,1,0:T(8,128)(2,1)S(1)}, bf16[33,16,128]{2,1,0:T(8,128)(2,1)S(1)}, u32[]{:S(2)}, u32[]{:S(2)}) collective-permute-start(bf16[33,16,128]{2,1,0:T(8,128)(2,1)S(1)} %visitor.3), channel_id=1, source_target_pairs={{0,8},{4,12},{8,0},{12,4},{1,9},{5,13},{9,1},{13,5},{2,10},{6,14},... | collective-permute-start | bytes 405512 | tf_op jit(solution)/shard_map/ppermute | solution.py:280
  17.2 3.0 %own_rest.1.rest = bf16[66,16,128]{2,1,0:T(8,128)(2,1)S(1)} custom-call(s32[1]{0:T(128)S(6)} %copy.17.length, bf16[64,16,128]{2,1,0:T(8,128)(2,1)S(1)} %get-tuple-element.40.q, bf16[2,4224,128]{2,1,0:T(8,128)(2,1)S(1)} %get-tuple-element.36.keys, bf16[2,4224,256]{2,1,0:T(8,128)(2,1)S(1)} %get-tuple-element.37.values), custom_call_target="tpu_custom_call" | custom-call | tf_op jit(solution)/shard_map/own_rest/pallas_call | solution.py:359
  20.2 0.2 near.1
  20.4 0.0 collective-permute-done.5.refs_0_
  20.4 0.8 %final.2.refs_1_ = bf16[64,16,128]{2,1,0:T(8,128)(2,1)} custom-call(f32[64,16,128]{2,1,0:T(8,128)S(1)} %get-tuple-element.41.near, f32[8,128]{1,0:T(8,128)S(1)} %get-tuple-element.42.near_l, bf16[34,16,128]{2,1,0:T(8,128)(2,1)S(1)} %collective-permute-done.5.refs_0_), custom_call_target="tpu_custom_call" | custom-call | tf_op jit(solution)/shard_map/final/pallas_call | solution.py:379
  21.3 0.4 %collective-permute-done.4.refs_0_ = bf16[33,16,128]{2,1,0:T(8,128)(2,1)S(1)} collective-permute-done((bf16[33,16,128]{2,1,0:T(8,128)(2,1)S(1)}, bf16[33,16,128]{2,1,0:T(8,128)(2,1)S(1)}, u32[]{:S(2)}, u32[]{:S(2)}) %collective-permute-start.4) | collective-permute-done | bytes 135200 | tf_op jit(solution)/shard_map/ppermute | solution.py:280
  21.7 0.8 %final.3 = bf16[64,16,128]{2,1,0:T(8,128)(2,1)} custom-call(f32[64,16,128]{2,1,0:T(8,128)S(1)} %get-tuple-element.41.near, f32[8,128]{1,0:T(8,128)S(1)} %get-tuple-element.42.near_l, bf16[33,16,128]{2,1,0:T(8,128)(2,1)S(1)} %collective-permute-done.4.refs_0_, bf16[64,16,128]{2,1,0:T(8,128)(2,1)} %final.2.refs_1_), custom_call_target="tpu_custom_call", output_to_operand_aliasing={{}: (3, {})} | custom-call | tf_op jit(solution)/shard_map/final/pallas_call | solution.py:379
  (1 shorter events, 0.0 us)
Async XLA Ops:
  0.0 9.7 %collective-permute-start.2 = (bf16[64,16,128]{2,1,0:T(8,128)(2,1)}, bf16[64,16,128]{2,1,0:T(8,128)(2,1)S(1)}, u32[]{:S(2)}, u32[]{:S(2)}) collective-permute-start(bf16[64,16,128]{2,1,0:T(8,128)(2,1)} %q.1), channel_id=1, source_target_pairs={{0,8},{4,12},{8,0},{12,4},{1,9},{5,13},{9,1},{13,5},{2,10},{6,14},... | collective-permute-start | bytes 786440 | tf_op jit(solution)/shard_map/ppermute | solution.py:280
  4.7 4.3 %collective-permute-start = (bf16[2048,2,128]{2,1,0:T(2,128)(2,1)S(1)}, bf16[2048,2,128]{2,1,0:T(2,128)(2,1)S(1)}, u32[]{:S(2)}, u32[]{:S(2)}) collective-permute-start(bf16[2048,2,128]{2,1,0:T(2,128)(2,1)S(1)} %get-tuple-element.25.k), channel_id=1, source_target_pairs={{0,4},{4,0},{8,12},{12,8},{1,5},{5,1},{9,13},{13,9},{2,6},{6,2},{1... | collective-permute-start | bytes 3145736 | tf_op jit(solution)/shard_map/ppermute | solution.py:277
  4.7 4.3 %collective-permute-start.1 = (bf16[2048,2,128]{2,1,0:T(2,128)(2,1)S(1)}, bf16[2048,2,128]{2,1,0:T(2,128)(2,1)S(1)}, u32[]{:S(2)}, u32[]{:S(2)}) collective-permute-start(bf16[2048,2,128]{2,1,0:T(2,128)(2,1)S(1)} %get-tuple-element.26.v), channel_id=1, source_target_pairs={{0,4},{4,0},{8,12},{12,8},{1,5},{5,1},{9,13},{13,9},{2,6},{6,2},{1... | collective-permute-start | bytes 3145736 | tf_op jit(solution)/shard_map/ppermute | solution.py:277
  5.2 3.8 %collective-permute-start.3 = (bf16[16,16,128]{2,1,0:T(8,128)(2,1)S(1)}, bf16[16,16,128]{2,1,0:T(8,128)(2,1)S(1)}, u32[]{:S(2)}, u32[]{:S(2)}) collective-permute-start(bf16[16,16,128]{2,1,0:T(8,128)(2,1)S(1)} %get-tuple-element.28.new), channel_id=1, source_target_pairs={{0,4},{4,0},{8,12},{12,8},{1,5},{5,1},{9,13},{13,9},{2,6},{6,2},{1... | collective-permute-start | bytes 196616 | tf_op jit(solution)/shard_map/ppermute | solution.py:277
  12.4 8.0 %collective-permute-start.5 = (bf16[34,16,128]{2,1,0:T(8,128)(2,1)S(1)}, bf16[34,16,128]{2,1,0:T(8,128)(2,1)S(1)}, u32[]{:S(2)}, u32[]{:S(2)}) collective-permute-start(bf16[34,16,128]{2,1,0:T(8,128)(2,1)S(1)} %visitor.2), channel_id=1, source_target_pairs={{0,8},{4,12},{8,0},{12,4},{1,9},{5,13},{9,1},{13,5},{2,10},{6,14},... | collective-permute-start | bytes 417800 | tf_op jit(solution)/shard_map/ppermute | solution.py:280
  16.6 5.1 %collective-permute-start.4 = (bf16[33,16,128]{2,1,0:T(8,128)(2,1)S(1)}, bf16[33,16,128]{2,1,0:T(8,128)(2,1)S(1)}, u32[]{:S(2)}, u32[]{:S(2)}) collective-permute-start(bf16[33,16,128]{2,1,0:T(8,128)(2,1)S(1)} %visitor.3), channel_id=1, source_target_pairs={{0,8},{4,12},{8,0},{12,4},{1,9},{5,13},{9,1},{13,5},{2,10},{6,14},... | collective-permute-start | bytes 405512 | tf_op jit(solution)/shard_map/ppermute | solution.py:280

commit v8 on v7

--- a/solution.py
+++ b/solution.py
@@ -70,7 +70,9 @@
             values[h, cut, hd:] = jnp.where(included, 1.0, 0.0).astype(BF16)
 
 
-def own_shard_kernel(slots, length, new, _k, _v, keys, values):
+def own_shard_kernel(length, k, v, new, keys, values):
+    slots = k.shape[0]
+    prepare_kernel(k, v, keys, values)
     count = jnp.clip(length[0] - lax.axis_index("ctx") * slots, 0, slots)
     first_new = new[0].astype(F32)
 
@@ -319,17 +321,15 @@
     new_core = over_core(new)
     places = 2 * slots + CORES * tokens
     both = [jax.ShapeDtypeStruct((kv, places, hd), BF16), jax.ShapeDtypeStruct((kv, places, 2 * hd), BF16)]
-    keys, values = call("prepare", prepare_kernel, both, (k, v), tiny)
     keys, values = pl.pallas_call(
-        functools.partial(own_shard_kernel, slots),
+        own_shard_kernel,
         out_shape=both,
         in_specs=[SMEM] + [VMEM] * 3,
         out_specs=[VMEM] * 2,
-        input_output_aliases={2: 0, 3: 1},
         compiler_params=params(),
         cost_estimate=tiny,
         name="own_shard",
-    )(cache_len, new, keys, values)
+    )(cache_len, k, v, new)
     kernel = functools.partial(own_near_kernel, slots)
     own_near = call("own_near", kernel, packed(tokens), (q_own, keys, values), cost(tokens * 50))
     k_core, v_core, own_near = lax.optimization_barrier((k_core, v_core, own_near))

time: 22.8 us -> 22.8 us (level)
    pallas_call x5 -> x4, Pallas kernels: 8.73 us -> 8.28 us  [call(): pl.pallas_call(kernel, out_shape=out, in_specs=[VMEM] * len(args), out_sp...]
    pallas_call x1, Pallas kernels: 0.02 us -> 0.45 us  [per_device(): pl.pallas_call(own_shard_kernel, out_shape=both, in_specs=[SMEM] + [VMEM]...]
where the time goes in v8:
time: 22.8 us; the launch traced here: 22.7 us
  Pallas kernels  15.7 us (69%)
  starting transfers between devices  5.6 us (25%)
  between operations  0.92 us (4%)
  waiting for transfers between devices  0.45 us (2%)
    pallas_call x4, Pallas kernels, call(): pl.pallas_call(kernel, out_shape=out, in_specs=[VMEM] * len(args), out_sp...  8.28 us
    ppermute x3, starting transfers between devices, over_chip(): lax.ppermute(x, 'ctx', [(i, (i // CORES + step) % chips * CORES + i % COR...  4.95 us
    pallas_call x1, Pallas kernels, per_device(): pl.pallas_call(functools.partial(own_rest_kernel, slots), out_shape=packe...  2.99 us
    pallas_call x1, Pallas kernels, per_device(): pl.pallas_call(load_kernel, out_shape=out, in_specs=[HBM] * len(moved), o...  1.71 us
    pallas_call x2, Pallas kernels, per_device(): pl.pallas_call(functools.partial(final_kernel, group, first, n_tokens), o...  1.65 us
    ppermute x3, starting transfers between devices, over_core(): return lax.ppermute(x, 'ctx', [(i, i ^ 1) for i in range(n)])  0.65 us
    pallas_call x1, Pallas kernels, per_device(): pl.pallas_call(other_shard_kernel, out_shape=both, in_specs=[SMEM] + [VME...  0.62 us
  transfers between devices with their start and end apart: 6, of which 1 were waited for; matrix products, arithmetic and copies ran while one was open for 0% of the time, Pallas kernels for 53%

profile of v8, /device:TPU:0, one launch (start us, length us, event | category | flops | bytes accessed | tf_op | source)
XLA Modules:
  0.0 22.7 jit_solution(14681365305807228637)
XLA Ops:
  0.0 2.9 %collective-permute-start.2 = (bf16[64,16,128]{2,1,0:T(8,128)(2,1)}, bf16[64,16,128]{2,1,0:T(8,128)(2,1)S(1)}, u32[]{:S(2)}, u32[]{:S(2)}) collective-permute-start(bf16[64,16,128]{2,1,0:T(8,128)(2,1)} %q.1), channel_id=1, source_target_pairs={{0,8},{4,12},{8,0},{12,4},{1,9},{5,13},{9,1},{13,5},{2,10},{6,14},... | collective-permute-start | bytes 786440 | tf_op jit(solution)/shard_map/ppermute | solution.py:282
  2.9 1.7 %load.1 = (bf16[2048,2,128]{2,1,0:T(2,128)(2,1)S(1)}, bf16[2048,2,128]{2,1,0:T(2,128)(2,1)S(1)}, bf16[64,16,128]{2,1,0:T(8,128)(2,1)S(1)}, bf16[16,16,128]{2,1,0:T(8,128)(2,1)S(1)}) custom-call(bf16[2048,2,128]{2,1,0:T(2,128)(2,1)} %k.1, bf16[2048,2,128]{2,1,0:T(2,128)(2,1)} %v.1, bf16[64,16,128]{2,1,0:T(8,128)(2,1)} %q.1, bf16[8,16,128]{2,1,0:T(8,128)(2,1)} %bitcast.2, ...), custom_call_target="tpu_custom_call" | custom-call | tf_op jit(solution)/shard_map/load/pallas_call | solution.py:310
  4.7 0.1 collective-permute-start
  4.7 0.5 %collective-permute-start.1 = (bf16[2048,2,128]{2,1,0:T(2,128)(2,1)S(1)}, bf16[2048,2,128]{2,1,0:T(2,128)(2,1)S(1)}, u32[]{:S(2)}, u32[]{:S(2)}) collective-permute-start(bf16[2048,2,128]{2,1,0:T(2,128)(2,1)S(1)} %get-tuple-element.24.v), channel_id=1, source_target_pairs={{0,4},{4,0},{8,12},{12,8},{1,5},{5,1},{9,13},{13,9},{2,6},{6,2},{1... | collective-permute-start | bytes 3145736 | tf_op jit(solution)/shard_map/ppermute | solution.py:279
  5.2 0.1 collective-permute-start.3
  6.0 0.5 %own_shard.1 = (bf16[2,4224,128]{2,1,0:T(8,128)(2,1)S(1)}, bf16[2,4224,256]{2,1,0:T(8,128)(2,1)S(1)}) custom-call(s32[1]{0:T(128)S(6)} %copy.13.length, bf16[2048,2,128]{2,1,0:T(2,128)(2,1)S(1)} %get-tuple-element.23.k, bf16[2048,2,128]{2,1,0:T(2,128)(2,1)S(1)} %get-tuple-element.24.v, bf16[16,16,128]{2,1,0:T(8,128)(2,1)S(1)} %get-tuple-element.26.new), custom_call_target="tpu_custom_call" | custom-call | tf_op jit(solution)/shard_map/own_shard/pallas_call | solution.py:324
  6.4 2.6 %own_near.1.near = bf16[66,16,128]{2,1,0:T(8,128)(2,1)S(1)} custom-call(bf16[64,16,128]{2,1,0:T(8,128)(2,1)S(1)} %get-tuple-element.36.q, bf16[2,4224,128]{2,1,0:T(8,128)(2,1)S(1)} %get-tuple-element.27.keys._k, bf16[2,4224,256]{2,1,0:T(8,128)(2,1)S(1)} %get-tuple-element.28.values._v), custom_call_target="tpu_custom_call" | custom-call | flops 107374182400 | bytes 4194304 | tf_op jit(solution)/shard_map/own_near/pallas_call | solution.py:293
  9.0 0.0 collective-permute-done.k
  9.0 0.0 collective-permute-done.1.v
  9.0 0.0 collective-permute-done.3.new_core
  9.0 0.6 %other_shard.1 = (bf16[2,4224,128]{2,1,0:T(8,128)(2,1)S(1)}, bf16[2,4224,256]{2,1,0:T(8,128)(2,1)S(1)}) custom-call(s32[1]{0:T(128)S(6)} %copy.13.length, bf16[2048,2,128]{2,1,0:T(2,128)(2,1)S(1)} %collective-permute-done.k, bf16[2048,2,128]{2,1,0:T(2,128)(2,1)S(1)} %collective-permute-done.1.v, ...), custom_call_target="tpu_custom_call", output_to_operand_aliasing={{0}: (5, {}), {1}: (6, {})} | custom-call | tf_op jit(solution)/shard_map/other_shard/pallas_call | solution.py:336
  9.6 0.0 collective-permute-done.2.q
  9.6 2.8 %visitor.2 = bf16[34,16,128]{2,1,0:T(8,128)(2,1)S(1)} custom-call(bf16[64,16,128]{2,1,0:T(8,128)(2,1)S(1)} %collective-permute-done.2.q, bf16[2,4224,128]{2,1,0:T(8,128)(2,1)S(1)} %get-tuple-element.32.keys, bf16[2,4224,256]{2,1,0:T(8,128)(2,1)S(1)} %get-tuple-element.33.values), custom_call_target="tpu_custom_call" | custom-call | flops 1073741824 | bytes 4194304 | tf_op jit(solution)/shard_map/visitor/pallas_call | solution.py:293
  12.4 1.4 %collective-permute-start.5 = (bf16[34,16,128]{2,1,0:T(8,128)(2,1)S(1)}, bf16[34,16,128]{2,1,0:T(8,128)(2,1)S(1)}, u32[]{:S(2)}, u32[]{:S(2)}) collective-permute-start(bf16[34,16,128]{2,1,0:T(8,128)(2,1)S(1)} %visitor.2), channel_id=1, source_target_pairs={{0,8},{4,12},{8,0},{12,4},{1,9},{5,13},{9,1},{13,5},{2,10},{6,14},... | collective-permute-start | bytes 417800 | tf_op jit(solution)/shard_map/ppermute | solution.py:282
  13.9 2.7 %visitor.3 = bf16[33,16,128]{2,1,0:T(8,128)(2,1)S(1)} custom-call(bf16[64,16,128]{2,1,0:T(8,128)(2,1)S(1)} %collective-permute-done.2.q, bf16[2,4224,128]{2,1,0:T(8,128)(2,1)S(1)} %get-tuple-element.32.keys, bf16[2,4224,256]{2,1,0:T(8,128)(2,1)S(1)} %get-tuple-element.33.values), custom_call_target="tpu_custom_call" | custom-call | tf_op jit(solution)/shard_map/visitor/pallas_call | solution.py:293
  16.6 0.6 %collective-permute-start.4 = (bf16[33,16,128]{2,1,0:T(8,128)(2,1)S(1)}, bf16[33,16,128]{2,1,0:T(8,128)(2,1)S(1)}, u32[]{:S(2)}, u32[]{:S(2)}) collective-permute-start(bf16[33,16,128]{2,1,0:T(8,128)(2,1)S(1)} %visitor.3), channel_id=1, source_target_pairs={{0,8},{4,12},{8,0},{12,4},{1,9},{5,13},{9,1},{13,5},{2,10},{6,14},... | collective-permute-start | bytes 405512 | tf_op jit(solution)/shard_map/ppermute | solution.py:282
  17.2 3.0 %own_rest.1.rest = bf16[66,16,128]{2,1,0:T(8,128)(2,1)S(1)} custom-call(s32[1]{0:T(128)S(6)} %copy.13.length, bf16[64,16,128]{2,1,0:T(8,128)(2,1)S(1)} %get-tuple-element.36.q, bf16[2,4224,128]{2,1,0:T(8,128)(2,1)S(1)} %get-tuple-element.32.keys, bf16[2,4224,256]{2,1,0:T(8,128)(2,1)S(1)} %get-tuple-element.33.values), custom_call_target="tpu_custom_call" | custom-call | tf_op jit(solution)/shard_map/own_rest/pallas_call | solution.py:359
  20.2 0.2 near.1
  20.4 0.0 collective-permute-done.5.refs_0_
  20.4 0.8 %final.2.refs_1_ = bf16[64,16,128]{2,1,0:T(8,128)(2,1)} custom-call(f32[64,16,128]{2,1,0:T(8,128)S(1)} %get-tuple-element.37.near, f32[8,128]{1,0:T(8,128)S(1)} %get-tuple-element.38.near_l, bf16[34,16,128]{2,1,0:T(8,128)(2,1)S(1)} %collective-permute-done.5.refs_0_), custom_call_target="tpu_custom_call" | custom-call | tf_op jit(solution)/shard_map/final/pallas_call | solution.py:379
  21.2 0.4 %collective-permute-done.4.refs_0_ = bf16[33,16,128]{2,1,0:T(8,128)(2,1)S(1)} collective-permute-done((bf16[33,16,128]{2,1,0:T(8,128)(2,1)S(1)}, bf16[33,16,128]{2,1,0:T(8,128)(2,1)S(1)}, u32[]{:S(2)}, u32[]{:S(2)}) %collective-permute-start.4) | collective-permute-done | bytes 135200 | tf_op jit(solution)/shard_map/ppermute | solution.py:282
  21.7 0.8 %final.3 = bf16[64,16,128]{2,1,0:T(8,128)(2,1)} custom-call(f32[64,16,128]{2,1,0:T(8,128)S(1)} %get-tuple-element.37.near, f32[8,128]{1,0:T(8,128)S(1)} %get-tuple-element.38.near_l, bf16[33,16,128]{2,1,0:T(8,128)(2,1)S(1)} %collective-permute-done.4.refs_0_, bf16[64,16,128]{2,1,0:T(8,128)(2,1)} %final.2.refs_1_), custom_call_target="tpu_custom_call", output_to_operand_aliasing={{}: (3, {})} | custom-call | tf_op jit(solution)/shard_map/final/pallas_call | solution.py:379
Async XLA Ops:
  0.0 9.6 %collective-permute-start.2 = (bf16[64,16,128]{2,1,0:T(8,128)(2,1)}, bf16[64,16,128]{2,1,0:T(8,128)(2,1)S(1)}, u32[]{:S(2)}, u32[]{:S(2)}) collective-permute-start(bf16[64,16,128]{2,1,0:T(8,128)(2,1)} %q.1), channel_id=1, source_target_pairs={{0,8},{4,12},{8,0},{12,4},{1,9},{5,13},{9,1},{13,5},{2,10},{6,14},... | collective-permute-start | bytes 786440 | tf_op jit(solution)/shard_map/ppermute | solution.py:282
  4.7 4.3 %collective-permute-start = (bf16[2048,2,128]{2,1,0:T(2,128)(2,1)S(1)}, bf16[2048,2,128]{2,1,0:T(2,128)(2,1)S(1)}, u32[]{:S(2)}, u32[]{:S(2)}) collective-permute-start(bf16[2048,2,128]{2,1,0:T(2,128)(2,1)S(1)} %get-tuple-element.23.k), channel_id=1, source_target_pairs={{0,4},{4,0},{8,12},{12,8},{1,5},{5,1},{9,13},{13,9},{2,6},{6,2},{1... | collective-permute-start | bytes 3145736 | tf_op jit(solution)/shard_map/ppermute | solution.py:279
  4.7 4.3 %collective-permute-start.1 = (bf16[2048,2,128]{2,1,0:T(2,128)(2,1)S(1)}, bf16[2048,2,128]{2,1,0:T(2,128)(2,1)S(1)}, u32[]{:S(2)}, u32[]{:S(2)}) collective-permute-start(bf16[2048,2,128]{2,1,0:T(2,128)(2,1)S(1)} %get-tuple-element.24.v), channel_id=1, source_target_pairs={{0,4},{4,0},{8,12},{12,8},{1,5},{5,1},{9,13},{13,9},{2,6},{6,2},{1... | collective-permute-start | bytes 3145736 | tf_op jit(solution)/shard_map/ppermute | solution.py:279
  5.2 3.8 %collective-permute-start.3 = (bf16[16,16,128]{2,1,0:T(8,128)(2,1)S(1)}, bf16[16,16,128]{2,1,0:T(8,128)(2,1)S(1)}, u32[]{:S(2)}, u32[]{:S(2)}) collective-permute-start(bf16[16,16,128]{2,1,0:T(8,128)(2,1)S(1)} %get-tuple-element.26.new), channel_id=1, source_target_pairs={{0,4},{4,0},{8,12},{12,8},{1,5},{5,1},{9,13},{13,9},{2,6},{6,2},{1... | collective-permute-start | bytes 196616 | tf_op jit(solution)/shard_map/ppermute | solution.py:279
  12.4 8.0 %collective-permute-start.5 = (bf16[34,16,128]{2,1,0:T(8,128)(2,1)S(1)}, bf16[34,16,128]{2,1,0:T(8,128)(2,1)S(1)}, u32[]{:S(2)}, u32[]{:S(2)}) collective-permute-start(bf16[34,16,128]{2,1,0:T(8,128)(2,1)S(1)} %visitor.2), channel_id=1, source_target_pairs={{0,8},{4,12},{8,0},{12,4},{1,9},{5,13},{9,1},{13,5},{2,10},{6,14},... | collective-permute-start | bytes 417800 | tf_op jit(solution)/shard_map/ppermute | solution.py:282
  16.6 5.1 %collective-permute-start.4 = (bf16[33,16,128]{2,1,0:T(8,128)(2,1)S(1)}, bf16[33,16,128]{2,1,0:T(8,128)(2,1)S(1)}, u32[]{:S(2)}, u32[]{:S(2)}) collective-permute-start(bf16[33,16,128]{2,1,0:T(8,128)(2,1)S(1)} %visitor.3), channel_id=1, source_target_pairs={{0,8},{4,12},{8,0},{12,4},{1,9},{5,13},{9,1},{13,5},{2,10},{6,14},... | collective-permute-start | bytes 405512 | tf_op jit(solution)/shard_map/ppermute | solution.py:282
